TPU v7x, 32 devices: a whole 2x2x4 slice. The times are simulated.
32 devices in a mesh: tile: 8 (over z, x), pos: 4 (over y, core).
Axes of the slice: x: 2, y: 2, z: 4, core: 2. Of those that a mesh axis runs over, the one named last changes fastest.
Arguments:
- probe_field: float32 [2, 256, 256], replicated, may hold values from -6 to 6
- specimen: bfloat16 [2, 2, 4096, 512], P(None, None, 'tile'), may hold values from -6 to 6
- amplitude: bfloat16 [256, 256, 256], P(('tile', 'pos')), may hold values from 0 to 2
- scan_anchor: int32 [256, 2], P(('tile', 'pos')), may hold values from 0 to 3840, as said below
- counts: int32 [32], P(('tile', 'pos')), may hold values from 2 to 8, as said below
Outputs:
- object_grad: float32 [2, 2, 4096, 512], P(None, None, 'tile')
- probe_grad: float32 [2, 256, 256], replicated
Inputs may be any that keep to these rules, and one draw needn't show every extreme that they name: `scan_anchor`: slot q's patch row r lies in the tile of index t = q // 32: t * 512 <= r < (t + 1) * 512, and the patch lies inside the object. Live slots of a device are its first counts slots; some device is full in every draw.
All inputs are finite; a program needn't handle non-finite values.
Results may differ from a plain program's by a relative error of at most 0.012.
Values may be sent and summed in bfloat16 or wider, within the bound.
No kernel may reach another device: no remote copies, remote signals or barrier semaphores. Data moves between devices by JAX's collectives and lax.ppermute only.
A program may use at most 64 MiB of HBM per device.

v0:
```python
import math

import jax
import jax.numpy as jnp
from jax import lax
from jax.sharding import PartitionSpec as P

PROP_COEF = 0.5
AMP_EPS = 0.05


def passed_along(value, axis, steps):
    count = lax.axis_size(axis)
    initial, last = (max(0, -steps), min(count, count - steps))
    return lax.ppermute(value, axis, [(source, source + steps) for source in range(initial, last)])


def make_tables(patch_edge):
    index_row = jnp.arange(patch_edge, dtype=jnp.int32)
    product = index_row[:, None] * index_row[None, :] % patch_edge
    angles = product.astype(jnp.float32) * (2.0 * math.pi / patch_edge)
    cosine = jnp.cos(angles) / math.sqrt(patch_edge)
    sine_part = jnp.sin(angles) / math.sqrt(patch_edge)
    table_one = jnp.concatenate(
        [jnp.concatenate([cosine, sine_part], 1), jnp.concatenate([-sine_part, cosine], 1)], 0
    )
    table_two = jnp.concatenate(
        [jnp.concatenate([cosine, -sine_part], 1), jnp.concatenate([sine_part, cosine], 1)], 0
    )
    return (table_one.astype(jnp.bfloat16), table_two.astype(jnp.bfloat16))


def make_kernel(patch_edge):
    index_row = jnp.arange(patch_edge, dtype=jnp.int32)
    centred = jnp.where(index_row < patch_edge // 2, index_row, index_row - patch_edge)
    square = centred * centred
    summed = (square[:, None] + square[None, :]).astype(jnp.float32)
    angles = summed * (PROP_COEF * math.pi / patch_edge)
    return (jnp.cos(angles), -jnp.sin(angles))


def transform(wave, left_table, right_table):
    patch_edge = wave[0].shape[0]
    stacked = jnp.concatenate([wave[0], wave[1]], 0).astype(jnp.bfloat16)
    middle = jnp.dot(left_table, stacked, preferred_element_type=jnp.float32).astype(jnp.bfloat16)
    joined = jnp.concatenate([middle[:patch_edge], middle[patch_edge:]], 1)
    result = jnp.dot(joined, right_table, preferred_element_type=jnp.float32)
    return (result[:, :patch_edge], result[:, patch_edge:])


def complex_mul(left_pair, right_pair):
    return (
        left_pair[0] * right_pair[0] - left_pair[1] * right_pair[1],
        left_pair[0] * right_pair[1] + left_pair[1] * right_pair[0],
    )


def conj_mul(left_pair, right_pair):
    return (
        left_pair[0] * right_pair[0] + left_pair[1] * right_pair[1],
        left_pair[0] * right_pair[1] - left_pair[1] * right_pair[0],
    )


def position_grads(probe_field, patch_re, patch_im, measured, table_one, table_two, kernel):
    slices = patch_re.shape[0]
    arriving = [(probe_field[0], probe_field[1])]
    leaving = arriving[0]
    for slice_index in range(slices):
        leaving = complex_mul(arriving[slice_index], (patch_re[slice_index], patch_im[slice_index]))
        if slice_index + 1 < slices:
            spectrum = complex_mul(kernel, transform(leaving, table_one, table_two))
            arriving.append(transform(spectrum, table_two, table_one))
    far_re, far_im = transform(leaving, table_one, table_two)
    modulus = jnp.sqrt(far_re * far_re + far_im * far_im + AMP_EPS)
    factor = 1.0 - measured.astype(jnp.float32) / modulus
    adjoint = transform((factor * far_re, factor * far_im), table_two, table_one)
    grads_re = [None] * slices
    grads_im = [None] * slices
    for slice_index in range(slices - 1, -1, -1):
        grads_re[slice_index], grads_im[slice_index] = conj_mul(arriving[slice_index], adjoint)
        adjoint = conj_mul((patch_re[slice_index], patch_im[slice_index]), adjoint)
        if slice_index > 0:
            spectrum = conj_mul(kernel, transform(adjoint, table_one, table_two))
            adjoint = transform(spectrum, table_two, table_one)
    return (jnp.stack(grads_re), jnp.stack(grads_im), adjoint)


def body(probe_field, specimen, amplitude, scan_anchor, counts):
    slices = specimen.shape[1]
    tile_rows = specimen.shape[2]
    patch_edge = probe_field.shape[1]
    table_one, table_two = make_tables(patch_edge)
    kernel = make_kernel(patch_edge)
    base_row = lax.axis_index("tile") * tile_rows
    rim_rows = passed_along(specimen[:, :, :patch_edge, :], "tile", -1)
    padded = jnp.concatenate([specimen, rim_rows], axis=2)
    slot_count = amplitude.shape[0]
    visit_order = jnp.arange(slot_count, dtype=jnp.int32)
    live_total = counts[0]
    zero_index = jnp.zeros((), jnp.int32)

    def visit(step_index, carry):
        object_acc, probe_acc = carry
        slot_now = visit_order[step_index]
        row_start = scan_anchor[slot_now, 0] - base_row
        col_start = scan_anchor[slot_now, 1]
        corner = (zero_index, zero_index, row_start, col_start)
        patch_now = lax.dynamic_slice(padded, corner, (2, slices, patch_edge, patch_edge)).astype(
            jnp.float32
        )
        grad_re, grad_im, probe_term = position_grads(
            probe_field,
            patch_now[0],
            patch_now[1],
            amplitude[slot_now],
            table_one,
            table_two,
            kernel,
        )
        current = lax.dynamic_slice(object_acc, corner, (2, slices, patch_edge, patch_edge))
        object_acc = lax.dynamic_update_slice(
            object_acc, current + jnp.stack([grad_re, grad_im]), corner
        )
        return (object_acc, probe_acc + jnp.stack([probe_term[0], probe_term[1]]))

    start_carry = (jnp.zeros(padded.shape, jnp.float32), jnp.zeros(probe_field.shape, jnp.float32))
    object_acc, probe_acc = lax.fori_loop(0, live_total, visit, start_carry)
    returned = passed_along(object_acc[:, :, tile_rows:, :].astype(jnp.bfloat16), "tile", 1).astype(
        jnp.float32
    )
    own_rows = object_acc[:, :, :tile_rows, :]
    own_rows = jnp.concatenate(
        [own_rows[:, :, :patch_edge, :] + returned, own_rows[:, :, patch_edge:, :]], axis=2
    )
    tile_grad = lax.psum(own_rows.astype(jnp.bfloat16), "pos").astype(jnp.float32)
    probe_total = lax.psum(probe_acc, ("tile", "pos"))
    return (tile_grad, probe_total)


def solution(mesh):
    return jax.shard_map(
        body,
        mesh=mesh,
        in_specs=(
            P(),
            P(None, None, "tile", None),
            P(("tile", "pos"), None, None),
            P(("tile", "pos"), None),
            P(("tile", "pos")),
        ),
        out_specs=(P(None, None, "tile", None), P()),
        check_vma=False,
    )
```

profile of v0, /device:TPU:0, one launch (start us, length us, event | category | flops | bytes accessed | tf_op | source)
XLA Modules:
  0.0 502.3 jit_solution(3514368539532029983)
XLA Ops:
  7.2 1.3 slice.121
  8.5 1.3 collective-permute-start
  9.8 1.0 fusion.98
  10.8 1.1 negate_convert_fusion
  12.0 24.5 %collective-permute-done = bf16[2,2,256,512]{3,2,1,0:T(8,128)(2,1)S(1)} collective-permute-done((bf16[2,2,256,512]{3,2,1,0:T(8,128)(2,1)S(1)}, bf16[2,2,256,512]{3,2,1,0:T(8,128)(2,1)S(1)}, u32[]{:S(2)}, u32[]{:S(2)}) %collective-permute-start) | collective-permute-done | bytes 1048608 | tf_op jit(solution)/shard_map/ppermute | solution.py:15
  36.5 3.5 pad_maximum_fusion
  40.0 3.5 broadcast_in_dim.4
  43.5 58.3 %while.15 = (s32[]{:T(128)}, f32[2,2,768,512]{3,2,1,0:T(8,128)}, f32[2,256,256]{2,1,0:T(8,128)S(1)}, s32[]{:T(128)}, s32[8]{0:T(128)S(1)}, /*index=5*/s32[8,2]{0...) while((s32[]{:T(128)}, f32[2,2,768,512]{3,2,1,0:T(8,128)}, ...), condition=%wide.region_1.2_spmd.clone.clone.clone, body=%wide.region_0.1_spmd.clone.clone.clone.sunk | while | flops 1624047616 | bytes 37884280 | solution.py:128
  44.2 0.6 dynamic_slice.51
  46.7 0.7 constant_dynamic-slice_fusion.3
  50.0 1.4 dynamic-slice_convert_fusion.2
  51.4 0.3 fusion.189
  51.8 0.3 fusion.191
  52.1 1.2 fusion.192
  53.3 0.3 fusion.193
  54.1 0.3 fusion.196
  54.8 1.0 multiply_convert_fusion.4
  55.8 0.3 fusion.199
  56.7 0.3 fusion.202
  57.4 1.2 fusion.205
  58.6 0.3 fusion.206
  59.5 1.6 maximum_add_fusion.4
  61.3 9.8 %dynamic_update_slice.7 = f32[2,2,768,512]{3,2,1,0:T(8,128)} dynamic-update-slice(f32[2,2,768,512]{3,2,1,0:T(8,128)} %get-tuple-element.439, f32[2,2,256,256]{3,2,1,0:T(8,128)S(1)} %maximum_add_fusion.4, s32[]{:T(128)} %constant.14.clone.1..sunk, s32[]{:T(128)} %constant.14.clone.1..sunk, s32[]{:T(128)S(6)} %select_n.99, s32[]{:T(128)S(6)} %select_n.100) | dynamic-update-slice | bytes 2097156 | tf_op jit(solution)/shard_map/while/body/dynamic_update_slice | solution.py:122
  71.7 0.6 dynamic_slice.51
  74.3 0.7 constant_dynamic-slice_fusion.3
  77.5 1.5 dynamic-slice_convert_fusion.2
  79.1 0.3 fusion.189
  79.5 0.3 fusion.191
  79.8 1.2 fusion.192
  81.0 0.3 fusion.193
  81.8 0.3 fusion.196
  82.5 1.0 multiply_convert_fusion.4
  83.5 0.3 fusion.199
  84.3 0.3 fusion.202
  85.0 1.2 fusion.205
  86.3 0.3 fusion.206
  87.2 1.8 maximum_add_fusion.4
  89.1 12.0 %dynamic_update_slice.7 = f32[2,2,768,512]{3,2,1,0:T(8,128)} dynamic-update-slice(f32[2,2,768,512]{3,2,1,0:T(8,128)} %get-tuple-element.439, f32[2,2,256,256]{3,2,1,0:T(8,128)S(1)} %maximum_add_fusion.4, s32[]{:T(128)} %constant.14.clone.1..sunk, s32[]{:T(128)} %constant.14.clone.1..sunk, s32[]{:T(128)S(6)} %select_n.99, s32[]{:T(128)S(6)} %select_n.100) | dynamic-update-slice | bytes 2097156 | tf_op jit(solution)/shard_map/while/body/dynamic_update_slice | solution.py:122
  101.8 3.4 convert.76
  105.4 186.8 %collective-permute-start.1 = (bf16[2,2,256,512]{3,2,1,0:T(8,128)(2,1)S(1)}, bf16[2,2,256,512]{3,2,1,0:T(8,128)(2,1)S(1)}, u32[]{:S(2)}, u32[]{:S(2)}) collective-permute-start(bf16[2,2,256,512]{3,2,1,0:T(8,128)(2,1)S(1)} %get-tuple-element.266), channel_id=1, source_target_pairs={{0,4},{4,8},{8,12},{12,16},{16,20},{20,24},{24,28},{1,5},{5,9},{9,... | collective-permute-start | bytes 3145736 | tf_op jit(solution)/shard_map/ppermute | solution.py:15
  292.2 12.2 %collective-permute-done.1 = bf16[2,2,256,512]{3,2,1,0:T(8,128)(2,1)S(1)} collective-permute-done((bf16[2,2,256,512]{3,2,1,0:T(8,128)(2,1)S(1)}, bf16[2,2,256,512]{3,2,1,0:T(8,128)(2,1)S(1)}, u32[]{:S(2)}, u32[]{:S(2)}) %collective-permute-start.1) | collective-permute-done | bytes 1048608 | tf_op jit(solution)/shard_map/ppermute | solution.py:15
  304.5 1.9 add_convert_fusion.2
  306.4 1.5 pad_maximum_fusion.1
  307.9 0.7 all-reduce.5.cloned.1.call-update
  308.6 50.3 %all-reduce.3.cloned.1.call-done = bf16[2,2,512,512]{3,2,1,0:T(8,128)(2,1)} async-done(((bf16[2,2,512,512]{3,2,1,0:T(8,128)(2,1)}), bf16[2,2,512,512]{3,2,1,0:T(8,128)(2,1)}) %all-reduce.3.cloned.1.call-update) | async-done | bytes 2097168 | tf_op jit(solution)/shard_map/psum | solution.py:136
  359.0 4.2 convert_element_type.98
  363.2 130.4 %all-reduce.5.cloned.1.call-done = f32[2,256,256]{2,1,0:T(8,128)} async-done(((f32[2,256,256]{2,1,0:T(8,128)}), f32[2,256,256]{2,1,0:T(8,128)}) %all-reduce.5.cloned.1.call-update) | async-done | bytes 524304 | tf_op jit(solution)/shard_map/psum | solution.py:137
  493.6 1.9 copy.19
  (48 shorter events, 5.0 us)
Async XLA Ops:
  7.2 351.8 %all-reduce.3.cloned.1.call-start = ((), (), s32[]{:S(2)}) async-start(), calls=%async_computation | async-start | bytes 4194304 | tf_op jit(solution)/shard_map/psum | solution.py:136
  8.5 28.0 %collective-permute-start = (bf16[2,2,256,512]{3,2,1,0:T(8,128)(2,1)S(1)}, bf16[2,2,256,512]{3,2,1,0:T(8,128)(2,1)S(1)}, u32[]{:S(2)}, u32[]{:S(2)}) collective-permute-start(bf16[2,2,256,512]{3,2,1,0:T(8,128)(2,1)S(1)} %slice.121), channel_id=1, source_target_pairs={{4,0},{8,4},{12,8},{16,12},{20,16},{24,20},{28,24},{5,1},{9,5},{13... | collective-permute-start | bytes 3145736 | tf_op jit(solution)/shard_map/ppermute | solution.py:15
  40.0 3.5 copy-start
  40.0 3.5 copy-start.2
  101.8 3.4 copy-start.1
  105.4 199.1 %collective-permute-start.1 = (bf16[2,2,256,512]{3,2,1,0:T(8,128)(2,1)S(1)}, bf16[2,2,256,512]{3,2,1,0:T(8,128)(2,1)S(1)}, u32[]{:S(2)}, u32[]{:S(2)}) collective-permute-start(bf16[2,2,256,512]{3,2,1,0:T(8,128)(2,1)S(1)} %get-tuple-element.266), channel_id=1, source_target_pairs={{0,4},{4,8},{8,12},{12,16},{16,20},{20,24},{24,28},{1,5},{5,9},{9,... | collective-permute-start | bytes 3145736 | tf_op jit(solution)/shard_map/ppermute | solution.py:15
  307.9 185.7 %all-reduce.5.cloned.1.call-start = ((), (), s32[]{:S(2)}) async-start(), calls=%async_computation.1 | async-start | bytes 1048576 | tf_op jit(solution)/shard_map/psum | solution.py:137
Sparse Core Ops, SparseCore 0:
  308.0 50.9 all-reduce.2
  365.7 127.8 all-reduce.4
where the time goes:
time: 507 us; the launch traced here: 502 us
  waiting for transfers between devices  218 us (43%)
  starting transfers between devices  188 us (37%)
  local copies, waits for them, and re-layouts  31.5 us (6%)
  other arithmetic  31 us (6%)
  between operations  14.1 us (3%)
  loops' own time  11.3 us (2%)
  matrix products  7.9 us (2%)
    ppermute x2, starting transfers between devices, passed_along(): lax.ppermute(value, axis, [(source, source + steps) for source in range(i...  188 us
    psum x1, waiting for transfers between devices, body(): probe_total = lax.psum(probe_acc, ('tile', 'pos'))  130 us
    psum x1, waiting for transfers between devices, body(): lax.psum(own_rows.astype(jnp.bfloat16), 'pos').astype(jnp.float32)  50.3 us
    ppermute x2, waiting for transfers between devices, passed_along(): lax.ppermute(value, axis, [(source, source + steps) for source in range(i...  36.7 us
    dynamic_update_slice x2, local copies, waits for them, and re-layouts, visit(): lax.dynamic_update_slice(object_acc, current + jnp.stack([grad_re, grad_i...  21.8 us
    another operation x14, other arithmetic  14.6 us
    another operation x1, loops' own time, body(): object_acc, probe_acc = lax.fori_loop(0, live_total, visit, start_carry)  11.3 us
  transfers between devices with their start and end apart: 4, of which 4 were waited for; matrix products, arithmetic and copies ran while one was open for 1% of the time, Pallas kernels for 0%

commit v1 on v0

v1 whole, which is shorter than its diff:
```python
import math

import jax
import jax.numpy as jnp
import ml_dtypes
import numpy as np
from jax import lax
from jax.experimental import pallas as pl
from jax.experimental.pallas import tpu as pltpu
from jax.sharding import PartitionSpec as P

PROP_COEF = 0.5
AMP_EPS = 0.05
LANES = 128
CHUNK = 32


def fixed_tables(edge):
    index = np.arange(edge)
    angles = (np.outer(index, index) % edge) * (2.0 * math.pi / edge)
    cosine = (np.cos(angles) / math.sqrt(edge)).astype(ml_dtypes.bfloat16).astype(np.float64)
    sine = (np.sin(angles) / math.sqrt(edge)).astype(ml_dtypes.bfloat16).astype(np.float64)
    forward = cosine - 1j * sine
    centred = np.where(index < edge // 2, index, index - edge)
    ramp = np.exp(-1j * (PROP_COEF * math.pi / edge) * centred * centred)
    spread = (np.conj(forward) * ramp[None, :]) @ forward

    def left_form(matrix):
        return np.block([[matrix.real, -matrix.imag], [matrix.imag, matrix.real]])

    tables = []
    for matrix in (spread, forward):
        tables += [left_form(matrix), left_form(matrix).T]
    return [jnp.asarray(table.astype(ml_dtypes.bfloat16)) for table in tables]


def slots_kernel(
    meta,
    anchor,
    probe,
    spec,
    rim,
    amp,
    left_a,
    right_a,
    left_f,
    right_f,
    send,
    keep,
    keep_probe,
    wide,
    acc,
    probe_acc,
    rolled,
    arriving,
    field,
    stack,
    joined,
):
    edge = probe.shape[1]
    tile_rows = spec.shape[2]
    slices = spec.shape[1]
    col_tiles = spec.shape[3] // LANES
    parts = edge // LANES
    live = meta[0]
    base_row = meta[1]
    half = meta[2]
    lane = lax.broadcasted_iota(jnp.int32, (CHUNK, LANES), 1)

    for part in range(2):
        for s in range(slices):
            for t in range(col_tiles):
                cols = pl.ds(t * LANES, LANES)
                wide[part, s, t, pl.ds(0, tile_rows), :] = spec[part, s, :, cols].astype(
                    jnp.float32
                )
                wide[part, s, t, pl.ds(tile_rows, edge), :] = rim[part, s, :, cols].astype(
                    jnp.float32
                )
                acc[part, s, t] = jnp.zeros(acc.shape[3:], jnp.float32)
    probe_acc[...] = jnp.zeros(probe_acc.shape, jnp.float32)

    def two_sided(left, right, out):
        for part in range(2):
            rows = pl.ds(part * edge, edge)
            joined[:, rows] = jnp.dot(
                left[rows, :], stack[...], preferred_element_type=jnp.float32
            ).astype(jnp.bfloat16)
        for part in range(2):
            out[part] = jnp.dot(
                joined[...],
                right[:, pl.ds(part * edge, edge)],
                preferred_element_type=jnp.float32,
            )

    def visit(slot, carry):
        row = anchor[slot, 0] - base_row
        col = anchor[slot, 1]
        first = jnp.minimum(col // LANES, col_tiles - parts - 1)
        shift = col - first * LANES
        turn = jnp.where(shift >= LANES, 0, shift)
        back = jnp.where(turn == 0, 0, LANES - turn)
        own = lane >= shift

        def patch(part, s, i, j):
            rows = pl.ds(row + i, CHUNK)
            main = wide[part, s, first + j, rows, :]
            if j > 0:
                return main
            return jnp.where(own, main, wide[part, s, first + parts, rows, :])

        def place(part, s, i, j, value):
            rows = pl.ds(row + i, CHUNK)
            if j > 0:
                acc[part, s, first + j, rows, :] += value
            else:
                acc[part, s, first, rows, :] += jnp.where(own, value, 0.0)
                acc[part, s, first + parts, rows, :] += jnp.where(own, 0.0, value)

        def put(i, j, re, im):
            cols = pl.ds(j * LANES, LANES)
            stack[pl.ds(i, CHUNK), cols] = re.astype(jnp.bfloat16)
            stack[pl.ds(edge + i, CHUNK), cols] = im.astype(jnp.bfloat16)

        def tiles():
            for i in range(0, edge, CHUNK):
                for j in range(parts):
                    yield i, j, pl.ds(i, CHUNK), pl.ds(j * LANES, LANES)

        for i in range(0, edge, CHUNK):
            rows = pl.ds(i, CHUNK)
            turned = [
                [
                    pltpu.roll(probe[part, rows, pl.ds(j * LANES, LANES)], turn, 1)
                    for j in range(parts)
                ]
                for part in range(2)
            ]
            for j in range(parts):
                u_re, u_im = [
                    jnp.where(own, turned[part][j], turned[part][j - 1]) for part in range(2)
                ]
                rolled[0, rows, pl.ds(j * LANES, LANES)] = u_re
                rolled[1, rows, pl.ds(j * LANES, LANES)] = u_im
                o_re, o_im = patch(0, 0, i, j), patch(1, 0, i, j)
                put(i, j, u_re * o_re - u_im * o_im, u_re * o_im + u_im * o_re)
        two_sided(left_a, right_a, arriving)
        for i, j, rows, cols in tiles():
            u_re, u_im = arriving[0, rows, cols], arriving[1, rows, cols]
            o_re, o_im = patch(0, 1, i, j), patch(1, 1, i, j)
            put(i, j, u_re * o_re - u_im * o_im, u_re * o_im + u_im * o_re)
        two_sided(left_f, right_f, field)
        for i, j, rows, cols in tiles():
            far_re, far_im = field[0, rows, cols], field[1, rows, cols]
            measured = amp[slot, rows, cols].astype(jnp.float32)
            ratio = measured * lax.rsqrt(far_re * far_re + far_im * far_im + AMP_EPS)
            put(i, j, far_re - ratio * far_re, ratio * far_im - far_im)
        two_sided(left_f, right_f, field)
        for i, j, rows, cols in tiles():
            u_re, u_im = arriving[0, rows, cols], arriving[1, rows, cols]
            w_re, w_im = field[0, rows, cols], field[1, rows, cols]
            place(0, 1, i, j, u_re * w_re - u_im * w_im)
            place(1, 1, i, j, u_re * w_im + u_im * w_re)
            o_re, o_im = patch(0, 1, i, j), patch(1, 1, i, j)
            put(i, j, o_re * w_re - o_im * w_im, o_re * w_im + o_im * w_re)
        two_sided(left_a, right_a, field)
        for i in range(0, edge, CHUNK):
            rows = pl.ds(i, CHUNK)
            turned = [[None] * parts for _ in range(2)]
            for j in range(parts):
                cols = pl.ds(j * LANES, LANES)
                u_re, u_im = rolled[0, rows, cols], rolled[1, rows, cols]
                w_re, w_im = field[0, rows, cols], field[1, rows, cols]
                place(0, 0, i, j, u_re * w_re - u_im * w_im)
                place(1, 0, i, j, u_re * w_im + u_im * w_re)
                o_re, o_im = patch(0, 0, i, j), patch(1, 0, i, j)
                turned[0][j] = pltpu.roll(o_re * w_re - o_im * w_im, back, 1)
                turned[1][j] = pltpu.roll(o_re * w_im + o_im * w_re, back, 1)
            near = lane < LANES - shift
            for part in range(2):
                for j in range(parts):
                    after = turned[part][(j + 1) % parts]
                    probe_acc[part, rows, pl.ds(j * LANES, LANES)] += jnp.where(
                        near, turned[part][j], after
                    )
        return carry

    lax.fori_loop(0, live, visit, 0)

    other = 1 - half
    total = tile_rows + edge
    for part in range(2):
        sign = 1.0 if part == 0 else -1.0
        for t in range(col_tiles):
            cols = pl.ds(t * LANES, LANES)
            send[pl.ds(part * total, total), cols] = (sign * acc[part, other, t]).astype(
                jnp.bfloat16
            )
            keep[part, :, cols] = sign * acc[part, half, t]
    side = send.shape[1] // edge
    deep = edge // side
    flip = jnp.where(other == 1, -1.0, 1.0)
    for piece in range(side):
        send[pl.ds(2 * total, deep), pl.ds(piece * edge, edge)] = (
            flip * probe_acc[other, pl.ds(piece * deep, deep), :]
        ).astype(jnp.bfloat16)
    keep_probe[...] = -flip * probe_acc[half]


def run_slots(meta, anchor, probe, spec, rim, amp, tables):
    edge = probe.shape[1]
    _, slices, tile_rows, width = spec.shape
    col_tiles = width // LANES
    total = tile_rows + edge
    side = width // edge
    vmem = pl.BlockSpec(memory_space=pltpu.VMEM)
    smem = pl.BlockSpec(memory_space=pltpu.SMEM)
    return pl.pallas_call(
        slots_kernel,
        out_shape=(
            jax.ShapeDtypeStruct((2 * total + edge // side, width), jnp.bfloat16),
            jax.ShapeDtypeStruct((2, total, width), jnp.float32),
            jax.ShapeDtypeStruct((edge, edge), jnp.float32),
        ),
        in_specs=[smem, smem] + [vmem] * 8,
        out_specs=(vmem, vmem, vmem),
        scratch_shapes=[
            pltpu.VMEM((2, slices, col_tiles, total, LANES), jnp.float32),
            pltpu.VMEM((2, slices, col_tiles, total, LANES), jnp.float32),
            pltpu.VMEM((2, edge, edge), jnp.float32),
            pltpu.VMEM((2, edge, edge), jnp.float32),
            pltpu.VMEM((2, edge, edge), jnp.float32),
            pltpu.VMEM((2, edge, edge), jnp.float32),
            pltpu.VMEM((2 * edge, edge), jnp.bfloat16),
            pltpu.VMEM((edge, 2 * edge), jnp.bfloat16),
        ],
        compiler_params=pltpu.CompilerParams(vmem_limit_bytes=48 * 1024 * 1024),
        name="slots",
    )(meta, anchor, probe, spec, rim, amp, *tables)


def traded(value, axis, distance):
    count = lax.axis_size(axis)
    return lax.ppermute(value, axis, [(i, i ^ distance) for i in range(count)])


def passed_along(value, axis, steps):
    count = lax.axis_size(axis)
    initial, last = (max(0, -steps), min(count, count - steps))
    return lax.ppermute(value, axis, [(source, source + steps) for source in range(initial, last)])


def body(probe_field, specimen, amplitude, scan_anchor, counts):
    edge = probe_field.shape[1]
    _, slices, tile_rows, width = specimen.shape
    total = tile_rows + edge
    side = width // edge
    deep = edge // side
    half = lax.axis_index("pos") % 2
    base_row = lax.axis_index("tile") * tile_rows
    meta = jnp.stack([counts[0], base_row, half]).astype(jnp.int32)
    rim = passed_along(specimen[:, :, :edge, :], "tile", -1)
    sent, kept, kept_probe = run_slots(
        meta, scan_anchor, probe_field, specimen, rim, amplitude, fixed_tables(edge)
    )
    got = traded(sent, "pos", 1)
    grad = kept + got[: 2 * total].reshape(2, total, width).astype(jnp.float32)
    got_probe = jnp.concatenate(
        [got[2 * total :, p * edge : (p + 1) * edge] for p in range(side)], 0
    )
    probe_part = kept_probe + got_probe.astype(jnp.float32)
    below = passed_along(grad[:, tile_rows:].astype(jnp.bfloat16), "tile", 1)
    lower = grad[:, edge:tile_rows].astype(jnp.bfloat16)
    lower = (lower.astype(jnp.float32) + traded(lower, "pos", 2).astype(jnp.float32)).astype(
        jnp.bfloat16
    )
    upper = (grad[:, :edge] + below.astype(jnp.float32)).astype(jnp.bfloat16)
    upper = (upper.astype(jnp.float32) + traded(upper, "pos", 2).astype(jnp.float32)).astype(
        jnp.bfloat16
    )
    distance = 2
    while distance < lax.axis_size("pos"):
        outgoing = probe_part.astype(jnp.bfloat16)
        probe_part = outgoing.astype(jnp.float32) + traded(outgoing, "pos", distance).astype(
            jnp.float32
        )
        distance *= 2
    distance = 1
    while distance < lax.axis_size("tile"):
        outgoing = probe_part.astype(jnp.bfloat16)
        probe_part = outgoing.astype(jnp.float32) + traded(outgoing, "tile", distance).astype(
            jnp.float32
        )
        distance *= 2
    mine = jnp.concatenate([upper, lower], 1)
    theirs = traded(mine, "pos", 1)
    tile_grad = jnp.where(
        half == 0, jnp.stack([mine, theirs], 1), jnp.stack([theirs, mine], 1)
    ).astype(jnp.float32)
    probe_mine = probe_part.astype(jnp.bfloat16)
    probe_theirs = traded(probe_mine, "pos", 1)
    probe_total = jnp.where(
        half == 0, jnp.stack([probe_mine, probe_theirs]), jnp.stack([probe_theirs, probe_mine])
    ).astype(jnp.float32)
    return (tile_grad, probe_total)


def solution(mesh):
    return jax.shard_map(
        body,
        mesh=mesh,
        in_specs=(
            P(),
            P(None, None, "tile", None),
            P(("tile", "pos"), None, None),
            P(("tile", "pos"), None),
            P(("tile", "pos")),
        ),
        out_specs=(P(None, None, "tile", None), P()),
        check_vma=False,
    )
```

time: 507 us -> 117 us (0.23)
  starting transfers between devices: 188 us -> 21.1 us
  waiting for transfers between devices: 218 us -> 66.5 us
  other arithmetic: 31 us -> 2.68 us
  local copies, waits for them, and re-layouts: 31.5 us -> 8.27 us
  Pallas kernels: 0 us -> 16.4 us
  between operations: 14.1 us -> 1.51 us
  loops' own time: 11.3 us -> 0 us
  matrix products: 7.9 us -> 0 us
    ppermute x2, starting transfers between devices: 188 us -> 2.6 us  [passed_along(): lax.ppermute(value, axis, [(source, source + steps) for source in range(i...]
    psum x2 -> x0, waiting for transfers between devices: 181 us -> none  [the longest x1 130 us: body(): probe_total = lax.psum(probe_acc, ('tile', 'pos'))]
    ppermute x0 -> x9, waiting for transfers between devices: none -> 30.6 us  [traded(): return lax.ppermute(value, axis, [(i, i ^ distance) for i in range(count)])]
    dynamic_update_slice x2 -> x0, local copies, waits for them, and re-layouts: 21.8 us -> none  [visit(): lax.dynamic_update_slice(object_acc, current + jnp.stack([grad_re, grad_i...]
    ppermute x0 -> x9, starting transfers between devices: none -> 18.5 us  [traded(): return lax.ppermute(value, axis, [(i, i ^ distance) for i in range(count)])]
    pallas_call x0 -> x1, Pallas kernels: none -> 16.4 us  [run_slots(): pl.pallas_call(slots_kernel, out_shape=(jax.ShapeDtypeStruct((2 * total +...]
    another operation x20 -> x3, other arithmetic: 15.3 us -> 0.87 us
    another operation x1 -> x0, loops' own time: 11.3 us -> none  [body(): object_acc, probe_acc = lax.fori_loop(0, live_total, visit, start_carry)]
  transfers between devices with their start and end apart: 4 -> 11, of which waited for: 4 -> 8; matrix products, arithmetic and copies ran while one was open for 1% -> 2% of each run, Pallas kernels for 0% -> 0%
where the time goes in v1:
time: 117 us; the launch traced here: 116 us
  waiting for transfers between devices  66.5 us (57%)
  starting transfers between devices  21.1 us (18%)
  Pallas kernels  16.4 us (14%)
  local copies, waits for them, and re-layouts  8.27 us (7%)
  other arithmetic  2.68 us (2%)
  between operations  1.51 us (1%)
    ppermute x2, waiting for transfers between devices, passed_along(): lax.ppermute(value, axis, [(source, source + steps) for source in range(i...  35.9 us
    ppermute x9, waiting for transfers between devices, traded(): return lax.ppermute(value, axis, [(i, i ^ distance) for i in range(count)])  30.6 us
    ppermute x9, starting transfers between devices, traded(): return lax.ppermute(value, axis, [(i, i ^ distance) for i in range(count)])  18.5 us
    pallas_call x1, Pallas kernels, run_slots(): pl.pallas_call(slots_kernel, out_shape=(jax.ShapeDtypeStruct((2 * total +...  16.4 us
    unnamed x18, local copies, waits for them, and re-layouts  5.68 us
    ppermute x2, starting transfers between devices, passed_along(): lax.ppermute(value, axis, [(source, source + steps) for source in range(i...  2.6 us
    slice x1, local copies, waits for them, and re-layouts, body(): rim = passed_along(specimen[:, :, :edge, :], 'tile', -1)  2.41 us
  transfers between devices with their start and end apart: 11, of which 8 were waited for; matrix products, arithmetic and copies ran while one was open for 2% of the time, Pallas kernels for 0%

profile of v1, /device:TPU:0, one launch (start us, length us, event | category | flops | bytes accessed | tf_op | source)
XLA Modules:
  0.0 116.5 jit_solution(15674728569988863583)
XLA Ops:
  0.6 0.0 copy-start.2
  0.6 0.0 copy-start.7
  0.7 0.0 copy-start
  0.7 0.0 copy-start.1
  0.7 2.4 %slice.23 = bf16[2,2,256,512]{3,2,1,0:T(8,128)(2,1)} slice(bf16[2,2,512,512]{3,2,1,0:T(8,128)(2,1)} %spec.1), slice={[0:2], [0:2], [0:256], [0:512]} | slice | bytes 2097152 | tf_op jit(solution)/shard_map/slice | solution.py:262
  3.1 1.3 %collective-permute-start = (bf16[2,2,256,512]{3,2,1,0:T(8,128)(2,1)}, bf16[2,2,256,512]{3,2,1,0:T(8,128)(2,1)S(1)}, u32[]{:S(2)}, u32[]{:S(2)}) collective-permute-start(bf16[2,2,256,512]{3,2,1,0:T(8,128)(2,1)} %slice.23), channel_id=1, source_target_pairs={{4,0},{8,4},{12,8},{16,12},{20,16},{24,20},{28,24},{5,1},{9,5},{13... | collective-permute-start | bytes 3145736 | tf_op jit(solution)/shard_map/ppermute | solution.py:250
  5.0 0.0 copy-done.7
  5.0 0.1 copy.11.anchor
  5.1 0.1 pad_add_fusion.meta
  5.2 26.1 %collective-permute-done.rim = bf16[2,2,256,512]{3,2,1,0:T(8,128)(2,1)S(1)} collective-permute-done((bf16[2,2,256,512]{3,2,1,0:T(8,128)(2,1)}, bf16[2,2,256,512]{3,2,1,0:T(8,128)(2,1)S(1)}, u32[]{:S(2)}, u32[]{:S(2)}) %collective-permute-start) | collective-permute-done | bytes 1048608 | tf_op jit(solution)/shard_map/ppermute | solution.py:250
  31.3 0.0 copy-done.2
  31.3 0.0 copy-done
  31.3 0.0 copy-done.1
  31.3 0.0 copy-start.3
  31.3 1.0 copy-done.3
  32.3 1.0 copy-done.4
  33.4 1.0 copy-done.5
  34.4 16.4 %slots.1 = (bf16[1664,512]{1,0:T(8,128)(2,1)}, f32[2,768,512]{2,1,0:T(8,128)}, f32[256,256]{1,0:T(8,128)S(1)}) custom-call(s32[3]{0:T(128)S(1)} %pad_add_fusion.meta, s32[8,2]{1,0:T(8,128)S(1)} %copy.11.anchor, f32[2,256,256]{2,1,0:T(8,128)S(1)} %copy-done.1, bf16[2,2,512,512]{3,2,1,0:T(8,128)(2,1)} %spec.1, ...), custom_call_target="tpu_custom_call" | custom-call | tf_op jit(solution)/shard_map/slots/pallas_call | solution.py:218
  50.8 10.4 %collective-permute-start.1 = (bf16[1664,512]{1,0:T(8,128)(2,1)}, bf16[1664,512]{1,0:T(8,128)(2,1)S(1)}, u32[]{:S(2)}, u32[]{:S(2)}) collective-permute-start(bf16[1664,512]{1,0:T(8,128)(2,1)} %get-tuple-element.6), channel_id=1, source_target_pairs={{0,1},{1,0},{2,3},{3,2},{4,5},{5,4},{6,7},{7,6},{8,9},{9,8},{10,11... | collective-permute-start | bytes 5111816 | tf_op jit(solution)/shard_map/ppermute | solution.py:244
  61.3 3.4 %collective-permute-done.1 = bf16[1664,512]{1,0:T(8,128)(2,1)S(1)} collective-permute-done((bf16[1664,512]{1,0:T(8,128)(2,1)}, bf16[1664,512]{1,0:T(8,128)(2,1)S(1)}, u32[]{:S(2)}, u32[]{:S(2)}) %collective-permute-start.1) | collective-permute-done | bytes 1703968 | tf_op jit(solution)/shard_map/ppermute | solution.py:244
  64.7 0.1 slice.30
  64.8 0.6 fusion.4
  65.5 0.1 fusion.6
  65.6 1.3 %collective-permute-start.2 = (bf16[2,256,512]{2,1,0:T(8,128)(2,1)S(1)}, bf16[2,256,512]{2,1,0:T(8,128)(2,1)S(1)}, u32[]{:S(2)}, u32[]{:S(2)}) collective-permute-start(bf16[2,256,512]{2,1,0:T(8,128)(2,1)S(1)} %get-tuple-element.14), channel_id=1, source_target_pairs={{0,4},{4,8},{8,12},{12,16},{16,20},{20,24},{24,28},{1,5},{5,9},{9,... | collective-permute-start | bytes 1572872 | tf_op jit(solution)/shard_map/ppermute | solution.py:250
  67.0 0.1 collective-permute-start.6
  67.0 2.0 %collective-permute-start.4 = (bf16[2,256,512]{2,1,0:T(8,128)(2,1)S(1)}, bf16[2,256,512]{2,1,0:T(8,128)(2,1)S(1)}, u32[]{:S(2)}, u32[]{:S(2)}) collective-permute-start(bf16[2,256,512]{2,1,0:T(8,128)(2,1)S(1)} %get-tuple-element.15), channel_id=1, source_target_pairs={{0,2},{1,3},{2,0},{3,1},{4,6},{5,7},{6,4},{7,5},{8,10},{9,11},{10,... | collective-permute-start | bytes 1572872 | tf_op jit(solution)/shard_map/ppermute | solution.py:244
  69.1 9.8 %collective-permute-done.2 = bf16[2,256,512]{2,1,0:T(8,128)(2,1)S(1)} collective-permute-done((bf16[2,256,512]{2,1,0:T(8,128)(2,1)S(1)}, bf16[2,256,512]{2,1,0:T(8,128)(2,1)S(1)}, u32[]{:S(2)}, u32[]{:S(2)}) %collective-permute-start.2) | collective-permute-done | bytes 524320 | tf_op jit(solution)/shard_map/ppermute | solution.py:250
  78.8 0.2 fusion.1
  79.0 0.1 collective-permute-start.3
  79.1 0.0 collective-permute-done.6
  79.1 3.3 %collective-permute-start.7 = (bf16[256,256]{1,0:T(8,128)(2,1)S(1)}, bf16[256,256]{1,0:T(8,128)(2,1)S(1)}, u32[]{:S(2)}, u32[]{:S(2)}) collective-permute-start(bf16[256,256]{1,0:T(8,128)(2,1)S(1)} %add_convert_fusion.5), channel_id=1, source_target_pairs={{0,4},{4,0},{8,12},{12,8},{16,20},{20,16},{24,28},{28,24},{1,5},{5... | collective-permute-start | bytes 393224 | tf_op jit(solution)/shard_map/ppermute | solution.py:244
  82.4 2.2 %collective-permute-done.4 = bf16[2,256,512]{2,1,0:T(8,128)(2,1)S(1)} collective-permute-done((bf16[2,256,512]{2,1,0:T(8,128)(2,1)S(1)}, bf16[2,256,512]{2,1,0:T(8,128)(2,1)S(1)}, u32[]{:S(2)}, u32[]{:S(2)}) %collective-permute-start.4) | collective-permute-done | bytes 524320 | tf_op jit(solution)/shard_map/ppermute | solution.py:244
  84.6 0.1 add_convert_fusion
  84.7 10.5 %collective-permute-done.3 = bf16[2,256,512]{2,1,0:T(8,128)(2,1)S(1)} collective-permute-done((bf16[2,256,512]{2,1,0:T(8,128)(2,1)S(1)}, bf16[2,256,512]{2,1,0:T(8,128)(2,1)S(1)}, u32[]{:S(2)}, u32[]{:S(2)}) %collective-permute-start.3) | collective-permute-done | bytes 524320 | tf_op jit(solution)/shard_map/ppermute | solution.py:244
  95.3 0.1 add_convert_fusion.1
  95.4 0.2 fusion.3
  95.6 0.1 collective-permute-start.5
  95.6 0.0 collective-permute-done.7
  95.7 2.4 %collective-permute-start.8 = (bf16[256,256]{1,0:T(8,128)(2,1)S(1)}, bf16[256,256]{1,0:T(8,128)(2,1)S(1)}, u32[]{:S(2)}, u32[]{:S(2)}) collective-permute-start(bf16[256,256]{1,0:T(8,128)(2,1)S(1)} %add_convert_fusion.4), channel_id=1, source_target_pairs={{0,8},{4,12},{8,0},{12,4},{16,24},{20,28},{24,16},{28,20},{1,9},{5... | collective-permute-start | bytes 393224 | tf_op jit(solution)/shard_map/ppermute | solution.py:244
  98.1 4.1 %collective-permute-done.8 = bf16[256,256]{1,0:T(8,128)(2,1)S(1)} collective-permute-done((bf16[256,256]{1,0:T(8,128)(2,1)S(1)}, bf16[256,256]{1,0:T(8,128)(2,1)S(1)}, u32[]{:S(2)}, u32[]{:S(2)}) %collective-permute-start.8) | collective-permute-done | bytes 131104 | tf_op jit(solution)/shard_map/ppermute | solution.py:244
  102.3 0.1 collective-permute-start.9
  102.4 9.0 %collective-permute-done.9 = bf16[256,256]{1,0:T(8,128)(2,1)S(1)} collective-permute-done((bf16[256,256]{1,0:T(8,128)(2,1)S(1)}, bf16[256,256]{1,0:T(8,128)(2,1)S(1)}, u32[]{:S(2)}, u32[]{:S(2)}) %collective-permute-start.9) | collective-permute-done | bytes 131104 | tf_op jit(solution)/shard_map/ppermute | solution.py:244
  111.4 0.1 collective-permute-start.10
  111.5 1.3 %collective-permute-done.10 = bf16[256,256]{1,0:T(8,128)(2,1)S(1)} collective-permute-done((bf16[256,256]{1,0:T(8,128)(2,1)S(1)}, bf16[256,256]{1,0:T(8,128)(2,1)S(1)}, u32[]{:S(2)}, u32[]{:S(2)}) %collective-permute-start.10) | collective-permute-done | bytes 131104 | tf_op jit(solution)/shard_map/ppermute | solution.py:244
  112.8 0.8 fusion.2
  113.6 0.0 collective-permute-done.5
  113.6 0.4 fusion
  114.0 2.5 %copy.12 = f32[2,2,512,512]{3,2,1,0:T(8,128)} copy(f32[2,2,512,512]{3,2,0,1:T(8,128)S(1)} %fusion) | data formatting | bytes 8388608
  (10 shorter events, 0.2 us)
Async XLA Ops:
  0.6 30.6 %copy-start.2 = (bf16[512,512]{1,0:T(8,128)(2,1)S(1)}, bf16[512,512]{1,0:T(8,128)(2,1)}, u32[]{:S(2)}) copy-start(bf16[512,512]{1,0:T(8,128)(2,1)} %constant.36.clone.right_f) | copy-start | bytes 1572868
  0.6 4.4 %copy-start.7 = (s32[8,2]{0,1:T(2,128)S(1)}, s32[8,2]{0,1:T(2,128)}, u32[]{:S(2)}) copy-start(s32[8,2]{0,1:T(2,128)} %param.12) | copy-start | bytes 196
  0.7 30.6 %copy-start = (bf16[8,256,256]{2,1,0:T(8,128)(2,1)S(1)}, bf16[8,256,256]{2,1,0:T(8,128)(2,1)}, u32[]{:S(2)}) copy-start(bf16[8,256,256]{2,1,0:T(8,128)(2,1)} %amp.1) | copy-start | bytes 3145732
  0.7 30.6 %copy-start.1 = (f32[2,256,256]{2,1,0:T(8,128)S(1)}, f32[2,256,256]{2,1,0:T(8,128)}, u32[]{:S(2)}) copy-start(f32[2,256,256]{2,1,0:T(8,128)} %probe.1) | copy-start | bytes 1572868
  3.1 28.2 %collective-permute-start = (bf16[2,2,256,512]{3,2,1,0:T(8,128)(2,1)}, bf16[2,2,256,512]{3,2,1,0:T(8,128)(2,1)S(1)}, u32[]{:S(2)}, u32[]{:S(2)}) collective-permute-start(bf16[2,2,256,512]{3,2,1,0:T(8,128)(2,1)} %slice.23), channel_id=1, source_target_pairs={{4,0},{8,4},{12,8},{16,12},{20,16},{24,20},{28,24},{5,1},{9,5},{13... | collective-permute-start | bytes 3145736 | tf_op jit(solution)/shard_map/ppermute | solution.py:250
  31.3 1.0 copy-start.3
  32.3 1.0 copy-start.4
  33.4 1.0 copy-start.5
  50.8 14.0 %copy-start.6 = (f32[2,768,512]{2,1,0:T(8,128)S(1)}, f32[2,768,512]{2,1,0:T(8,128)}, u32[]{:S(2)}) copy-start(f32[2,768,512]{2,1,0:T(8,128)} %get-tuple-element.5) | copy-start | bytes 9437188
  50.8 13.9 %collective-permute-start.1 = (bf16[1664,512]{1,0:T(8,128)(2,1)}, bf16[1664,512]{1,0:T(8,128)(2,1)S(1)}, u32[]{:S(2)}, u32[]{:S(2)}) collective-permute-start(bf16[1664,512]{1,0:T(8,128)(2,1)} %get-tuple-element.6), channel_id=1, source_target_pairs={{0,1},{1,0},{2,3},{3,2},{4,5},{5,4},{6,7},{7,6},{8,9},{9,8},{10,11... | collective-permute-start | bytes 5111816 | tf_op jit(solution)/shard_map/ppermute | solution.py:244
  65.6 13.3 %collective-permute-start.2 = (bf16[2,256,512]{2,1,0:T(8,128)(2,1)S(1)}, bf16[2,256,512]{2,1,0:T(8,128)(2,1)S(1)}, u32[]{:S(2)}, u32[]{:S(2)}) collective-permute-start(bf16[2,256,512]{2,1,0:T(8,128)(2,1)S(1)} %get-tuple-element.14), channel_id=1, source_target_pairs={{0,4},{4,8},{8,12},{12,16},{16,20},{20,24},{24,28},{1,5},{5,9},{9,... | collective-permute-start | bytes 1572872 | tf_op jit(solution)/shard_map/ppermute | solution.py:250
  67.0 12.1 %collective-permute-start.6 = (bf16[256,256]{1,0:T(8,128)(2,1)S(1)}, bf16[256,256]{1,0:T(8,128)(2,1)S(1)}, u32[]{:S(2)}, u32[]{:S(2)}) collective-permute-start(bf16[256,256]{1,0:T(8,128)(2,1)S(1)} %add_convert_fusion.6), channel_id=1, source_target_pairs={{0,2},{1,3},{2,0},{3,1},{4,6},{5,7},{6,4},{7,5},{8,10},{9,11},{10,... | collective-permute-start | bytes 393224 | tf_op jit(solution)/shard_map/ppermute | solution.py:244
  67.0 17.6 %collective-permute-start.4 = (bf16[2,256,512]{2,1,0:T(8,128)(2,1)S(1)}, bf16[2,256,512]{2,1,0:T(8,128)(2,1)S(1)}, u32[]{:S(2)}, u32[]{:S(2)}) collective-permute-start(bf16[2,256,512]{2,1,0:T(8,128)(2,1)S(1)} %get-tuple-element.15), channel_id=1, source_target_pairs={{0,2},{1,3},{2,0},{3,1},{4,6},{5,7},{6,4},{7,5},{8,10},{9,11},{10,... | collective-permute-start | bytes 1572872 | tf_op jit(solution)/shard_map/ppermute | solution.py:244
  79.0 16.3 %collective-permute-start.3 = (bf16[2,256,512]{2,1,0:T(8,128)(2,1)S(1)}, bf16[2,256,512]{2,1,0:T(8,128)(2,1)S(1)}, u32[]{:S(2)}, u32[]{:S(2)}) collective-permute-start(bf16[2,256,512]{2,1,0:T(8,128)(2,1)S(1)} %fusion.1), channel_id=1, source_target_pairs={{0,2},{1,3},{2,0},{3,1},{4,6},{5,7},{6,4},{7,5},{8,10},{9,11},{10,... | collective-permute-start | bytes 1572872 | tf_op jit(solution)/shard_map/ppermute | solution.py:244
  79.1 16.5 %collective-permute-start.7 = (bf16[256,256]{1,0:T(8,128)(2,1)S(1)}, bf16[256,256]{1,0:T(8,128)(2,1)S(1)}, u32[]{:S(2)}, u32[]{:S(2)}) collective-permute-start(bf16[256,256]{1,0:T(8,128)(2,1)S(1)} %add_convert_fusion.5), channel_id=1, source_target_pairs={{0,4},{4,0},{8,12},{12,8},{16,20},{20,16},{24,28},{28,24},{1,5},{5... | collective-permute-start | bytes 393224 | tf_op jit(solution)/shard_map/ppermute | solution.py:244
  95.6 18.1 %collective-permute-start.5 = (bf16[2,512,512]{2,1,0:T(8,128)(2,1)S(1)}, bf16[2,512,512]{2,1,0:T(8,128)(2,1)S(1)}, u32[]{:S(2)}, u32[]{:S(2)}) collective-permute-start(bf16[2,512,512]{2,1,0:T(8,128)(2,1)S(1)} %get-tuple-element.17), channel_id=1, source_target_pairs={{0,1},{1,0},{2,3},{3,2},{4,5},{5,4},{6,7},{7,6},{8,9},{9,8},{10,11... | collective-permute-start | bytes 3145736 | tf_op jit(solution)/shard_map/ppermute | solution.py:244
  95.7 6.5 %collective-permute-start.8 = (bf16[256,256]{1,0:T(8,128)(2,1)S(1)}, bf16[256,256]{1,0:T(8,128)(2,1)S(1)}, u32[]{:S(2)}, u32[]{:S(2)}) collective-permute-start(bf16[256,256]{1,0:T(8,128)(2,1)S(1)} %add_convert_fusion.4), channel_id=1, source_target_pairs={{0,8},{4,12},{8,0},{12,4},{16,24},{20,28},{24,16},{28,20},{1,9},{5... | collective-permute-start | bytes 393224 | tf_op jit(solution)/shard_map/ppermute | solution.py:244
  102.3 9.1 %collective-permute-start.9 = (bf16[256,256]{1,0:T(8,128)(2,1)S(1)}, bf16[256,256]{1,0:T(8,128)(2,1)S(1)}, u32[]{:S(2)}, u32[]{:S(2)}) collective-permute-start(bf16[256,256]{1,0:T(8,128)(2,1)S(1)} %add_convert_fusion.3), channel_id=1, source_target_pairs={{0,16},{4,20},{8,24},{12,28},{16,0},{20,4},{24,8},{28,12},{1,17},{... | collective-permute-start | bytes 393224 | tf_op jit(solution)/shard_map/ppermute | solution.py:244
  111.4 1.4 %collective-permute-start.10 = (bf16[256,256]{1,0:T(8,128)(2,1)S(1)}, bf16[256,256]{1,0:T(8,128)(2,1)S(1)}, u32[]{:S(2)}, u32[]{:S(2)}) collective-permute-start(bf16[256,256]{1,0:T(8,128)(2,1)S(1)} %add_convert_fusion.2), channel_id=1, source_target_pairs={{0,1},{1,0},{2,3},{3,2},{4,5},{5,4},{6,7},{7,6},{8,9},{9,8},{10,11... | collective-permute-start | bytes 393224 | tf_op jit(solution)/shard_map/ppermute | solution.py:244

commit v2 on v0

v2 whole, which is shorter than its diff:
```python
import math

import jax
import jax.numpy as jnp
import ml_dtypes
import numpy as np
from jax import lax
from jax.experimental import pallas as pl
from jax.experimental.pallas import tpu as pltpu
from jax.sharding import PartitionSpec as P

PROP_COEF = 0.5
AMP_EPS = 0.05
LANES = 128
CHUNK = 32


def fixed_tables(edge):
    index = np.arange(edge)
    angles = (np.outer(index, index) % edge) * (2.0 * math.pi / edge)
    cosine = (np.cos(angles) / math.sqrt(edge)).astype(ml_dtypes.bfloat16).astype(np.float64)
    sine = (np.sin(angles) / math.sqrt(edge)).astype(ml_dtypes.bfloat16).astype(np.float64)
    forward = cosine - 1j * sine
    centred = np.where(index < edge // 2, index, index - edge)
    ramp = np.exp(-1j * (PROP_COEF * math.pi / edge) * centred * centred)
    spread = (np.conj(forward) * ramp[None, :]) @ forward

    def left_form(matrix):
        return np.block([[matrix.real, -matrix.imag], [matrix.imag, matrix.real]])

    tables = []
    for matrix in (spread, forward):
        tables += [left_form(matrix), left_form(matrix).T]
    return [jnp.asarray(table.astype(ml_dtypes.bfloat16)) for table in tables]


def interleaved(first, second):
    marks = [(k / len(first), 0, k) for k in range(len(first))]
    marks += [((k + 0.5) / len(second), 1, k) for k in range(len(second))]
    for _, which, k in sorted(marks):
        (first, second)[which][k]()


def slot_stages(slot, alive, base_row, refs, work):
    anchor, probe, amp, tables, wide, acc, probe_acc = refs
    rolled, arriving, field, stack, joined = work
    left_a, right_a, left_f, right_f = tables
    edge = probe.shape[1]
    col_tiles = wide.shape[2]
    parts = edge // LANES
    lane = lax.broadcasted_iota(jnp.int32, (CHUNK, LANES), 1)
    row = anchor[slot, 0] - base_row
    col = anchor[slot, 1]
    first = jnp.minimum(col // LANES, col_tiles - parts - 1)
    shift = col - first * LANES
    turn = jnp.where(shift >= LANES, 0, shift)
    back = jnp.where(turn == 0, 0, LANES - turn)
    own = lane >= shift
    near = lane < LANES - shift

    def patch(part, s, i, j):
        rows = pl.ds(row + i, CHUNK)
        main = wide[part, s, first + j, rows, :]
        if j > 0:
            return main
        return jnp.where(own, main, wide[part, s, first + parts, rows, :])

    def place(part, s, i, j, value):
        rows = pl.ds(row + i, CHUNK)
        if j > 0:
            acc[part, s, first + j, rows, :] += value
        else:
            acc[part, s, first, rows, :] += jnp.where(own, value, 0.0)
            acc[part, s, first + parts, rows, :] += jnp.where(own, 0.0, value)

    def put(i, j, re, im):
        cols = pl.ds(j * LANES, LANES)
        stack[pl.ds(i, CHUNK), cols] = re.astype(jnp.bfloat16)
        stack[pl.ds(edge + i, CHUNK), cols] = im.astype(jnp.bfloat16)

    def halves():
        return [(j, pl.ds(j * LANES, LANES)) for j in range(parts)]

    def enter(i):
        rows = pl.ds(i, CHUNK)
        turned = [
            [pltpu.roll(probe[part, rows, cols], turn, 1) for j, cols in halves()]
            for part in range(2)
        ]
        for j, cols in halves():
            u_re, u_im = [
                jnp.where(own, turned[part][j], turned[part][j - 1]) for part in range(2)
            ]
            rolled[0, rows, cols] = u_re
            rolled[1, rows, cols] = u_im
            o_re, o_im = patch(0, 0, i, j), patch(1, 0, i, j)
            put(i, j, u_re * o_re - u_im * o_im, u_re * o_im + u_im * o_re)

    def second_slice(i):
        rows = pl.ds(i, CHUNK)
        for j, cols in halves():
            u_re, u_im = arriving[0, rows, cols], arriving[1, rows, cols]
            o_re, o_im = patch(0, 1, i, j), patch(1, 1, i, j)
            put(i, j, u_re * o_re - u_im * o_im, u_re * o_im + u_im * o_re)

    def residual(i):
        rows = pl.ds(i, CHUNK)
        for j, cols in halves():
            far_re, far_im = field[0, rows, cols], field[1, rows, cols]
            measured = amp[slot, rows, cols].astype(jnp.float32) * alive
            ratio = measured * lax.rsqrt(far_re * far_re + far_im * far_im + AMP_EPS)
            put(i, j, (alive - ratio) * far_re, (ratio - alive) * far_im)

    def second_grad(i):
        rows = pl.ds(i, CHUNK)
        for j, cols in halves():
            u_re, u_im = arriving[0, rows, cols], arriving[1, rows, cols]
            w_re, w_im = field[0, rows, cols], field[1, rows, cols]
            place(0, 1, i, j, u_re * w_re - u_im * w_im)
            place(1, 1, i, j, u_re * w_im + u_im * w_re)
            o_re, o_im = patch(0, 1, i, j), patch(1, 1, i, j)
            put(i, j, o_re * w_re - o_im * w_im, o_re * w_im + o_im * w_re)

    def first_grad(i):
        rows = pl.ds(i, CHUNK)
        turned = [[None] * parts for _ in range(2)]
        for j, cols in halves():
            u_re, u_im = rolled[0, rows, cols], rolled[1, rows, cols]
            w_re, w_im = field[0, rows, cols], field[1, rows, cols]
            place(0, 0, i, j, u_re * w_re - u_im * w_im)
            place(1, 0, i, j, u_re * w_im + u_im * w_re)
            o_re, o_im = patch(0, 0, i, j), patch(1, 0, i, j)
            turned[0][j] = pltpu.roll(o_re * w_re - o_im * w_im, back, 1)
            turned[1][j] = pltpu.roll(o_re * w_im + o_im * w_re, back, 1)
        for part in range(2):
            for j, cols in halves():
                after = turned[part][(j + 1) % parts]
                probe_acc[part, rows, cols] += jnp.where(near, turned[part][j], after)

    def two_sided(left, right, out):
        def rows_of(part):
            span = pl.ds(part * edge, edge)
            joined[:, span] = jnp.dot(
                left[span, :], stack[...], preferred_element_type=jnp.float32
            ).astype(jnp.bfloat16)

        def cols_of(part):
            out[part] = jnp.dot(
                joined[...],
                right[:, pl.ds(part * edge, edge)],
                preferred_element_type=jnp.float32,
            )

        return [lambda p=p: rows_of(p) for p in range(2)] + [
            lambda p=p: cols_of(p) for p in range(2)
        ]

    def each(step):
        return [lambda i=i: step(i) for i in range(0, edge, CHUNK)]

    return [
        each(enter),
        two_sided(left_a, right_a, arriving),
        each(second_slice),
        two_sided(left_f, right_f, field),
        each(residual),
        two_sided(left_f, right_f, field),
        each(second_grad),
        two_sided(left_a, right_a, field),
        each(first_grad),
    ]


def listed(order, anchor, live, base_row, edge, tile_rows, second_call):
    slots = anchor.shape[0]
    inner = [
        jnp.where((q < live) & (anchor[q, 0] - base_row + edge <= tile_rows), 1, 0)
        for q in range(slots)
    ]
    early = sum(inner) // 2 * 2
    taken = jnp.int32(0)
    rank = jnp.int32(0)
    order[0] = 0
    for q in range(slots):
        ahead = jnp.where(rank < early, inner[q], 0)
        rank = rank + inner[q]
        take = jnp.where(q < live, 1 - ahead, 0) if second_call else ahead
        order[taken] = q
        taken = taken + take
    return taken


def run_pairs(order, total, base_row, refs, work):
    def visit(step, carry):
        a = order[2 * step]
        b_lives = 2 * step + 1 < total
        b = jnp.where(b_lives, order[2 * step + 1], a)
        ones = slot_stages(a, 1.0, base_row, refs, work[0])
        twos = slot_stages(b, jnp.where(b_lives, 1.0, 0.0), base_row, refs, work[1])
        for step_now in ones[0]:
            step_now()
        for k in range(1, len(ones)):
            if k % 2:
                interleaved(ones[k], twos[k - 1])
            else:
                interleaved(twos[k - 1], ones[k])
        for step_now in twos[-1]:
            step_now()
        return carry

    lax.fori_loop(0, (total + 1) // 2, visit, 0)


def widen(wide, source, start, part, s_from, s_to):
    rows = source.shape[-2]
    for t in range(wide.shape[2]):
        wide[part, s_to, t, pl.ds(start, rows), :] = source[
            part, s_from, :, pl.ds(t * LANES, LANES)
        ].astype(jnp.float32)


def early_kernel(
    meta, anchor, probe, spec, amp, la, ra, lf, rf, acc, probe_acc, order, wide, *work
):
    slices, tile_rows = spec.shape[1:3]
    for part in range(2):
        for s in range(slices):
            widen(wide, spec, 0, part, s, s)
            for t in range(wide.shape[2]):
                acc[part, s, t] = jnp.zeros(acc.shape[3:], jnp.float32)
    probe_acc[...] = jnp.zeros(probe_acc.shape, jnp.float32)
    total = listed(order, anchor, meta[0], meta[1], probe.shape[1], tile_rows, False)
    refs = (anchor, probe, amp, (la, ra, lf, rf), wide, acc, probe_acc)
    run_pairs(order, total, meta[1], refs, (work[:5], work[5:]))


def late_kernel(
    meta,
    anchor,
    probe,
    spec,
    rim_own,
    rim_other,
    acc_in,
    probe_in,
    amp,
    la,
    ra,
    lf,
    rf,
    send_low,
    send_top,
    keep_low,
    keep_top,
    keep_probe,
    order,
    wide,
    acc,
    probe_acc,
    *work,
):
    slices, tile_rows, width = spec.shape[1:]
    edge = probe.shape[1]
    half = meta[2]
    other = 1 - half
    col_tiles = width // LANES
    for part in range(2):
        for s in range(slices):
            widen(wide, spec, 0, part, s, s)
            for t in range(col_tiles):
                acc[part, s, t, pl.ds(0, tile_rows), :] = acc_in[part, s, t]
                acc[part, s, t, pl.ds(tile_rows, edge), :] = jnp.zeros((edge, LANES), jnp.float32)
        widen(wide, rim_own, tile_rows, part, 0, half)
        widen(wide, rim_other, tile_rows, part, 0, other)
    probe_acc[...] = probe_in[...]
    total = listed(order, anchor, meta[0], meta[1], edge, tile_rows, True)
    refs = (anchor, probe, amp, (la, ra, lf, rf), wide, acc, probe_acc)
    run_pairs(order, total, meta[1], refs, (work[:5], work[5:]))

    low = pl.ds(edge, tile_rows)
    top = pl.ds(0, edge)
    for part in range(2):
        sign = 1.0 if part == 0 else -1.0
        for t in range(col_tiles):
            cols = pl.ds(t * LANES, LANES)
            send_low[part, :, cols] = (sign * acc[part, other, t, low, :]).astype(jnp.bfloat16)
            keep_low[part, :, cols] = sign * acc[part, half, t, low, :]
            send_top[pl.ds(part * edge, edge), cols] = (sign * acc[part, other, t, top, :]).astype(
                jnp.bfloat16
            )
            keep_top[part, :, cols] = sign * acc[part, half, t, top, :]
    side = width // edge
    deep = edge // side
    flip = jnp.where(other == 1, -1.0, 1.0)
    for piece in range(side):
        send_top[pl.ds(2 * edge, deep), pl.ds(piece * edge, edge)] = (
            flip * probe_acc[other, pl.ds(piece * deep, deep), :]
        ).astype(jnp.bfloat16)
    keep_probe[...] = -flip * probe_acc[half]


VMEM = pl.BlockSpec(memory_space=pltpu.VMEM)
SMEM = pl.BlockSpec(memory_space=pltpu.SMEM)


def scratch(slots, slices, col_tiles, rows, edge):
    one = [
        pltpu.VMEM((2, edge, edge), jnp.float32),
        pltpu.VMEM((2, edge, edge), jnp.float32),
        pltpu.VMEM((2, edge, edge), jnp.float32),
        pltpu.VMEM((2 * edge, edge), jnp.bfloat16),
        pltpu.VMEM((edge, 2 * edge), jnp.bfloat16),
    ]
    order = pltpu.SMEM((slots + 1,), jnp.int32)
    return [order, pltpu.VMEM((2, slices, col_tiles, rows, LANES), jnp.float32)], one + one


def run_early(meta, anchor, probe, spec, amp, tables):
    edge = probe.shape[1]
    _, slices, tile_rows, width = spec.shape
    col_tiles = width // LANES
    lead, work = scratch(anchor.shape[0], slices, col_tiles, tile_rows, edge)
    return pl.pallas_call(
        early_kernel,
        out_shape=(
            jax.ShapeDtypeStruct((2, slices, col_tiles, tile_rows, LANES), jnp.float32),
            jax.ShapeDtypeStruct((2, edge, edge), jnp.float32),
        ),
        in_specs=[SMEM, SMEM] + [VMEM] * 7,
        out_specs=(VMEM, VMEM),
        scratch_shapes=lead + work,
        compiler_params=pltpu.CompilerParams(vmem_limit_bytes=40 * 1024 * 1024),
        name="early_slots",
    )(meta, anchor, probe, spec, amp, *tables)


def run_late(meta, anchor, probe, spec, rim_own, rim_other, acc, probe_acc, amp, tables):
    edge = probe.shape[1]
    _, slices, tile_rows, width = spec.shape
    col_tiles = width // LANES
    total = tile_rows + edge
    side = width // edge
    lead, work = scratch(anchor.shape[0], slices, col_tiles, total, edge)
    return pl.pallas_call(
        late_kernel,
        out_shape=(
            jax.ShapeDtypeStruct((2, tile_rows, width), jnp.bfloat16),
            jax.ShapeDtypeStruct((2 * edge + edge // side, width), jnp.bfloat16),
            jax.ShapeDtypeStruct((2, tile_rows, width), jnp.float32),
            jax.ShapeDtypeStruct((2, edge, width), jnp.float32),
            jax.ShapeDtypeStruct((edge, edge), jnp.float32),
        ),
        in_specs=[SMEM, SMEM] + [VMEM] * 11,
        out_specs=(VMEM,) * 5,
        scratch_shapes=lead
        + [
            pltpu.VMEM((2, slices, col_tiles, total, LANES), jnp.float32),
            pltpu.VMEM((2, edge, edge), jnp.float32),
        ]
        + work,
        compiler_params=pltpu.CompilerParams(vmem_limit_bytes=48 * 1024 * 1024),
        name="late_slots",
    )(meta, anchor, probe, spec, rim_own, rim_other, acc, probe_acc, amp, *tables)


def traded(value, axis, distance):
    count = lax.axis_size(axis)
    return lax.ppermute(value, axis, [(i, i ^ distance) for i in range(count)])


def passed_along(value, axis, steps):
    count = lax.axis_size(axis)
    initial, last = (max(0, -steps), min(count, count - steps))
    return lax.ppermute(value, axis, [(source, source + steps) for source in range(initial, last)])


def narrow_sum(own, got):
    return (own.astype(jnp.float32) + got.astype(jnp.float32)).astype(jnp.bfloat16)


def body(probe_field, specimen, amplitude, scan_anchor, counts):
    edge = probe_field.shape[1]
    _, slices, tile_rows, width = specimen.shape
    side = width // edge
    half = lax.axis_index("pos") % 2
    base_row = lax.axis_index("tile") * tile_rows
    meta = jnp.stack([counts[0], base_row, half]).astype(jnp.int32)
    tables = fixed_tables(edge)
    rim_own = passed_along(
        lax.dynamic_slice(specimen, (0, half, 0, 0), (2, 1, edge, width)), "tile", -1
    )
    rim_other = traded(rim_own, "pos", 1)
    acc, probe_acc = run_early(meta, scan_anchor, probe_field, specimen, amplitude, tables)
    sent_low, sent_top, kept_low, kept_top, kept_probe = run_late(
        meta,
        scan_anchor,
        probe_field,
        specimen,
        rim_own,
        rim_other,
        acc,
        probe_acc,
        amplitude,
        tables,
    )
    got_low = traded(sent_low, "pos", 1)
    got_top = traded(sent_top, "pos", 1)
    low = (kept_low + got_low.astype(jnp.float32)).astype(jnp.bfloat16)
    below = passed_along(low[:, tile_rows - edge :], "tile", 1)
    lower = low[:, : tile_rows - edge]
    lower_got = traded(lower, "pos", 2)
    top = kept_top + got_top[: 2 * edge].reshape(2, edge, width).astype(jnp.float32)
    got_probe = jnp.concatenate(
        [got_top[2 * edge :, p * edge : (p + 1) * edge] for p in range(side)], 0
    )
    probe_part = (kept_probe + got_probe.astype(jnp.float32)).astype(jnp.bfloat16)
    probe_part = narrow_sum(probe_part, traded(probe_part, "pos", 2))
    probe_part = narrow_sum(probe_part, traded(probe_part, "tile", 1))
    below, probe_part = lax.optimization_barrier((below, probe_part))
    upper = (top + below.astype(jnp.float32)).astype(jnp.bfloat16)
    upper_got = traded(upper, "pos", 2)
    distance = 2
    while distance < lax.axis_size("tile"):
        probe_part = narrow_sum(probe_part, traded(probe_part, "tile", distance))
        distance *= 2
    lower = narrow_sum(lower, lower_got)
    lower_theirs = traded(lower, "pos", 1)
    probe_theirs = traded(probe_part, "pos", 1)
    upper_got, lower_theirs, probe_theirs = lax.optimization_barrier(
        (upper_got, lower_theirs, probe_theirs)
    )
    upper = narrow_sum(upper, upper_got)
    upper_theirs = traded(upper, "pos", 1)
    mine = jnp.concatenate([upper, lower], 1)
    theirs = jnp.concatenate([upper_theirs, lower_theirs], 1)
    tile_grad = jnp.where(
        half == 0, jnp.stack([mine, theirs], 1), jnp.stack([theirs, mine], 1)
    ).astype(jnp.float32)
    probe_total = jnp.where(
        half == 0, jnp.stack([probe_part, probe_theirs]), jnp.stack([probe_theirs, probe_part])
    ).astype(jnp.float32)
    return (tile_grad, probe_total)


def solution(mesh):
    return jax.shard_map(
        body,
        mesh=mesh,
        in_specs=(
            P(),
            P(None, None, "tile", None),
            P(("tile", "pos"), None, None),
            P(("tile", "pos"), None),
            P(("tile", "pos")),
        ),
        out_specs=(P(None, None, "tile", None), P()),
        check_vma=False,
    )
```

time: 507 us -> 98.5 us (0.19); the launches traced: 502 us -> 98.9 us
  waiting for transfers between devices: 218 us -> 38.6 us
  starting transfers between devices: 188 us -> 25 us
  other arithmetic: 31 us -> 4.08 us
  local copies, waits for them, and re-layouts: 31.5 us -> 14.4 us
  Pallas kernels: 0 us -> 15.3 us
  between operations: 14.1 us -> 1.51 us
  loops' own time: 11.3 us -> 0 us
  matrix products: 7.9 us -> 0 us
    ppermute x2, starting transfers between devices: 188 us -> 5.23 us  [passed_along(): lax.ppermute(value, axis, [(source, source + steps) for source in range(i...]
    psum x2 -> x0, waiting for transfers between devices: 181 us -> none  [the longest x1 130 us: body(): probe_total = lax.psum(probe_acc, ('tile', 'pos'))]
    dynamic_update_slice x2 -> x0, local copies, waits for them, and re-layouts: 21.8 us -> none  [visit(): lax.dynamic_update_slice(object_acc, current + jnp.stack([grad_re, grad_i...]
    ppermute x0 -> x12, waiting for transfers between devices: none -> 20.7 us  [traded(): return lax.ppermute(value, axis, [(i, i ^ distance) for i in range(count)])]
    ppermute x0 -> x12, starting transfers between devices: none -> 19.7 us  [traded(): return lax.ppermute(value, axis, [(i, i ^ distance) for i in range(count)])]
    ppermute x2, waiting for transfers between devices: 36.7 us -> 17.9 us  [passed_along(): lax.ppermute(value, axis, [(source, source + steps) for source in range(i...]
    pallas_call x0 -> x2, Pallas kernels: none -> 15.3 us  [the longest x1 10.2 us: run_late(): pl.pallas_call(late_kernel, out_shape=(jax.ShapeDtypeStruct((2, tile_rows...]
    another operation x20 -> x3, other arithmetic: 15.3 us -> 0.21 us  [the longest x2 0.14 us: body(): jnp.stack([mine, theirs], 1)]
  transfers between devices with their start and end apart: 4 -> 14, of which waited for: 4 -> 11; matrix products, arithmetic and copies ran while one was open for 1% -> 4% of each run, Pallas kernels for 0% -> 5%
where the time goes in v2:
time: 98.5 us; the launch traced here: 98.9 us
  waiting for transfers between devices  38.6 us (39%)
  starting transfers between devices  25 us (25%)
  Pallas kernels  15.3 us (16%)
  local copies, waits for them, and re-layouts  14.4 us (15%)
  other arithmetic  4.08 us (4%)
  between operations  1.51 us (2%)
    ppermute x12, waiting for transfers between devices, traded(): return lax.ppermute(value, axis, [(i, i ^ distance) for i in range(count)])  20.7 us
    ppermute x12, starting transfers between devices, traded(): return lax.ppermute(value, axis, [(i, i ^ distance) for i in range(count)])  19.7 us
    ppermute x2, waiting for transfers between devices, passed_along(): lax.ppermute(value, axis, [(source, source + steps) for source in range(i...  17.9 us
    unnamed x32, local copies, waits for them, and re-layouts  13.3 us
    pallas_call x1, Pallas kernels, run_late(): pl.pallas_call(late_kernel, out_shape=(jax.ShapeDtypeStruct((2, tile_rows...  10.2 us
    ppermute x2, starting transfers between devices, passed_along(): lax.ppermute(value, axis, [(source, source + steps) for source in range(i...  5.23 us
    pallas_call x1, Pallas kernels, run_early(): pl.pallas_call(early_kernel, out_shape=(jax.ShapeDtypeStruct((2, slices,...  5.06 us
    convert_element_type x1, other arithmetic, body(): low = (kept_low + got_low.astype(jnp.float32)).astype(jnp.bfloat16)  2.01 us
  transfers between devices with their start and end apart: 14, of which 11 were waited for; matrix products, arithmetic and copies ran while one was open for 4% of the time, Pallas kernels for 5%

profile of v2, /device:TPU:0, one launch (start us, length us, event | category | flops | bytes accessed | tf_op | source)
XLA Modules:
  0.0 98.9 jit_solution(5374334644690102892)
XLA Ops:
  0.6 1.1 %constant_dynamic-slice_fusion = bf16[2,1,256,512]{3,2,1,0:T(8,128)(2,1)S(1)} fusion(bf16[2,2,512,512]{3,2,1,0:T(8,128)(2,1)} %spec.3, s32[]{:T(128)S(6)} %select_n.28), kind=kLoop, calls=%fused_computation.18 | loop fusion | bytes 1048580 | tf_op jit(solution)/shard_map/dynamic_slice | solution.py:390
  1.7 1.3 %collective-permute-start = (bf16[2,1,256,512]{3,2,1,0:T(8,128)(2,1)S(1)}, bf16[2,1,256,512]{3,2,1,0:T(8,128)(2,1)S(1)}, u32[]{:S(2)}, u32[]{:S(2)}) collective-permute-start(bf16[2,1,256,512]{3,2,1,0:T(8,128)(2,1)S(1)} %constant_dynamic-slice_fusion), channel_id=1, source_target_pairs={{4,0},{8,4},{12,8},{16,12},{20,16},{24,20},{28,24},{5,1},{9,5},{13... | collective-permute-start | bytes 1572872 | tf_op jit(solution)/shard_map/ppermute | solution.py:374
  3.0 15.5 %collective-permute-done.rim_own = bf16[2,1,256,512]{3,2,1,0:T(8,128)(2,1)S(1)} collective-permute-done((bf16[2,1,256,512]{3,2,1,0:T(8,128)(2,1)S(1)}, bf16[2,1,256,512]{3,2,1,0:T(8,128)(2,1)S(1)}, u32[]{:S(2)}, u32[]{:S(2)}) %collective-permute-start) | collective-permute-done | bytes 524320 | tf_op jit(solution)/shard_map/ppermute | solution.py:374
  19.2 0.8 copy.12.anchor
  19.9 0.1 pad_add_fusion.meta
  20.0 1.6 %copy-done = bf16[2,2,512,512]{3,2,1,0:T(8,128)(2,1)S(1)} copy-done((bf16[2,2,512,512]{3,2,1,0:T(8,128)(2,1)S(1)}, bf16[2,2,512,512]{3,2,1,0:T(8,128)(2,1)}, u32[]{:S(2)}) %copy-start) | copy-done | bytes 2097176
  21.6 1.2 %copy-done.2 = bf16[8,256,256]{2,1,0:T(8,128)(2,1)S(1)} copy-done((bf16[8,256,256]{2,1,0:T(8,128)(2,1)S(1)}, bf16[8,256,256]{2,1,0:T(8,128)(2,1)}, u32[]{:S(2)}) %copy-start.2) | copy-done | bytes 1048600
  22.8 1.0 %copy-done.3 = f32[2,256,256]{2,1,0:T(8,128)S(1)} copy-done((f32[2,256,256]{2,1,0:T(8,128)S(1)}, f32[2,256,256]{2,1,0:T(8,128)}, u32[]{:S(2)}) %copy-start.3) | copy-done | bytes 524312
  23.8 1.0 %copy-done.5 = bf16[512,512]{1,0:T(8,128)(2,1)S(1)} copy-done((bf16[512,512]{1,0:T(8,128)(2,1)S(1)}, bf16[512,512]{1,0:T(8,128)(2,1)}, u32[]{:S(2)}) %copy-start.5) | copy-done | bytes 524312
  24.9 1.0 %copy-done.7 = bf16[512,512]{1,0:T(8,128)(2,1)S(1)} copy-done((bf16[512,512]{1,0:T(8,128)(2,1)S(1)}, bf16[512,512]{1,0:T(8,128)(2,1)}, u32[]{:S(2)}) %copy-start.7) | copy-done | bytes 524312
  25.9 1.0 %copy-done.9 = bf16[512,512]{1,0:T(8,128)(2,1)S(1)} copy-done((bf16[512,512]{1,0:T(8,128)(2,1)S(1)}, bf16[512,512]{1,0:T(8,128)(2,1)}, u32[]{:S(2)}) %copy-start.9) | copy-done | bytes 524312
  27.0 1.0 %copy-done.11 = bf16[512,512]{1,0:T(8,128)(2,1)S(1)} copy-done((bf16[512,512]{1,0:T(8,128)(2,1)S(1)}, bf16[512,512]{1,0:T(8,128)(2,1)}, u32[]{:S(2)}) %copy-start.11) | copy-done | bytes 524312
  28.0 0.0 copy-start.12
  28.0 5.1 %early_slots.1 = (f32[2,2,4,512,128]{4,3,2,1,0:T(8,128)S(1)}, f32[2,256,256]{2,1,0:T(8,128)S(1)}) custom-call(s32[3]{0:T(128)S(1)} %pad_add_fusion.meta, s32[8,2]{1,0:T(8,128)S(1)} %copy.12.anchor, f32[2,256,256]{2,1,0:T(8,128)S(1)} %copy-done.3, bf16[2,2,512,512]{3,2,1,0:T(8,128)(2,1)S(1)} %copy-done, bf16[8,256,256]{2,1,0:T(8,128)(2,1)S(1)} %copy-done.2, ...), custom_call_target="tpu_custom_call" | custom-call | tf_op jit(solution)/shard_map/early_slots/pallas_call | solution.py:323
  33.1 0.0 copy-start.1
  33.1 2.0 %copy-done.1 = f32[2,2,4,512,128]{4,3,2,1,0:T(8,128)} copy-done((f32[2,2,4,512,128]{4,3,2,1,0:T(8,128)}, f32[2,2,4,512,128]{4,3,2,1,0:T(8,128)S(1)}, u32[]{:S(2)}) %copy-start.1) | copy-done | bytes 4194328
  35.2 10.2 %late_slots.1 = (bf16[2,512,512]{2,1,0:T(8,128)(2,1)S(1)}, bf16[640,512]{1,0:T(8,128)(2,1)S(1)}, f32[2,512,512]{2,1,0:T(8,128)}, f32[2,256,512]{2,1,0:T(8,128)}, f32[256,256]{1,0:T(8,128)S(1)}) custom-call(s32[3]{0:T(128)S(1)} %pad_add_fusion.meta, s32[8,2]{1,0:T(8,128)S(1)} %copy.12.anchor, f32[2,256,256]{2,1,0:T(8,128)S(1)} %copy-done.4, ...), custom_call_target="tpu_custom_call" | custom-call | tf_op jit(solution)/shard_map/late_slots/pallas_call | solution.py:344
  45.4 0.5 collective-permute-start.2
  45.9 1.7 %collective-permute-done.2 = bf16[640,512]{1,0:T(8,128)(2,1)S(1)} collective-permute-done((bf16[640,512]{1,0:T(8,128)(2,1)S(1)}, bf16[640,512]{1,0:T(8,128)(2,1)S(1)}, u32[]{:S(2)}, u32[]{:S(2)}) %collective-permute-start.2) | collective-permute-done | bytes 655392 | tf_op jit(solution)/shard_map/ppermute | solution.py:368
  47.7 9.6 %collective-permute-start.5 = (bf16[256,256]{1,0:T(8,128)(2,1)S(1)}, bf16[256,256]{1,0:T(8,128)(2,1)S(1)}, u32[]{:S(2)}, u32[]{:S(2)}) collective-permute-start(bf16[256,256]{1,0:T(8,128)(2,1)S(1)} %add_convert_fusion.7), channel_id=1, source_target_pairs={{0,2},{1,3},{2,0},{3,1},{4,6},{5,7},{6,4},{7,5},{8,10},{9,11},{10,... | collective-permute-start | bytes 393224 | tf_op jit(solution)/shard_map/ppermute | solution.py:368
  57.3 2.0 %add_convert_fusion = bf16[2,512,512]{2,1,0:T(8,128)(2,1)S(1)} fusion(f32[2,512,512]{2,1,0:T(8,128)} %get-tuple-element.18, bf16[2,512,512]{2,1,0:T(8,128)(2,1)S(1)} %collective-permute-done.3), kind=kLoop, calls=%fused_computation.2 | loop fusion | flops 1572864 | bytes 4194304 | tf_op jit(solution)/shard_map/convert_element_type | solution.py:408
  59.3 0.1 fusion.4
  59.4 1.4 %collective-permute-start.8 = (bf16[2,256,512]{2,1,0:T(8,128)(2,1)S(1)}, bf16[2,256,512]{2,1,0:T(8,128)(2,1)S(1)}, u32[]{:S(2)}, u32[]{:S(2)}) collective-permute-start(bf16[2,256,512]{2,1,0:T(8,128)(2,1)S(1)} %get-tuple-element.28), channel_id=1, source_target_pairs={{0,2},{1,3},{2,0},{3,1},{4,6},{5,7},{6,4},{7,5},{8,10},{9,11},{10,... | collective-permute-start | bytes 1572872 | tf_op jit(solution)/shard_map/ppermute | solution.py:368
  60.9 0.3 collective-permute-done.5
  61.2 0.1 collective-permute-start.6
  61.2 3.9 %collective-permute-start.4 = (bf16[2,256,512]{2,1,0:T(8,128)(2,1)S(1)}, bf16[2,256,512]{2,1,0:T(8,128)(2,1)S(1)}, u32[]{:S(2)}, u32[]{:S(2)}) collective-permute-start(bf16[2,256,512]{2,1,0:T(8,128)(2,1)S(1)} %get-tuple-element.29), channel_id=1, source_target_pairs={{0,4},{4,8},{8,12},{12,16},{16,20},{20,24},{24,28},{1,5},{5,9},{9,... | collective-permute-start | bytes 1572872 | tf_op jit(solution)/shard_map/ppermute | solution.py:374
  65.2 1.0 %collective-permute-done.6 = bf16[256,256]{1,0:T(8,128)(2,1)S(1)} collective-permute-done((bf16[256,256]{1,0:T(8,128)(2,1)S(1)}, bf16[256,256]{1,0:T(8,128)(2,1)S(1)}, u32[]{:S(2)}, u32[]{:S(2)}) %collective-permute-start.6) | collective-permute-done | bytes 131104 | tf_op jit(solution)/shard_map/ppermute | solution.py:368
  66.3 6.9 %collective-permute-done.8 = bf16[2,256,512]{2,1,0:T(8,128)(2,1)S(1)} collective-permute-done((bf16[2,256,512]{2,1,0:T(8,128)(2,1)S(1)}, bf16[2,256,512]{2,1,0:T(8,128)(2,1)S(1)}, u32[]{:S(2)}, u32[]{:S(2)}) %collective-permute-start.8) | collective-permute-done | bytes 524320 | tf_op jit(solution)/shard_map/ppermute | solution.py:368
  73.2 0.1 add_convert_fusion.2
  73.3 0.1 collective-permute-start.9
  73.4 2.4 %collective-permute-done.4 = bf16[2,256,512]{2,1,0:T(8,128)(2,1)S(1)} collective-permute-done((bf16[2,256,512]{2,1,0:T(8,128)(2,1)S(1)}, bf16[2,256,512]{2,1,0:T(8,128)(2,1)S(1)}, u32[]{:S(2)}, u32[]{:S(2)}) %collective-permute-start.4) | collective-permute-done | bytes 524320 | tf_op jit(solution)/shard_map/ppermute | solution.py:374
  75.8 5.6 %collective-permute-start.10 = (bf16[256,256]{1,0:T(8,128)(2,1)S(1)}, bf16[256,256]{1,0:T(8,128)(2,1)S(1)}, u32[]{:S(2)}, u32[]{:S(2)}) collective-permute-start(bf16[256,256]{1,0:T(8,128)(2,1)S(1)} %add_convert_fusion.5), channel_id=1, source_target_pairs={{0,8},{4,12},{8,0},{12,4},{16,24},{20,28},{24,16},{28,20},{1,9},{5... | collective-permute-start | bytes 393224 | tf_op jit(solution)/shard_map/ppermute | solution.py:368
  81.5 0.2 fusion.2
  81.7 1.6 %collective-permute-start.7 = (bf16[2,256,512]{2,1,0:T(8,128)(2,1)S(1)}, bf16[2,256,512]{2,1,0:T(8,128)(2,1)S(1)}, u32[]{:S(2)}, u32[]{:S(2)}) collective-permute-start(bf16[2,256,512]{2,1,0:T(8,128)(2,1)S(1)} %fusion.2), channel_id=1, source_target_pairs={{0,2},{1,3},{2,0},{3,1},{4,6},{5,7},{6,4},{7,5},{8,10},{9,11},{10,... | collective-permute-start | bytes 1572872 | tf_op jit(solution)/shard_map/ppermute | solution.py:368
  83.2 1.2 %collective-permute-done.10 = bf16[256,256]{1,0:T(8,128)(2,1)S(1)} collective-permute-done((bf16[256,256]{1,0:T(8,128)(2,1)S(1)}, bf16[256,256]{1,0:T(8,128)(2,1)S(1)}, u32[]{:S(2)}, u32[]{:S(2)}) %collective-permute-start.10) | collective-permute-done | bytes 131104 | tf_op jit(solution)/shard_map/ppermute | solution.py:368
  84.4 0.7 collective-permute-start.11
  85.1 5.3 %collective-permute-done.11 = bf16[256,256]{1,0:T(8,128)(2,1)S(1)} collective-permute-done((bf16[256,256]{1,0:T(8,128)(2,1)S(1)}, bf16[256,256]{1,0:T(8,128)(2,1)S(1)}, u32[]{:S(2)}, u32[]{:S(2)}) %collective-permute-start.11) | collective-permute-done | bytes 131104 | tf_op jit(solution)/shard_map/ppermute | solution.py:368
  90.4 0.1 collective-permute-start.12
  90.5 1.3 %collective-permute-done.12 = bf16[256,256]{1,0:T(8,128)(2,1)S(1)} collective-permute-done((bf16[256,256]{1,0:T(8,128)(2,1)S(1)}, bf16[256,256]{1,0:T(8,128)(2,1)S(1)}, u32[]{:S(2)}, u32[]{:S(2)}) %collective-permute-start.12) | collective-permute-done | bytes 131104 | tf_op jit(solution)/shard_map/ppermute | solution.py:368
  91.8 2.1 %collective-permute-done.7 = bf16[2,256,512]{2,1,0:T(8,128)(2,1)S(1)} collective-permute-done((bf16[2,256,512]{2,1,0:T(8,128)(2,1)S(1)}, bf16[2,256,512]{2,1,0:T(8,128)(2,1)S(1)}, u32[]{:S(2)}, u32[]{:S(2)}) %collective-permute-start.7) | collective-permute-done | bytes 524320 | tf_op jit(solution)/shard_map/ppermute | solution.py:368
  93.9 0.1 add_convert_fusion.1
  94.0 0.1 collective-permute-start.13
  94.1 0.8 fusion.3
  94.9 0.1 maximum_bitcast_fusion
  95.0 1.0 collective-permute-done.13
  96.0 0.1 maximum_bitcast_fusion.1
  96.1 0.4 fusion
  96.5 2.5 %copy.13 = f32[2,2,512,512]{3,2,1,0:T(8,128)} copy(f32[2,2,512,512]{3,2,0,1:T(8,128)S(1)} %fusion) | data formatting | bytes 8388608
  (33 shorter events, 0.2 us)
Async XLA Ops:
  1.7 16.8 %collective-permute-start = (bf16[2,1,256,512]{3,2,1,0:T(8,128)(2,1)S(1)}, bf16[2,1,256,512]{3,2,1,0:T(8,128)(2,1)S(1)}, u32[]{:S(2)}, u32[]{:S(2)}) collective-permute-start(bf16[2,1,256,512]{3,2,1,0:T(8,128)(2,1)S(1)} %constant_dynamic-slice_fusion), channel_id=1, source_target_pairs={{4,0},{8,4},{12,8},{16,12},{20,16},{24,20},{28,24},{5,1},{9,5},{13... | collective-permute-start | bytes 1572872 | tf_op jit(solution)/shard_map/ppermute | solution.py:374
  18.5 16.6 %collective-permute-start.1 = (bf16[2,1,256,512]{3,2,1,0:T(8,128)(2,1)S(1)}, bf16[2,1,256,512]{3,2,1,0:T(8,128)(2,1)S(1)}, u32[]{:S(2)}, u32[]{:S(2)}) collective-permute-start(bf16[2,1,256,512]{3,2,1,0:T(8,128)(2,1)S(1)} %collective-permute-done.rim_own), channel_id=1, source_target_pairs={{0,1},{1,0},{2,3},{3,2},{4,5},{5,4},{6,7},{7,6},{8,9},{9,8},{10,11... | collective-permute-start | bytes 1572872 | tf_op jit(solution)/shard_map/ppermute | solution.py:368
  20.0 1.6 %copy-start = (bf16[2,2,512,512]{3,2,1,0:T(8,128)(2,1)S(1)}, bf16[2,2,512,512]{3,2,1,0:T(8,128)(2,1)}, u32[]{:S(2)}) copy-start(bf16[2,2,512,512]{3,2,1,0:T(8,128)(2,1)} %spec.3) | copy-start | bytes 6291460
  21.6 1.2 %copy-start.2 = (bf16[8,256,256]{2,1,0:T(8,128)(2,1)S(1)}, bf16[8,256,256]{2,1,0:T(8,128)(2,1)}, u32[]{:S(2)}) copy-start(bf16[8,256,256]{2,1,0:T(8,128)(2,1)} %amp.3) | copy-start | bytes 3145732
  22.8 1.0 %copy-start.3 = (f32[2,256,256]{2,1,0:T(8,128)S(1)}, f32[2,256,256]{2,1,0:T(8,128)}, u32[]{:S(2)}) copy-start(f32[2,256,256]{2,1,0:T(8,128)} %probe.3) | copy-start | bytes 1572868
  23.8 1.0 %copy-start.5 = (bf16[512,512]{1,0:T(8,128)(2,1)S(1)}, bf16[512,512]{1,0:T(8,128)(2,1)}, u32[]{:S(2)}) copy-start(bf16[512,512]{1,0:T(8,128)(2,1)} %constant.36.clone.rf) | copy-start | bytes 1572868
  24.9 1.0 %copy-start.7 = (bf16[512,512]{1,0:T(8,128)(2,1)S(1)}, bf16[512,512]{1,0:T(8,128)(2,1)}, u32[]{:S(2)}) copy-start(bf16[512,512]{1,0:T(8,128)(2,1)} %constant.35.clone.lf) | copy-start | bytes 1572868
  25.9 1.0 %copy-start.9 = (bf16[512,512]{1,0:T(8,128)(2,1)S(1)}, bf16[512,512]{1,0:T(8,128)(2,1)}, u32[]{:S(2)}) copy-start(bf16[512,512]{1,0:T(8,128)(2,1)} %constant.34.clone.ra) | copy-start | bytes 1572868
  27.0 1.0 %copy-start.11 = (bf16[512,512]{1,0:T(8,128)(2,1)S(1)}, bf16[512,512]{1,0:T(8,128)(2,1)}, u32[]{:S(2)}) copy-start(bf16[512,512]{1,0:T(8,128)(2,1)} %constant.33.clone.la) | copy-start | bytes 1572868
  28.0 7.1 %copy-start.4 = (f32[2,256,256]{2,1,0:T(8,128)S(1)}, f32[2,256,256]{2,1,0:T(8,128)}, u32[]{:S(2)}) copy-start(f32[2,256,256]{2,1,0:T(8,128)} %probe.3) | copy-start | bytes 1572868
  28.0 7.1 %copy-start.6 = (bf16[512,512]{1,0:T(8,128)(2,1)S(1)}, bf16[512,512]{1,0:T(8,128)(2,1)}, u32[]{:S(2)}) copy-start(bf16[512,512]{1,0:T(8,128)(2,1)} %constant.36.clone.rf) | copy-start | bytes 1572868
  28.0 7.1 %copy-start.8 = (bf16[512,512]{1,0:T(8,128)(2,1)S(1)}, bf16[512,512]{1,0:T(8,128)(2,1)}, u32[]{:S(2)}) copy-start(bf16[512,512]{1,0:T(8,128)(2,1)} %constant.35.clone.lf) | copy-start | bytes 1572868
  28.0 7.1 %copy-start.10 = (bf16[512,512]{1,0:T(8,128)(2,1)S(1)}, bf16[512,512]{1,0:T(8,128)(2,1)}, u32[]{:S(2)}) copy-start(bf16[512,512]{1,0:T(8,128)(2,1)} %constant.34.clone.ra) | copy-start | bytes 1572868
  28.0 7.1 %copy-start.12 = (bf16[512,512]{1,0:T(8,128)(2,1)S(1)}, bf16[512,512]{1,0:T(8,128)(2,1)}, u32[]{:S(2)}) copy-start(bf16[512,512]{1,0:T(8,128)(2,1)} %constant.33.clone.la) | copy-start | bytes 1572868
  33.1 2.0 %copy-start.1 = (f32[2,2,4,512,128]{4,3,2,1,0:T(8,128)}, f32[2,2,4,512,128]{4,3,2,1,0:T(8,128)S(1)}, u32[]{:S(2)}) copy-start(f32[2,2,4,512,128]{4,3,2,1,0:T(8,128)S(1)} %get-tuple-element.14.acc_in) | copy-start | bytes 12582916
  45.4 2.3 %collective-permute-start.2 = (bf16[640,512]{1,0:T(8,128)(2,1)S(1)}, bf16[640,512]{1,0:T(8,128)(2,1)S(1)}, u32[]{:S(2)}, u32[]{:S(2)}) collective-permute-start(bf16[640,512]{1,0:T(8,128)(2,1)S(1)} %get-tuple-element.17), channel_id=1, source_target_pairs={{0,1},{1,0},{2,3},{3,2},{4,5},{5,4},{6,7},{7,6},{8,9},{9,8},{10,11... | collective-permute-start | bytes 1966088 | tf_op jit(solution)/shard_map/ppermute | solution.py:368
  45.9 11.4 %collective-permute-start.3 = (bf16[2,512,512]{2,1,0:T(8,128)(2,1)S(1)}, bf16[2,512,512]{2,1,0:T(8,128)(2,1)S(1)}, u32[]{:S(2)}, u32[]{:S(2)}) collective-permute-start(bf16[2,512,512]{2,1,0:T(8,128)(2,1)S(1)} %get-tuple-element.19), channel_id=1, source_target_pairs={{0,1},{1,0},{2,3},{3,2},{4,5},{5,4},{6,7},{7,6},{8,9},{9,8},{10,11... | collective-permute-start | bytes 3145736 | tf_op jit(solution)/shard_map/ppermute | solution.py:368
  47.7 17.5 %copy-start.13 = (bf16[640,512]{1,0:T(8,128)(2,1)}, bf16[640,512]{1,0:T(8,128)(2,1)S(1)}, u32[]{:S(2)}) copy-start(bf16[640,512]{1,0:T(8,128)(2,1)S(1)} %collective-permute-done.2) | copy-start | bytes 1966084
  47.7 13.4 %collective-permute-start.5 = (bf16[256,256]{1,0:T(8,128)(2,1)S(1)}, bf16[256,256]{1,0:T(8,128)(2,1)S(1)}, u32[]{:S(2)}, u32[]{:S(2)}) collective-permute-start(bf16[256,256]{1,0:T(8,128)(2,1)S(1)} %add_convert_fusion.7), channel_id=1, source_target_pairs={{0,2},{1,3},{2,0},{3,1},{4,6},{5,7},{6,4},{7,5},{8,10},{9,11},{10,... | collective-permute-start | bytes 393224 | tf_op jit(solution)/shard_map/ppermute | solution.py:368
  59.4 22.0 %copy-start.14 = (f32[2,256,512]{2,1,0:T(8,128)S(1)}, f32[2,256,512]{2,1,0:T(8,128)}, u32[]{:S(2)}) copy-start(f32[2,256,512]{2,1,0:T(8,128)} %get-tuple-element.16) | copy-start | bytes 3145732
  59.4 13.8 %collective-permute-start.8 = (bf16[2,256,512]{2,1,0:T(8,128)(2,1)S(1)}, bf16[2,256,512]{2,1,0:T(8,128)(2,1)S(1)}, u32[]{:S(2)}, u32[]{:S(2)}) collective-permute-start(bf16[2,256,512]{2,1,0:T(8,128)(2,1)S(1)} %get-tuple-element.28), channel_id=1, source_target_pairs={{0,2},{1,3},{2,0},{3,1},{4,6},{5,7},{6,4},{7,5},{8,10},{9,11},{10,... | collective-permute-start | bytes 1572872 | tf_op jit(solution)/shard_map/ppermute | solution.py:368
  61.2 5.1 %collective-permute-start.6 = (bf16[256,256]{1,0:T(8,128)(2,1)S(1)}, bf16[256,256]{1,0:T(8,128)(2,1)S(1)}, u32[]{:S(2)}, u32[]{:S(2)}) collective-permute-start(bf16[256,256]{1,0:T(8,128)(2,1)S(1)} %add_convert_fusion.6), channel_id=1, source_target_pairs={{0,4},{4,0},{8,12},{12,8},{16,20},{20,16},{24,28},{28,24},{1,5},{5... | collective-permute-start | bytes 393224 | tf_op jit(solution)/shard_map/ppermute | solution.py:368
  61.2 14.6 %collective-permute-start.4 = (bf16[2,256,512]{2,1,0:T(8,128)(2,1)S(1)}, bf16[2,256,512]{2,1,0:T(8,128)(2,1)S(1)}, u32[]{:S(2)}, u32[]{:S(2)}) collective-permute-start(bf16[2,256,512]{2,1,0:T(8,128)(2,1)S(1)} %get-tuple-element.29), channel_id=1, source_target_pairs={{0,4},{4,8},{8,12},{12,16},{16,20},{20,24},{24,28},{1,5},{5,9},{9,... | collective-permute-start | bytes 1572872 | tf_op jit(solution)/shard_map/ppermute | solution.py:374
  65.2 16.3 %slice-start = ((bf16[640,512]{1,0:T(8,128)(2,1)}), bf16[512,512]{1,0:T(8,128)(2,1)S(1)}, s32[]{:S(2)}) async-start(bf16[640,512]{1,0:T(8,128)(2,1)} %copy-done.13), calls=%async_computation | async-start | bytes 1048576 | tf_op jit(solution)/shard_map/slice | solution.py:412
  73.3 18.5 %collective-permute-start.9 = (bf16[2,256,512]{2,1,0:T(8,128)(2,1)S(1)}, bf16[2,256,512]{2,1,0:T(8,128)(2,1)S(1)}, u32[]{:S(2)}, u32[]{:S(2)}) collective-permute-start(bf16[2,256,512]{2,1,0:T(8,128)(2,1)S(1)} %add_convert_fusion.2), channel_id=1, source_target_pairs={{0,1},{1,0},{2,3},{3,2},{4,5},{5,4},{6,7},{7,6},{8,9},{9,8},{10,11... | collective-permute-start | bytes 1572872 | tf_op jit(solution)/shard_map/ppermute | solution.py:368
  75.8 8.6 %collective-permute-start.10 = (bf16[256,256]{1,0:T(8,128)(2,1)S(1)}, bf16[256,256]{1,0:T(8,128)(2,1)S(1)}, u32[]{:S(2)}, u32[]{:S(2)}) collective-permute-start(bf16[256,256]{1,0:T(8,128)(2,1)S(1)} %add_convert_fusion.5), channel_id=1, source_target_pairs={{0,8},{4,12},{8,0},{12,4},{16,24},{20,28},{24,16},{28,20},{1,9},{5... | collective-permute-start | bytes 393224 | tf_op jit(solution)/shard_map/ppermute | solution.py:368
  81.7 12.2 %collective-permute-start.7 = (bf16[2,256,512]{2,1,0:T(8,128)(2,1)S(1)}, bf16[2,256,512]{2,1,0:T(8,128)(2,1)S(1)}, u32[]{:S(2)}, u32[]{:S(2)}) collective-permute-start(bf16[2,256,512]{2,1,0:T(8,128)(2,1)S(1)} %fusion.2), channel_id=1, source_target_pairs={{0,2},{1,3},{2,0},{3,1},{4,6},{5,7},{6,4},{7,5},{8,10},{9,11},{10,... | collective-permute-start | bytes 1572872 | tf_op jit(solution)/shard_map/ppermute | solution.py:368
  84.4 5.9 %collective-permute-start.11 = (bf16[256,256]{1,0:T(8,128)(2,1)S(1)}, bf16[256,256]{1,0:T(8,128)(2,1)S(1)}, u32[]{:S(2)}, u32[]{:S(2)}) collective-permute-start(bf16[256,256]{1,0:T(8,128)(2,1)S(1)} %add_convert_fusion.4), channel_id=1, source_target_pairs={{0,16},{4,20},{8,24},{12,28},{16,0},{20,4},{24,8},{28,12},{1,17},{... | collective-permute-start | bytes 393224 | tf_op jit(solution)/shard_map/ppermute | solution.py:368
  90.4 1.4 %collective-permute-start.12 = (bf16[256,256]{1,0:T(8,128)(2,1)S(1)}, bf16[256,256]{1,0:T(8,128)(2,1)S(1)}, u32[]{:S(2)}, u32[]{:S(2)}) collective-permute-start(bf16[256,256]{1,0:T(8,128)(2,1)S(1)} %add_convert_fusion.3), channel_id=1, source_target_pairs={{0,1},{1,0},{2,3},{3,2},{4,5},{5,4},{6,7},{7,6},{8,9},{9,8},{10,11... | collective-permute-start | bytes 393224 | tf_op jit(solution)/shard_map/ppermute | solution.py:368
  94.0 2.0 %collective-permute-start.13 = (bf16[2,256,512]{2,1,0:T(8,128)(2,1)S(1)}, bf16[2,256,512]{2,1,0:T(8,128)(2,1)S(1)}, u32[]{:S(2)}, u32[]{:S(2)}) collective-permute-start(bf16[2,256,512]{2,1,0:T(8,128)(2,1)S(1)} %add_convert_fusion.1), channel_id=1, source_target_pairs={{0,1},{1,0},{2,3},{3,2},{4,5},{5,4},{6,7},{7,6},{8,9},{9,8},{10,11... | collective-permute-start | bytes 1572872 | tf_op jit(solution)/shard_map/ppermute | solution.py:368

commit v3 on v2

--- a/solution.py
+++ b/solution.py
@@ -219,61 +219,143 @@
         ].astype(jnp.float32)
 
 
+def fetch(copies, sems):
+    started = {}
+    for k, (group, source, target) in enumerate(copies):
+        copy = pltpu.make_async_copy(source, target, sems.at[k])
+        copy.start()
+        started.setdefault(group, []).append(copy)
+
+    def wait(group):
+        for copy in started[group]:
+            copy.wait()
+
+    return wait
+
+
 def early_kernel(
-    meta, anchor, probe, spec, amp, la, ra, lf, rf, acc, probe_acc, order, wide, *work
-):
-    slices, tile_rows = spec.shape[1:3]
-    for part in range(2):
-        for s in range(slices):
-            widen(wide, spec, 0, part, s, s)
-            for t in range(wide.shape[2]):
-                acc[part, s, t] = jnp.zeros(acc.shape[3:], jnp.float32)
-    probe_acc[...] = jnp.zeros(probe_acc.shape, jnp.float32)
-    total = listed(order, anchor, meta[0], meta[1], probe.shape[1], tile_rows, False)
-    refs = (anchor, probe, amp, (la, ra, lf, rf), wide, acc, probe_acc)
-    run_pairs(order, total, meta[1], refs, (work[:5], work[5:]))
-
-
-def late_kernel(
     meta,
     anchor,
+    probe_hbm,
+    spec_hbm,
+    amp_hbm,
+    la_hbm,
+    ra_hbm,
+    lf_hbm,
+    rf_hbm,
+    acc,
+    probe_acc,
+    order,
+    sems,
     probe,
     spec,
-    rim_own,
-    rim_other,
-    acc_in,
-    probe_in,
     amp,
     la,
     ra,
     lf,
     rf,
+    wide,
+    *work,
+):
+    wait = fetch(
+        [
+            ("spec", spec_hbm, spec),
+            ("rest", probe_hbm, probe),
+            ("rest", la_hbm, la),
+            ("rest", ra_hbm, ra),
+            ("rest", lf_hbm, lf),
+            ("rest", rf_hbm, rf),
+            ("rest", amp_hbm, amp),
+        ],
+        sems,
+    )
+    slices, tile_rows = spec.shape[1:3]
+    for part in range(2):
+        for s in range(slices):
+            for t in range(wide.shape[2]):
+                acc[part, s, t] = jnp.zeros(acc.shape[3:], jnp.float32)
+    probe_acc[...] = jnp.zeros(probe_acc.shape, jnp.float32)
+    total = listed(order, anchor, meta[0], meta[1], probe.shape[1], tile_rows, False)
+    wait("spec")
+    for part in range(2):
+        for s in range(slices):
+            widen(wide, spec, 0, part, s, s)
+    wait("rest")
+    refs = (anchor, probe, amp, (la, ra, lf, rf), wide, acc, probe_acc)
+    run_pairs(order, total, meta[1], refs, (work[:5], work[5:]))
+
+
+def late_kernel(
+    meta,
+    anchor,
+    probe_hbm,
+    spec_hbm,
+    rim_own_any,
+    rim_other_any,
+    acc_any,
+    probe_acc_any,
+    amp_hbm,
+    la_hbm,
+    ra_hbm,
+    lf_hbm,
+    rf_hbm,
     send_low,
     send_top,
     keep_low,
     keep_top,
     keep_probe,
     order,
+    sems,
+    probe,
+    spec,
+    amp,
+    la,
+    ra,
+    lf,
+    rf,
     wide,
+    rim_own,
+    rim_other,
     acc,
     probe_acc,
     *work,
 ):
     slices, tile_rows, width = spec.shape[1:]
     edge = probe.shape[1]
+    wait = fetch(
+        [
+            ("spec", spec_hbm, spec),
+            ("rim", rim_own_any, rim_own),
+            ("rim", rim_other_any, rim_other),
+            ("acc", acc_any, acc.at[:, :, :, pl.ds(0, tile_rows), :]),
+            ("acc", probe_acc_any, probe_acc),
+            ("rest", probe_hbm, probe),
+            ("rest", la_hbm, la),
+            ("rest", ra_hbm, ra),
+            ("rest", lf_hbm, lf),
+            ("rest", rf_hbm, rf),
+            ("rest", amp_hbm, amp),
+        ],
+        sems,
+    )
     half = meta[2]
     other = 1 - half
     col_tiles = width // LANES
     for part in range(2):
         for s in range(slices):
+            for t in range(col_tiles):
+                acc[part, s, t, pl.ds(tile_rows, edge), :] = jnp.zeros((edge, LANES), jnp.float32)
+    total = listed(order, anchor, meta[0], meta[1], edge, tile_rows, True)
+    wait("spec")
+    for part in range(2):
+        for s in range(slices):
             widen(wide, spec, 0, part, s, s)
-            for t in range(col_tiles):
-                acc[part, s, t, pl.ds(0, tile_rows), :] = acc_in[part, s, t]
-                acc[part, s, t, pl.ds(tile_rows, edge), :] = jnp.zeros((edge, LANES), jnp.float32)
+    wait("rim")
+    for part in range(2):
         widen(wide, rim_own, tile_rows, part, 0, half)
         widen(wide, rim_other, tile_rows, part, 0, other)
-    probe_acc[...] = probe_in[...]
-    total = listed(order, anchor, meta[0], meta[1], edge, tile_rows, True)
+    wait("acc")
+    wait("rest")
     refs = (anchor, probe, amp, (la, ra, lf, rf), wide, acc, probe_acc)
     run_pairs(order, total, meta[1], refs, (work[:5], work[5:]))
 
@@ -301,35 +383,44 @@
 
 VMEM = pl.BlockSpec(memory_space=pltpu.VMEM)
 SMEM = pl.BlockSpec(memory_space=pltpu.SMEM)
-
-
-def scratch(slots, slices, col_tiles, rows, edge):
-    one = [
-        pltpu.VMEM((2, edge, edge), jnp.float32),
-        pltpu.VMEM((2, edge, edge), jnp.float32),
-        pltpu.VMEM((2, edge, edge), jnp.float32),
-        pltpu.VMEM((2 * edge, edge), jnp.bfloat16),
-        pltpu.VMEM((edge, 2 * edge), jnp.bfloat16),
+HBM = pl.BlockSpec(memory_space=pltpu.HBM)
+ANY = pl.BlockSpec(memory_space=pl.ANY)
+
+
+def scratch(slots, slices, width, tile_rows, rows, edge, copies):
+    planes = pltpu.VMEM((2, edge, edge), jnp.float32)
+    table = pltpu.VMEM((2 * edge, 2 * edge), jnp.bfloat16)
+    stack = pltpu.VMEM((2 * edge, edge), jnp.bfloat16)
+    joined = pltpu.VMEM((edge, 2 * edge), jnp.bfloat16)
+    lead = [
+        pltpu.SMEM((slots + 1,), jnp.int32),
+        pltpu.SemaphoreType.DMA((copies,)),
+        planes,
+        pltpu.VMEM((2, slices, tile_rows, width), jnp.bfloat16),
+        pltpu.VMEM((slots, edge, edge), jnp.bfloat16),
+        table,
+        table,
+        table,
+        table,
+        pltpu.VMEM((2, slices, width // LANES, rows, LANES), jnp.float32),
     ]
-    order = pltpu.SMEM((slots + 1,), jnp.int32)
-    return [order, pltpu.VMEM((2, slices, col_tiles, rows, LANES), jnp.float32)], one + one
+    return lead, [planes, planes, planes, stack, joined] * 2
 
 
 def run_early(meta, anchor, probe, spec, amp, tables):
     edge = probe.shape[1]
     _, slices, tile_rows, width = spec.shape
-    col_tiles = width // LANES
-    lead, work = scratch(anchor.shape[0], slices, col_tiles, tile_rows, edge)
+    lead, work = scratch(anchor.shape[0], slices, width, tile_rows, tile_rows, edge, 7)
     return pl.pallas_call(
         early_kernel,
         out_shape=(
-            jax.ShapeDtypeStruct((2, slices, col_tiles, tile_rows, LANES), jnp.float32),
+            jax.ShapeDtypeStruct((2, slices, width // LANES, tile_rows, LANES), jnp.float32),
             jax.ShapeDtypeStruct((2, edge, edge), jnp.float32),
         ),
-        in_specs=[SMEM, SMEM] + [VMEM] * 7,
+        in_specs=[SMEM, SMEM] + [HBM] * 7,
         out_specs=(VMEM, VMEM),
         scratch_shapes=lead + work,
-        compiler_params=pltpu.CompilerParams(vmem_limit_bytes=40 * 1024 * 1024),
+        compiler_params=pltpu.CompilerParams(vmem_limit_bytes=32 * 1024 * 1024),
         name="early_slots",
     )(meta, anchor, probe, spec, amp, *tables)
 
@@ -337,10 +428,10 @@
 def run_late(meta, anchor, probe, spec, rim_own, rim_other, acc, probe_acc, amp, tables):
     edge = probe.shape[1]
     _, slices, tile_rows, width = spec.shape
-    col_tiles = width // LANES
     total = tile_rows + edge
     side = width // edge
-    lead, work = scratch(anchor.shape[0], slices, col_tiles, total, edge)
+    lead, work = scratch(anchor.shape[0], slices, width, tile_rows, total, edge, 11)
+    rim = pltpu.VMEM((2, 1, edge, width), jnp.bfloat16)
     return pl.pallas_call(
         late_kernel,
         out_shape=(
@@ -350,17 +441,55 @@
             jax.ShapeDtypeStruct((2, edge, width), jnp.float32),
             jax.ShapeDtypeStruct((edge, edge), jnp.float32),
         ),
-        in_specs=[SMEM, SMEM] + [VMEM] * 11,
+        in_specs=[SMEM, SMEM, HBM, HBM] + [ANY] * 4 + [HBM] * 5,
         out_specs=(VMEM,) * 5,
         scratch_shapes=lead
         + [
-            pltpu.VMEM((2, slices, col_tiles, total, LANES), jnp.float32),
+            rim,
+            rim,
+            pltpu.VMEM((2, slices, width // LANES, total, LANES), jnp.float32),
             pltpu.VMEM((2, edge, edge), jnp.float32),
         ]
         + work,
-        compiler_params=pltpu.CompilerParams(vmem_limit_bytes=48 * 1024 * 1024),
+        compiler_params=pltpu.CompilerParams(vmem_limit_bytes=36 * 1024 * 1024),
         name="late_slots",
     )(meta, anchor, probe, spec, rim_own, rim_other, acc, probe_acc, amp, *tables)
+
+
+def write_rows(meta, own, theirs, start, shape, base=None):
+    slices, rows, width = shape[1], own.shape[1], own.shape[2]
+
+    def kernel(meta, own, theirs, *rest):
+        out, wide, sems = rest[-3:]
+        half = meta[2]
+        wide[half] = own[...].astype(jnp.float32)
+        wide[1 - half] = theirs[...].astype(jnp.float32)
+        copies = [
+            pltpu.make_async_copy(
+                wide.at[s, part], out.at[part, s, pl.ds(start, rows), :], sems.at[2 * s + part]
+            )
+            for s in range(slices)
+            for part in range(2)
+        ]
+        for copy in copies:
+            copy.start()
+        for copy in copies:
+            copy.wait()
+
+    extra = [] if base is None else [base]
+    return pl.pallas_call(
+        kernel,
+        out_shape=jax.ShapeDtypeStruct(shape, jnp.float32),
+        in_specs=[SMEM, VMEM, VMEM] + [HBM] * len(extra),
+        out_specs=HBM,
+        input_output_aliases={} if base is None else {3: 0},
+        scratch_shapes=[
+            pltpu.VMEM((slices, 2, rows, width), jnp.float32),
+            pltpu.SemaphoreType.DMA((2 * slices,)),
+        ],
+        compiler_params=pltpu.CompilerParams(vmem_limit_bytes=16 * 1024 * 1024),
+        name="write_rows",
+    )(meta, own, theirs, *extra)
 
 
 def traded(value, axis, distance):
@@ -389,8 +518,9 @@
     rim_own = passed_along(
         lax.dynamic_slice(specimen, (0, half, 0, 0), (2, 1, edge, width)), "tile", -1
     )
+    acc, probe_acc = run_early(meta, scan_anchor, probe_field, specimen, amplitude, tables)
+    rim_own, probe_acc = lax.optimization_barrier((rim_own, probe_acc))
     rim_other = traded(rim_own, "pos", 1)
-    acc, probe_acc = run_early(meta, scan_anchor, probe_field, specimen, amplitude, tables)
     sent_low, sent_top, kept_low, kept_top, kept_probe = run_late(
         meta,
         scan_anchor,
@@ -406,9 +536,10 @@
     got_low = traded(sent_low, "pos", 1)
     got_top = traded(sent_top, "pos", 1)
     low = (kept_low + got_low.astype(jnp.float32)).astype(jnp.bfloat16)
-    below = passed_along(low[:, tile_rows - edge :], "tile", 1)
+    got_top, low = lax.optimization_barrier((got_top, low))
     lower = low[:, : tile_rows - edge]
     lower_got = traded(lower, "pos", 2)
+    below = passed_along(low[:, tile_rows - edge :], "tile", 1)
     top = kept_top + got_top[: 2 * edge].reshape(2, edge, width).astype(jnp.float32)
     got_probe = jnp.concatenate(
         [got_top[2 * edge :, p * edge : (p + 1) * edge] for p in range(side)], 0
@@ -418,6 +549,7 @@
     probe_part = narrow_sum(probe_part, traded(probe_part, "tile", 1))
     below, probe_part = lax.optimization_barrier((below, probe_part))
     upper = (top + below.astype(jnp.float32)).astype(jnp.bfloat16)
+    lower_got, upper = lax.optimization_barrier((lower_got, upper))
     upper_got = traded(upper, "pos", 2)
     distance = 2
     while distance < lax.axis_size("tile"):
@@ -425,20 +557,17 @@
         distance *= 2
     lower = narrow_sum(lower, lower_got)
     lower_theirs = traded(lower, "pos", 1)
+    tile_grad = write_rows(meta, lower, lower_theirs, edge, specimen.shape)
     probe_theirs = traded(probe_part, "pos", 1)
-    upper_got, lower_theirs, probe_theirs = lax.optimization_barrier(
-        (upper_got, lower_theirs, probe_theirs)
-    )
-    upper = narrow_sum(upper, upper_got)
-    upper_theirs = traded(upper, "pos", 1)
-    mine = jnp.concatenate([upper, lower], 1)
-    theirs = jnp.concatenate([upper_theirs, lower_theirs], 1)
-    tile_grad = jnp.where(
-        half == 0, jnp.stack([mine, theirs], 1), jnp.stack([theirs, mine], 1)
-    ).astype(jnp.float32)
     probe_total = jnp.where(
         half == 0, jnp.stack([probe_part, probe_theirs]), jnp.stack([probe_theirs, probe_part])
     ).astype(jnp.float32)
+    upper_got, tile_grad, probe_total = lax.optimization_barrier(
+        (upper_got, tile_grad, probe_total)
+    )
+    upper = narrow_sum(upper, upper_got)
+    upper_theirs = traded(upper, "pos", 1)
+    tile_grad = write_rows(meta, upper, upper_theirs, 0, specimen.shape, tile_grad)
     return (tile_grad, probe_total)
 
 

time: 98.5 us -> 86.8 us (0.88); the launches traced: 98.9 us -> 88.3 us
  waiting for transfers between devices: 38.6 us -> 30.3 us
  local copies, waits for them, and re-layouts: 14.4 us -> 9.99 us
  starting transfers between devices: 25 us -> 28.5 us
  other arithmetic: 4.08 us -> 1.92 us
    ppermute x2, waiting for transfers between devices: 17.9 us -> 0.48 us  [passed_along(): lax.ppermute(value, axis, [(source, source + steps) for source in range(i...]
    ppermute x12, waiting for transfers between devices: 20.7 us -> 29.8 us  [traded(): return lax.ppermute(value, axis, [(i, i ^ distance) for i in range(count)])]
    ppermute x12, starting transfers between devices: 19.7 us -> 25.9 us  [traded(): return lax.ppermute(value, axis, [(i, i ^ distance) for i in range(count)])]
    unnamed x32 -> x23, local copies, waits for them, and re-layouts: 13.3 us -> 8.79 us
    pallas_call x0 -> x2, Pallas kernels: none -> 4.04 us  [write_rows(): pl.pallas_call(kernel, out_shape=jax.ShapeDtypeStruct(shape, jnp.float32)...]
    pallas_call x1, Pallas kernels: 10.2 us -> 6.62 us  [run_late(): pl.pallas_call(late_kernel, out_shape=(jax.ShapeDtypeStruct((2, tile_rows...]
    ppermute x2, starting transfers between devices: 5.23 us -> 2.61 us  [passed_along(): lax.ppermute(value, axis, [(source, source + steps) for source in range(i...]
    convert_element_type x1, other arithmetic: 2.01 us -> 0.36 us  [body(): low = (kept_low + got_low.astype(jnp.float32)).astype(jnp.bfloat16)]
  transfers between devices with their start and end apart: 14 -> 14, of which waited for: 11 -> 11; matrix products, arithmetic and copies ran while one was open for 4% -> 3% of each run, Pallas kernels for 5% -> 8%
where the time goes in v3:
time: 86.8 us; the launch traced here: 88.3 us
  waiting for transfers between devices  30.3 us (35%)
  starting transfers between devices  28.5 us (33%)
  Pallas kernels  16.1 us (19%)
  local copies, waits for them, and re-layouts  9.99 us (12%)
  other arithmetic  1.92 us (2%)
  between operations  1.46 us (2%)
    ppermute x12, waiting for transfers between devices, traded(): return lax.ppermute(value, axis, [(i, i ^ distance) for i in range(count)])  29.8 us
    ppermute x12, starting transfers between devices, traded(): return lax.ppermute(value, axis, [(i, i ^ distance) for i in range(count)])  25.9 us
    unnamed x23, local copies, waits for them, and re-layouts  8.79 us
    pallas_call x1, Pallas kernels, run_late(): pl.pallas_call(late_kernel, out_shape=(jax.ShapeDtypeStruct((2, tile_rows...  6.62 us
    pallas_call x1, Pallas kernels, run_early(): pl.pallas_call(early_kernel, out_shape=(jax.ShapeDtypeStruct((2, slices,...  5.45 us
    pallas_call x2, Pallas kernels, write_rows(): pl.pallas_call(kernel, out_shape=jax.ShapeDtypeStruct(shape, jnp.float32)...  4.04 us
    ppermute x2, starting transfers between devices, passed_along(): lax.ppermute(value, axis, [(source, source + steps) for source in range(i...  2.61 us
  transfers between devices with their start and end apart: 14, of which 11 were waited for; matrix products, arithmetic and copies ran while one was open for 3% of the time, Pallas kernels for 8%

profile of v3, /device:TPU:0, one launch (start us, length us, event | category | flops | bytes accessed | tf_op | source)
XLA Modules:
  0.0 88.3 jit_solution(9707108792286359184)
XLA Ops:
  0.6 1.1 %constant_dynamic-slice_fusion = bf16[2,1,256,512]{3,2,1,0:T(8,128)(2,1)S(1)} fusion(bf16[2,2,512,512]{3,2,1,0:T(8,128)(2,1)} %spec_hbm.3, s32[]{:T(128)S(6)} %select_n.19), kind=kLoop, calls=%fused_computation.14 | loop fusion | bytes 1048580 | tf_op jit(solution)/shard_map/dynamic_slice | solution.py:519
  1.7 1.3 %collective-permute-start = (bf16[2,1,256,512]{3,2,1,0:T(8,128)(2,1)S(1)}, bf16[2,1,256,512]{3,2,1,0:T(8,128)(2,1)S(1)}, u32[]{:S(2)}, u32[]{:S(2)}) collective-permute-start(bf16[2,1,256,512]{3,2,1,0:T(8,128)(2,1)S(1)} %constant_dynamic-slice_fusion), channel_id=1, source_target_pairs={{4,0},{8,4},{12,8},{16,12},{20,16},{24,20},{28,24},{5,1},{9,5},{13... | collective-permute-start | bytes 1572872 | tf_op jit(solution)/shard_map/ppermute | solution.py:503
  3.7 0.8 copy.13.anchor
  4.4 0.1 pad_add_fusion.meta
  4.5 1.6 %copy-done = bf16[2,2,512,512]{3,2,1,0:T(8,128)(2,1)S(1)} copy-done((bf16[2,2,512,512]{3,2,1,0:T(8,128)(2,1)S(1)}, bf16[2,2,512,512]{3,2,1,0:T(8,128)(2,1)}, u32[]{:S(2)}) %copy-start) | copy-done | bytes 2097176
  6.1 1.2 %copy-done.2 = bf16[8,256,256]{2,1,0:T(8,128)(2,1)S(1)} copy-done((bf16[8,256,256]{2,1,0:T(8,128)(2,1)S(1)}, bf16[8,256,256]{2,1,0:T(8,128)(2,1)}, u32[]{:S(2)}) %copy-start.2) | copy-done | bytes 1048600
  7.3 1.0 %copy-done.4 = f32[2,256,256]{2,1,0:T(8,128)S(1)} copy-done((f32[2,256,256]{2,1,0:T(8,128)S(1)}, f32[2,256,256]{2,1,0:T(8,128)}, u32[]{:S(2)}) %copy-start.4) | copy-done | bytes 524312
  8.4 1.0 %copy-done.6 = bf16[512,512]{1,0:T(8,128)(2,1)S(1)} copy-done((bf16[512,512]{1,0:T(8,128)(2,1)S(1)}, bf16[512,512]{1,0:T(8,128)(2,1)}, u32[]{:S(2)}) %copy-start.6) | copy-done | bytes 524312
  9.4 1.0 %copy-done.7 = bf16[512,512]{1,0:T(8,128)(2,1)S(1)} copy-done((bf16[512,512]{1,0:T(8,128)(2,1)S(1)}, bf16[512,512]{1,0:T(8,128)(2,1)}, u32[]{:S(2)}) %copy-start.7) | copy-done | bytes 524312
  10.5 1.0 %copy-done.8 = bf16[512,512]{1,0:T(8,128)(2,1)S(1)} copy-done((bf16[512,512]{1,0:T(8,128)(2,1)S(1)}, bf16[512,512]{1,0:T(8,128)(2,1)}, u32[]{:S(2)}) %copy-start.8) | copy-done | bytes 524312
  11.5 1.0 %copy-done.9 = bf16[512,512]{1,0:T(8,128)(2,1)S(1)} copy-done((bf16[512,512]{1,0:T(8,128)(2,1)S(1)}, bf16[512,512]{1,0:T(8,128)(2,1)}, u32[]{:S(2)}) %copy-start.9) | copy-done | bytes 524312
  12.6 5.4 %early_slots.1 = (f32[2,2,4,512,128]{4,3,2,1,0:T(8,128)S(1)}, f32[2,256,256]{2,1,0:T(8,128)S(1)}) custom-call(s32[3]{0:T(128)S(1)} %pad_add_fusion.meta, s32[8,2]{1,0:T(8,128)S(1)} %copy.13.anchor, f32[2,256,256]{2,1,0:T(8,128)S(1)} %copy-done.4, bf16[2,2,512,512]{3,2,1,0:T(8,128)(2,1)S(1)} %copy-done, bf16[8,256,256]{2,1,0:T(8,128)(2,1)S(1)} %copy-done.2, ...), custom_call_target="tpu_custom_call" | custom-call | tf_op jit(solution)/shard_map/early_slots/pallas_call | solution.py:414
  18.0 0.5 collective-permute-done.rim_own_any
  18.5 0.0 collective-permute-start.1
  18.5 1.9 %collective-permute-done.1.rim_other_any = bf16[2,1,256,512]{3,2,1,0:T(8,128)(2,1)S(1)} collective-permute-done((bf16[2,1,256,512]{3,2,1,0:T(8,128)(2,1)S(1)}, bf16[2,1,256,512]{3,2,1,0:T(8,128)(2,1)S(1)}, u32[]{:S(2)}, u32[]{:S(2)}) %collective-permute-start.1) | collective-permute-done | bytes 524320 | tf_op jit(solution)/shard_map/ppermute | solution.py:497
  20.4 6.6 %late_slots.1 = (bf16[2,512,512]{2,1,0:T(8,128)(2,1)S(1)}, bf16[640,512]{1,0:T(8,128)(2,1)S(1)}, f32[2,512,512]{2,1,0:T(8,128)S(1)}, f32[2,256,512]{2,1,0:T(8,128)S(1)}, f32[256,256]{1,0:T(8,128)S(1)}) custom-call(s32[3]{0:T(128)S(1)} %pad_add_fusion.meta, s32[8,2]{1,0:T(8,128)S(1)} %copy.13.anchor, f32[2,256,256]{2,1,0:T(8,128)S(1)} %copy-done.5, ...), custom_call_target="tpu_custom_call" | custom-call | tf_op jit(solution)/shard_map/late_slots/pallas_call | solution.py:435
  27.1 3.9 %collective-permute-start.3 = (bf16[2,512,512]{2,1,0:T(8,128)(2,1)S(1)}, bf16[2,512,512]{2,1,0:T(8,128)(2,1)S(1)}, u32[]{:S(2)}, u32[]{:S(2)}) collective-permute-start(bf16[2,512,512]{2,1,0:T(8,128)(2,1)S(1)} %get-tuple-element.26), channel_id=1, source_target_pairs={{0,1},{1,0},{2,3},{3,2},{4,5},{5,4},{6,7},{7,6},{8,9},{9,8},{10,11... | collective-permute-start | bytes 3145736 | tf_op jit(solution)/shard_map/ppermute | solution.py:497
  31.0 0.1 collective-permute-start.2
  31.1 2.2 %collective-permute-done.3 = bf16[2,512,512]{2,1,0:T(8,128)(2,1)S(1)} collective-permute-done((bf16[2,512,512]{2,1,0:T(8,128)(2,1)S(1)}, bf16[2,512,512]{2,1,0:T(8,128)(2,1)S(1)}, u32[]{:S(2)}, u32[]{:S(2)}) %collective-permute-start.3) | collective-permute-done | bytes 1048608 | tf_op jit(solution)/shard_map/ppermute | solution.py:497
  33.3 0.4 add_convert_fusion
  33.6 0.6 collective-permute-done.2
  34.3 6.9 %collective-permute-start.6 = (bf16[256,256]{1,0:T(8,128)(2,1)S(1)}, bf16[256,256]{1,0:T(8,128)(2,1)S(1)}, u32[]{:S(2)}, u32[]{:S(2)}) collective-permute-start(bf16[256,256]{1,0:T(8,128)(2,1)S(1)} %add_convert_fusion.7), channel_id=1, source_target_pairs={{0,2},{1,3},{2,0},{3,1},{4,6},{5,7},{6,4},{7,5},{8,10},{9,11},{10,... | collective-permute-start | bytes 393224 | tf_op jit(solution)/shard_map/ppermute | solution.py:497
  41.2 0.1 fusion.3
  41.2 1.3 %collective-permute-start.5 = (bf16[2,256,512]{2,1,0:T(8,128)(2,1)S(1)}, bf16[2,256,512]{2,1,0:T(8,128)(2,1)S(1)}, u32[]{:S(2)}, u32[]{:S(2)}) collective-permute-start(bf16[2,256,512]{2,1,0:T(8,128)(2,1)S(1)} %get-tuple-element.38), channel_id=1, source_target_pairs={{0,4},{4,8},{8,12},{12,16},{16,20},{20,24},{24,28},{1,5},{5,9},{9,... | collective-permute-start | bytes 1572872 | tf_op jit(solution)/shard_map/ppermute | solution.py:503
  42.6 2.4 %collective-permute-done.6 = bf16[256,256]{1,0:T(8,128)(2,1)S(1)} collective-permute-done((bf16[256,256]{1,0:T(8,128)(2,1)S(1)}, bf16[256,256]{1,0:T(8,128)(2,1)S(1)}, u32[]{:S(2)}, u32[]{:S(2)}) %collective-permute-start.6) | collective-permute-done | bytes 131104 | tf_op jit(solution)/shard_map/ppermute | solution.py:497
  45.0 1.9 %collective-permute-start.7 = (bf16[256,256]{1,0:T(8,128)(2,1)S(1)}, bf16[256,256]{1,0:T(8,128)(2,1)S(1)}, u32[]{:S(2)}, u32[]{:S(2)}) collective-permute-start(bf16[256,256]{1,0:T(8,128)(2,1)S(1)} %add_convert_fusion.6), channel_id=1, source_target_pairs={{0,4},{4,0},{8,12},{12,8},{16,20},{20,16},{24,28},{28,24},{1,5},{5... | collective-permute-start | bytes 393224 | tf_op jit(solution)/shard_map/ppermute | solution.py:497
  46.9 2.1 %collective-permute-start.4 = (bf16[2,256,512]{2,1,0:T(8,128)(2,1)S(1)}, bf16[2,256,512]{2,1,0:T(8,128)(2,1)S(1)}, u32[]{:S(2)}, u32[]{:S(2)}) collective-permute-start(bf16[2,256,512]{2,1,0:T(8,128)(2,1)S(1)} %get-tuple-element.39), channel_id=1, source_target_pairs={{0,2},{1,3},{2,0},{3,1},{4,6},{5,7},{6,4},{7,5},{8,10},{9,11},{10,... | collective-permute-start | bytes 1572872 | tf_op jit(solution)/shard_map/ppermute | solution.py:497
  49.0 7.8 %collective-permute-done.7 = bf16[256,256]{1,0:T(8,128)(2,1)S(1)} collective-permute-done((bf16[256,256]{1,0:T(8,128)(2,1)S(1)}, bf16[256,256]{1,0:T(8,128)(2,1)S(1)}, u32[]{:S(2)}, u32[]{:S(2)}) %collective-permute-start.7) | collective-permute-done | bytes 131104 | tf_op jit(solution)/shard_map/ppermute | solution.py:497
  56.9 0.0 collective-permute-done.5
  56.9 6.2 %collective-permute-start.10 = (bf16[256,256]{1,0:T(8,128)(2,1)S(1)}, bf16[256,256]{1,0:T(8,128)(2,1)S(1)}, u32[]{:S(2)}, u32[]{:S(2)}) collective-permute-start(bf16[256,256]{1,0:T(8,128)(2,1)S(1)} %add_convert_fusion.5), channel_id=1, source_target_pairs={{0,8},{4,12},{8,0},{12,4},{16,24},{20,28},{24,16},{28,20},{1,9},{5... | collective-permute-start | bytes 393224 | tf_op jit(solution)/shard_map/ppermute | solution.py:497
  63.1 0.2 fusion.1
  63.3 0.0 collective-permute-done.4
  63.3 3.4 %collective-permute-done.10 = bf16[256,256]{1,0:T(8,128)(2,1)S(1)} collective-permute-done((bf16[256,256]{1,0:T(8,128)(2,1)S(1)}, bf16[256,256]{1,0:T(8,128)(2,1)S(1)}, u32[]{:S(2)}, u32[]{:S(2)}) %collective-permute-start.10) | collective-permute-done | bytes 131104 | tf_op jit(solution)/shard_map/ppermute | solution.py:497
  66.8 2.8 %collective-permute-start.11 = (bf16[256,256]{1,0:T(8,128)(2,1)S(1)}, bf16[256,256]{1,0:T(8,128)(2,1)S(1)}, u32[]{:S(2)}, u32[]{:S(2)}) collective-permute-start(bf16[256,256]{1,0:T(8,128)(2,1)S(1)} %add_convert_fusion.4), channel_id=1, source_target_pairs={{0,16},{4,20},{8,24},{12,28},{16,0},{20,4},{24,8},{28,12},{1,17},{... | collective-permute-start | bytes 393224 | tf_op jit(solution)/shard_map/ppermute | solution.py:497
  69.6 0.1 add_convert_fusion.2.own
  69.7 0.1 collective-permute-start.9
  69.8 1.8 %collective-permute-start.8 = (bf16[2,256,512]{2,1,0:T(8,128)(2,1)S(1)}, bf16[2,256,512]{2,1,0:T(8,128)(2,1)S(1)}, u32[]{:S(2)}, u32[]{:S(2)}) collective-permute-start(bf16[2,256,512]{2,1,0:T(8,128)(2,1)S(1)} %fusion.1), channel_id=1, source_target_pairs={{0,2},{1,3},{2,0},{3,1},{4,6},{5,7},{6,4},{7,5},{8,10},{9,11},{10,... | collective-permute-start | bytes 1572872 | tf_op jit(solution)/shard_map/ppermute | solution.py:497
  71.6 3.9 %collective-permute-done.11 = bf16[256,256]{1,0:T(8,128)(2,1)S(1)} collective-permute-done((bf16[256,256]{1,0:T(8,128)(2,1)S(1)}, bf16[256,256]{1,0:T(8,128)(2,1)S(1)}, u32[]{:S(2)}, u32[]{:S(2)}) %collective-permute-start.11) | collective-permute-done | bytes 131104 | tf_op jit(solution)/shard_map/ppermute | solution.py:497
  75.5 0.1 collective-permute-start.12
  75.6 1.3 %collective-permute-done.12 = bf16[256,256]{1,0:T(8,128)(2,1)S(1)} collective-permute-done((bf16[256,256]{1,0:T(8,128)(2,1)S(1)}, bf16[256,256]{1,0:T(8,128)(2,1)S(1)}, u32[]{:S(2)}, u32[]{:S(2)}) %collective-permute-start.12) | collective-permute-done | bytes 131104 | tf_op jit(solution)/shard_map/ppermute | solution.py:497
  76.9 0.8 fusion.2
  77.8 0.0 collective-permute-done.9.theirs
  77.8 2.0 %write_rows.2.rest_0_ = f32[2,2,512,512]{3,2,1,0:T(8,128)} custom-call(s32[3]{0:T(128)S(1)} %pad_add_fusion.meta, bf16[2,256,512]{2,1,0:T(8,128)(2,1)S(1)} %add_convert_fusion.2.own, bf16[2,256,512]{2,1,0:T(8,128)(2,1)S(1)} %collective-permute-done.9.theirs), custom_call_target="tpu_custom_call" | custom-call | tf_op jit(solution)/shard_map/write_rows/pallas_call | solution.py:480
  79.8 4.3 %collective-permute-done.8 = bf16[2,256,512]{2,1,0:T(8,128)(2,1)S(1)} collective-permute-done((bf16[2,256,512]{2,1,0:T(8,128)(2,1)S(1)}, bf16[2,256,512]{2,1,0:T(8,128)(2,1)S(1)}, u32[]{:S(2)}, u32[]{:S(2)}) %collective-permute-start.8) | collective-permute-done | bytes 524320 | tf_op jit(solution)/shard_map/ppermute | solution.py:497
  84.1 0.1 add_convert_fusion.1.own
  84.3 0.1 collective-permute-start.13
  84.3 1.9 %collective-permute-done.13.theirs = bf16[2,256,512]{2,1,0:T(8,128)(2,1)S(1)} collective-permute-done((bf16[2,256,512]{2,1,0:T(8,128)(2,1)S(1)}, bf16[2,256,512]{2,1,0:T(8,128)(2,1)S(1)}, u32[]{:S(2)}, u32[]{:S(2)}) %collective-permute-start.13) | collective-permute-done | bytes 524320 | tf_op jit(solution)/shard_map/ppermute | solution.py:497
  86.2 2.0 %write_rows.3 = f32[2,2,512,512]{3,2,1,0:T(8,128)} custom-call(s32[3]{0:T(128)S(1)} %pad_add_fusion.meta, bf16[2,256,512]{2,1,0:T(8,128)(2,1)S(1)} %add_convert_fusion.1.own, bf16[2,256,512]{2,1,0:T(8,128)(2,1)S(1)} %collective-permute-done.13.theirs, f32[2,2,512,512]{3,2,1,0:T(8,128)} %write_rows.2.rest_0_), custom_call_target="tpu_custom_call", output_to_operand_aliasing={{}: (3, {})} | custom-call | tf_op jit(solution)/shard_map/write_rows/pallas_call | solution.py:480
  (22 shorter events, 0.2 us)
Async XLA Ops:
  1.7 16.8 %collective-permute-start = (bf16[2,1,256,512]{3,2,1,0:T(8,128)(2,1)S(1)}, bf16[2,1,256,512]{3,2,1,0:T(8,128)(2,1)S(1)}, u32[]{:S(2)}, u32[]{:S(2)}) collective-permute-start(bf16[2,1,256,512]{3,2,1,0:T(8,128)(2,1)S(1)} %constant_dynamic-slice_fusion), channel_id=1, source_target_pairs={{4,0},{8,4},{12,8},{16,12},{20,16},{24,20},{28,24},{5,1},{9,5},{13... | collective-permute-start | bytes 1572872 | tf_op jit(solution)/shard_map/ppermute | solution.py:503
  4.5 1.6 %copy-start = (bf16[2,2,512,512]{3,2,1,0:T(8,128)(2,1)S(1)}, bf16[2,2,512,512]{3,2,1,0:T(8,128)(2,1)}, u32[]{:S(2)}) copy-start(bf16[2,2,512,512]{3,2,1,0:T(8,128)(2,1)} %spec_hbm.3) | copy-start | bytes 6291460
  6.1 1.2 %copy-start.2 = (bf16[8,256,256]{2,1,0:T(8,128)(2,1)S(1)}, bf16[8,256,256]{2,1,0:T(8,128)(2,1)}, u32[]{:S(2)}) copy-start(bf16[8,256,256]{2,1,0:T(8,128)(2,1)} %amp_hbm.3) | copy-start | bytes 3145732
  7.3 1.0 %copy-start.4 = (f32[2,256,256]{2,1,0:T(8,128)S(1)}, f32[2,256,256]{2,1,0:T(8,128)}, u32[]{:S(2)}) copy-start(f32[2,256,256]{2,1,0:T(8,128)} %probe_hbm.3) | copy-start | bytes 1572868
  8.4 1.0 %copy-start.6 = (bf16[512,512]{1,0:T(8,128)(2,1)S(1)}, bf16[512,512]{1,0:T(8,128)(2,1)}, u32[]{:S(2)}) copy-start(bf16[512,512]{1,0:T(8,128)(2,1)} %constant.36.clone.rf_hbm) | copy-start | bytes 1572868
  9.4 1.0 %copy-start.7 = (bf16[512,512]{1,0:T(8,128)(2,1)S(1)}, bf16[512,512]{1,0:T(8,128)(2,1)}, u32[]{:S(2)}) copy-start(bf16[512,512]{1,0:T(8,128)(2,1)} %constant.35.clone.lf_hbm) | copy-start | bytes 1572868
  10.5 1.0 %copy-start.8 = (bf16[512,512]{1,0:T(8,128)(2,1)S(1)}, bf16[512,512]{1,0:T(8,128)(2,1)}, u32[]{:S(2)}) copy-start(bf16[512,512]{1,0:T(8,128)(2,1)} %constant.34.clone.ra_hbm) | copy-start | bytes 1572868
  11.5 1.0 %copy-start.9 = (bf16[512,512]{1,0:T(8,128)(2,1)S(1)}, bf16[512,512]{1,0:T(8,128)(2,1)}, u32[]{:S(2)}) copy-start(bf16[512,512]{1,0:T(8,128)(2,1)} %constant.33.clone.la_hbm) | copy-start | bytes 1572868
  12.5 7.9 %copy-start.1 = (bf16[2,2,512,512]{3,2,1,0:T(8,128)(2,1)S(1)}, bf16[2,2,512,512]{3,2,1,0:T(8,128)(2,1)}, u32[]{:S(2)}) copy-start(bf16[2,2,512,512]{3,2,1,0:T(8,128)(2,1)} %spec_hbm.3) | copy-start | bytes 6291460
  12.5 7.9 %copy-start.3 = (bf16[8,256,256]{2,1,0:T(8,128)(2,1)S(1)}, bf16[8,256,256]{2,1,0:T(8,128)(2,1)}, u32[]{:S(2)}) copy-start(bf16[8,256,256]{2,1,0:T(8,128)(2,1)} %amp_hbm.3) | copy-start | bytes 3145732
  12.6 7.9 %copy-start.5 = (f32[2,256,256]{2,1,0:T(8,128)S(1)}, f32[2,256,256]{2,1,0:T(8,128)}, u32[]{:S(2)}) copy-start(f32[2,256,256]{2,1,0:T(8,128)} %probe_hbm.3) | copy-start | bytes 1572868
  12.6 7.9 %copy-start.10 = (bf16[512,512]{1,0:T(8,128)(2,1)S(1)}, bf16[512,512]{1,0:T(8,128)(2,1)}, u32[]{:S(2)}) copy-start(bf16[512,512]{1,0:T(8,128)(2,1)} %constant.33.clone.la_hbm) | copy-start | bytes 1572868
  18.5 1.9 %collective-permute-start.1 = (bf16[2,1,256,512]{3,2,1,0:T(8,128)(2,1)S(1)}, bf16[2,1,256,512]{3,2,1,0:T(8,128)(2,1)S(1)}, u32[]{:S(2)}, u32[]{:S(2)}) collective-permute-start(bf16[2,1,256,512]{3,2,1,0:T(8,128)(2,1)S(1)} %collective-permute-done.rim_own_any), channel_id=1, source_target_pairs={{0,1},{1,0},{2,3},{3,2},{4,5},{5,4},{6,7},{7,6},{8,9},{9,8},{10,11... | collective-permute-start | bytes 1572872 | tf_op jit(solution)/shard_map/ppermute | solution.py:497
  27.1 6.2 %collective-permute-start.3 = (bf16[2,512,512]{2,1,0:T(8,128)(2,1)S(1)}, bf16[2,512,512]{2,1,0:T(8,128)(2,1)S(1)}, u32[]{:S(2)}, u32[]{:S(2)}) collective-permute-start(bf16[2,512,512]{2,1,0:T(8,128)(2,1)S(1)} %get-tuple-element.26), channel_id=1, source_target_pairs={{0,1},{1,0},{2,3},{3,2},{4,5},{5,4},{6,7},{7,6},{8,9},{9,8},{10,11... | collective-permute-start | bytes 3145736 | tf_op jit(solution)/shard_map/ppermute | solution.py:497
  31.0 3.2 %collective-permute-start.2 = (bf16[640,512]{1,0:T(8,128)(2,1)S(1)}, bf16[640,512]{1,0:T(8,128)(2,1)S(1)}, u32[]{:S(2)}, u32[]{:S(2)}) collective-permute-start(bf16[640,512]{1,0:T(8,128)(2,1)S(1)} %get-tuple-element.24), channel_id=1, source_target_pairs={{0,1},{1,0},{2,3},{3,2},{4,5},{5,4},{6,7},{7,6},{8,9},{9,8},{10,11... | collective-permute-start | bytes 1966088 | tf_op jit(solution)/shard_map/ppermute | solution.py:497
  34.3 10.7 %collective-permute-start.6 = (bf16[256,256]{1,0:T(8,128)(2,1)S(1)}, bf16[256,256]{1,0:T(8,128)(2,1)S(1)}, u32[]{:S(2)}, u32[]{:S(2)}) collective-permute-start(bf16[256,256]{1,0:T(8,128)(2,1)S(1)} %add_convert_fusion.7), channel_id=1, source_target_pairs={{0,2},{1,3},{2,0},{3,1},{4,6},{5,7},{6,4},{7,5},{8,10},{9,11},{10,... | collective-permute-start | bytes 393224 | tf_op jit(solution)/shard_map/ppermute | solution.py:497
  41.2 15.6 %collective-permute-start.5 = (bf16[2,256,512]{2,1,0:T(8,128)(2,1)S(1)}, bf16[2,256,512]{2,1,0:T(8,128)(2,1)S(1)}, u32[]{:S(2)}, u32[]{:S(2)}) collective-permute-start(bf16[2,256,512]{2,1,0:T(8,128)(2,1)S(1)} %get-tuple-element.38), channel_id=1, source_target_pairs={{0,4},{4,8},{8,12},{12,16},{16,20},{20,24},{24,28},{1,5},{5,9},{9,... | collective-permute-start | bytes 1572872 | tf_op jit(solution)/shard_map/ppermute | solution.py:503
  45.0 11.8 %collective-permute-start.7 = (bf16[256,256]{1,0:T(8,128)(2,1)S(1)}, bf16[256,256]{1,0:T(8,128)(2,1)S(1)}, u32[]{:S(2)}, u32[]{:S(2)}) collective-permute-start(bf16[256,256]{1,0:T(8,128)(2,1)S(1)} %add_convert_fusion.6), channel_id=1, source_target_pairs={{0,4},{4,0},{8,12},{12,8},{16,20},{20,16},{24,28},{28,24},{1,5},{5... | collective-permute-start | bytes 393224 | tf_op jit(solution)/shard_map/ppermute | solution.py:497
  46.9 16.4 %collective-permute-start.4 = (bf16[2,256,512]{2,1,0:T(8,128)(2,1)S(1)}, bf16[2,256,512]{2,1,0:T(8,128)(2,1)S(1)}, u32[]{:S(2)}, u32[]{:S(2)}) collective-permute-start(bf16[2,256,512]{2,1,0:T(8,128)(2,1)S(1)} %get-tuple-element.39), channel_id=1, source_target_pairs={{0,2},{1,3},{2,0},{3,1},{4,6},{5,7},{6,4},{7,5},{8,10},{9,11},{10,... | collective-permute-start | bytes 1572872 | tf_op jit(solution)/shard_map/ppermute | solution.py:497
  56.9 9.9 %collective-permute-start.10 = (bf16[256,256]{1,0:T(8,128)(2,1)S(1)}, bf16[256,256]{1,0:T(8,128)(2,1)S(1)}, u32[]{:S(2)}, u32[]{:S(2)}) collective-permute-start(bf16[256,256]{1,0:T(8,128)(2,1)S(1)} %add_convert_fusion.5), channel_id=1, source_target_pairs={{0,8},{4,12},{8,0},{12,4},{16,24},{20,28},{24,16},{28,20},{1,9},{5... | collective-permute-start | bytes 393224 | tf_op jit(solution)/shard_map/ppermute | solution.py:497
  66.8 8.7 %collective-permute-start.11 = (bf16[256,256]{1,0:T(8,128)(2,1)S(1)}, bf16[256,256]{1,0:T(8,128)(2,1)S(1)}, u32[]{:S(2)}, u32[]{:S(2)}) collective-permute-start(bf16[256,256]{1,0:T(8,128)(2,1)S(1)} %add_convert_fusion.4), channel_id=1, source_target_pairs={{0,16},{4,20},{8,24},{12,28},{16,0},{20,4},{24,8},{28,12},{1,17},{... | collective-permute-start | bytes 393224 | tf_op jit(solution)/shard_map/ppermute | solution.py:497
  69.7 8.1 %collective-permute-start.9 = (bf16[2,256,512]{2,1,0:T(8,128)(2,1)S(1)}, bf16[2,256,512]{2,1,0:T(8,128)(2,1)S(1)}, u32[]{:S(2)}, u32[]{:S(2)}) collective-permute-start(bf16[2,256,512]{2,1,0:T(8,128)(2,1)S(1)} %add_convert_fusion.2.own), channel_id=1, source_target_pairs={{0,1},{1,0},{2,3},{3,2},{4,5},{5,4},{6,7},{7,6},{8,9},{9,8},{10,11... | collective-permute-start | bytes 1572872 | tf_op jit(solution)/shard_map/ppermute | solution.py:497
  69.8 14.3 %collective-permute-start.8 = (bf16[2,256,512]{2,1,0:T(8,128)(2,1)S(1)}, bf16[2,256,512]{2,1,0:T(8,128)(2,1)S(1)}, u32[]{:S(2)}, u32[]{:S(2)}) collective-permute-start(bf16[2,256,512]{2,1,0:T(8,128)(2,1)S(1)} %fusion.1), channel_id=1, source_target_pairs={{0,2},{1,3},{2,0},{3,1},{4,6},{5,7},{6,4},{7,5},{8,10},{9,11},{10,... | collective-permute-start | bytes 1572872 | tf_op jit(solution)/shard_map/ppermute | solution.py:497
  75.5 1.4 %collective-permute-start.12 = (bf16[256,256]{1,0:T(8,128)(2,1)S(1)}, bf16[256,256]{1,0:T(8,128)(2,1)S(1)}, u32[]{:S(2)}, u32[]{:S(2)}) collective-permute-start(bf16[256,256]{1,0:T(8,128)(2,1)S(1)} %add_convert_fusion.3), channel_id=1, source_target_pairs={{0,1},{1,0},{2,3},{3,2},{4,5},{5,4},{6,7},{7,6},{8,9},{9,8},{10,11... | collective-permute-start | bytes 393224 | tf_op jit(solution)/shard_map/ppermute | solution.py:497
  84.3 2.0 %collective-permute-start.13 = (bf16[2,256,512]{2,1,0:T(8,128)(2,1)S(1)}, bf16[2,256,512]{2,1,0:T(8,128)(2,1)S(1)}, u32[]{:S(2)}, u32[]{:S(2)}) collective-permute-start(bf16[2,256,512]{2,1,0:T(8,128)(2,1)S(1)} %add_convert_fusion.1.own), channel_id=1, source_target_pairs={{0,1},{1,0},{2,3},{3,2},{4,5},{5,4},{6,7},{7,6},{8,9},{9,8},{10,11... | collective-permute-start | bytes 1572872 | tf_op jit(solution)/shard_map/ppermute | solution.py:497

commit v4 on v3

--- a/solution.py
+++ b/solution.py
@@ -420,7 +420,7 @@
         in_specs=[SMEM, SMEM] + [HBM] * 7,
         out_specs=(VMEM, VMEM),
         scratch_shapes=lead + work,
-        compiler_params=pltpu.CompilerParams(vmem_limit_bytes=32 * 1024 * 1024),
+        compiler_params=pltpu.CompilerParams(vmem_limit_bytes=62 * 1024 * 1024),
         name="early_slots",
     )(meta, anchor, probe, spec, amp, *tables)
 
@@ -451,7 +451,7 @@
             pltpu.VMEM((2, edge, edge), jnp.float32),
         ]
         + work,
-        compiler_params=pltpu.CompilerParams(vmem_limit_bytes=36 * 1024 * 1024),
+        compiler_params=pltpu.CompilerParams(vmem_limit_bytes=60 * 1024 * 1024),
         name="late_slots",
     )(meta, anchor, probe, spec, rim_own, rim_other, acc, probe_acc, amp, *tables)
 
@@ -507,10 +507,15 @@
     return (own.astype(jnp.float32) + got.astype(jnp.float32)).astype(jnp.bfloat16)
 
 
+def unfolded(value, edge):
+    return jnp.concatenate([value[:, k : k + edge] for k in range(0, value.shape[1], edge)], 0)
+
+
 def body(probe_field, specimen, amplitude, scan_anchor, counts):
     edge = probe_field.shape[1]
     _, slices, tile_rows, width = specimen.shape
     side = width // edge
+    deep = edge // side
     half = lax.axis_index("pos") % 2
     base_row = lax.axis_index("tile") * tile_rows
     meta = jnp.stack([counts[0], base_row, half]).astype(jnp.int32)
@@ -533,41 +538,38 @@
         amplitude,
         tables,
     )
-    got_low = traded(sent_low, "pos", 1)
+    low = (kept_low + traded(sent_low, "pos", 1).astype(jnp.float32)).astype(jnp.bfloat16)
+    sent_top, low = lax.optimization_barrier((sent_top, low))
     got_top = traded(sent_top, "pos", 1)
-    low = (kept_low + got_low.astype(jnp.float32)).astype(jnp.bfloat16)
-    got_top, low = lax.optimization_barrier((got_top, low))
+    below = passed_along(low[:, tile_rows - edge :], "tile", 1)
     lower = low[:, : tile_rows - edge]
     lower_got = traded(lower, "pos", 2)
-    below = passed_along(low[:, tile_rows - edge :], "tile", 1)
     top = kept_top + got_top[: 2 * edge].reshape(2, edge, width).astype(jnp.float32)
-    got_probe = jnp.concatenate(
-        [got_top[2 * edge :, p * edge : (p + 1) * edge] for p in range(side)], 0
-    )
+    got_probe = unfolded(got_top[2 * edge :], edge)
     probe_part = (kept_probe + got_probe.astype(jnp.float32)).astype(jnp.bfloat16)
-    probe_part = narrow_sum(probe_part, traded(probe_part, "pos", 2))
-    probe_part = narrow_sum(probe_part, traded(probe_part, "tile", 1))
-    below, probe_part = lax.optimization_barrier((below, probe_part))
-    upper = (top + below.astype(jnp.float32)).astype(jnp.bfloat16)
-    lower_got, upper = lax.optimization_barrier((lower_got, upper))
-    upper_got = traded(upper, "pos", 2)
     distance = 2
     while distance < lax.axis_size("tile"):
         probe_part = narrow_sum(probe_part, traded(probe_part, "tile", distance))
         distance *= 2
+    upper = (top + below.astype(jnp.float32)).astype(jnp.bfloat16)
+    folded = jnp.concatenate([probe_part[p * deep : (p + 1) * deep] for p in range(side)], 1)
+    upper = jnp.concatenate([upper.reshape(2 * edge, width), folded], 0)
+    lower_got, upper = lax.optimization_barrier((lower_got, upper))
+    upper_got = traded(upper, "pos", 2)
     lower = narrow_sum(lower, lower_got)
     lower_theirs = traded(lower, "pos", 1)
     tile_grad = write_rows(meta, lower, lower_theirs, edge, specimen.shape)
+    upper_got, tile_grad = lax.optimization_barrier((upper_got, tile_grad))
+    upper = narrow_sum(upper, upper_got)
+    probe_part = unfolded(upper[2 * edge :], edge)
+    probe_part = narrow_sum(probe_part, traded(probe_part, "tile", 1))
+    upper = upper[: 2 * edge].reshape(2, edge, width)
+    upper_theirs = traded(upper, "pos", 1)
+    tile_grad = write_rows(meta, upper, upper_theirs, 0, specimen.shape, tile_grad)
     probe_theirs = traded(probe_part, "pos", 1)
     probe_total = jnp.where(
         half == 0, jnp.stack([probe_part, probe_theirs]), jnp.stack([probe_theirs, probe_part])
     ).astype(jnp.float32)
-    upper_got, tile_grad, probe_total = lax.optimization_barrier(
-        (upper_got, tile_grad, probe_total)
-    )
-    upper = narrow_sum(upper, upper_got)
-    upper_theirs = traded(upper, "pos", 1)
-    tile_grad = write_rows(meta, upper, upper_theirs, 0, specimen.shape, tile_grad)
     return (tile_grad, probe_total)
 
 

time: 86.8 us -> 97.1 us (1.12)
  the two profiles are of different devices: /device:TPU:0 before, /device:TPU:27 now
where the time goes in v4:
time: 97.1 us; the launch traced here: 97.9 us
  waiting for transfers between devices  42.8 us (44%)
  starting transfers between devices  24.4 us (25%)
  Pallas kernels  21.5 us (22%)
  other arithmetic  4.22 us (4%)
  local copies, waits for them, and re-layouts  3.44 us (4%)
  between operations  1.54 us (2%)
    ppermute x11, waiting for transfers between devices, traded(): return lax.ppermute(value, axis, [(i, i ^ distance) for i in range(count)])  42.8 us
    ppermute x11, starting transfers between devices, traded(): return lax.ppermute(value, axis, [(i, i ^ distance) for i in range(count)])  21 us
    pallas_call x1, Pallas kernels, run_early(): pl.pallas_call(early_kernel, out_shape=(jax.ShapeDtypeStruct((2, slices,...  9.37 us
    pallas_call x1, Pallas kernels, run_late(): pl.pallas_call(late_kernel, out_shape=(jax.ShapeDtypeStruct((2, tile_rows...  8.04 us
    pallas_call x2, Pallas kernels, write_rows(): pl.pallas_call(kernel, out_shape=jax.ShapeDtypeStruct(shape, jnp.float32)...  4.04 us
    ppermute x2, starting transfers between devices, passed_along(): lax.ppermute(value, axis, [(source, source + steps) for source in range(i...  3.48 us
    unnamed x13, local copies, waits for them, and re-layouts  2.17 us
    convert_element_type x1, other arithmetic, body(): (kept_low + traded(sent_low, 'pos', 1).astype(jnp.float32)).astype(jnp.bf...  2 us
  transfers between devices with their start and end apart: 13, of which 9 were waited for; matrix products, arithmetic and copies ran while one was open for 4% of the time, Pallas kernels for 12%

profile of v4, /device:TPU:27, one launch (start us, length us, event | category | flops | bytes accessed | tf_op | source)
XLA Modules:
  0.0 97.9 jit_solution(5182526799518773041)
XLA Ops:
  0.6 1.1 %constant_dynamic-slice_fusion = bf16[2,1,256,512]{3,2,1,0:T(8,128)(2,1)S(1)} fusion(bf16[2,2,512,512]{3,2,1,0:T(8,128)(2,1)} %spec_hbm.3, s32[]{:T(128)S(6)} %select_n.19), kind=kLoop, calls=%fused_computation.15 | loop fusion | bytes 1048580 | tf_op jit(solution)/shard_map/dynamic_slice | solution.py:524
  1.7 2.2 %collective-permute-start = (bf16[2,1,256,512]{3,2,1,0:T(8,128)(2,1)S(1)}, bf16[2,1,256,512]{3,2,1,0:T(8,128)(2,1)S(1)}, u32[]{:S(2)}, u32[]{:S(2)}) collective-permute-start(bf16[2,1,256,512]{3,2,1,0:T(8,128)(2,1)S(1)} %constant_dynamic-slice_fusion), channel_id=1, source_target_pairs={{4,0},{8,4},{12,8},{16,12},{20,16},{24,20},{28,24},{5,1},{9,5},{13... | collective-permute-start | bytes 1572872 | tf_op jit(solution)/shard_map/ppermute | solution.py:503
  4.6 1.3 %copy.13.anchor = s32[8,2]{1,0:T(8,128)} copy(s32[8,2]{0,1:T(2,128)} %param.12) | data formatting | bytes 128 | tf_op args[3]
  5.9 0.6 pad_add_fusion.meta
  6.5 9.4 %early_slots.1 = (f32[2,2,4,512,128]{4,3,2,1,0:T(8,128)}, f32[2,256,256]{2,1,0:T(8,128)}) custom-call(s32[3]{0:T(128)} %pad_add_fusion.meta, s32[8,2]{1,0:T(8,128)} %copy.13.anchor, f32[2,256,256]{2,1,0:T(8,128)} %probe_hbm.3, bf16[2,2,512,512]{3,2,1,0:T(8,128)(2,1)} %spec_hbm.3, bf16[8,256,256]{2,1,0:T(8,128)(2,1)} %amp_hbm.3, ...), custom_call_target="tpu_custom_call" | custom-call | tf_op jit(solution)/shard_map/early_slots/pallas_call | solution.py:414
  15.9 0.0 collective-permute-done.rim_own_any
  15.9 0.0 copy-start.2
  15.9 1.0 %collective-permute-start.1 = (bf16[2,1,256,512]{3,2,1,0:T(8,128)(2,1)S(1)}, bf16[2,1,256,512]{3,2,1,0:T(8,128)(2,1)S(1)}, u32[]{:S(2)}, u32[]{:S(2)}) collective-permute-start(bf16[2,1,256,512]{3,2,1,0:T(8,128)(2,1)S(1)} %collective-permute-done.rim_own_any), channel_id=1, source_target_pairs={{0,1},{1,0},{2,3},{3,2},{4,5},{5,4},{6,7},{7,6},{8,9},{9,8},{10,11... | collective-permute-start | bytes 1572872 | tf_op jit(solution)/shard_map/ppermute | solution.py:497
  16.9 1.5 %collective-permute-done.1.rim_other_any = bf16[2,1,256,512]{3,2,1,0:T(8,128)(2,1)S(1)} collective-permute-done((bf16[2,1,256,512]{3,2,1,0:T(8,128)(2,1)S(1)}, bf16[2,1,256,512]{3,2,1,0:T(8,128)(2,1)S(1)}, u32[]{:S(2)}, u32[]{:S(2)}) %collective-permute-start.1) | collective-permute-done | bytes 524320 | tf_op jit(solution)/shard_map/ppermute | solution.py:497
  18.5 0.0 copy-done.2
  18.5 0.8 copy-done.3
  19.3 8.0 %late_slots.1 = (bf16[2,512,512]{2,1,0:T(8,128)(2,1)}, bf16[640,512]{1,0:T(8,128)(2,1)}, f32[2,512,512]{2,1,0:T(8,128)}, f32[2,256,512]{2,1,0:T(8,128)}, f32[256,256]{1,0:T(8,128)}) custom-call(s32[3]{0:T(128)} %pad_add_fusion.meta, s32[8,2]{1,0:T(8,128)} %copy.13.anchor, f32[2,256,256]{2,1,0:T(8,128)} %probe_hbm.3, bf16[2,2,512,512]{3,2,1,0:T(8,128)(2,1)} %spec_hbm.3, ...), custom_call_target="tpu_custom_call" | custom-call | tf_op jit(solution)/shard_map/late_slots/pallas_call | solution.py:435
  27.3 4.3 %collective-permute-start.2 = (bf16[2,512,512]{2,1,0:T(8,128)(2,1)}, bf16[2,512,512]{2,1,0:T(8,128)(2,1)S(1)}, u32[]{:S(2)}, u32[]{:S(2)}) collective-permute-start(bf16[2,512,512]{2,1,0:T(8,128)(2,1)} %get-tuple-element.23), channel_id=1, source_target_pairs={{0,1},{1,0},{2,3},{3,2},{4,5},{5,4},{6,7},{7,6},{8,9},{9,8},{10,11... | collective-permute-start | bytes 3145736 | tf_op jit(solution)/shard_map/ppermute | solution.py:497
  31.6 2.5 %collective-permute-done.2 = bf16[2,512,512]{2,1,0:T(8,128)(2,1)S(1)} collective-permute-done((bf16[2,512,512]{2,1,0:T(8,128)(2,1)}, bf16[2,512,512]{2,1,0:T(8,128)(2,1)S(1)}, u32[]{:S(2)}, u32[]{:S(2)}) %collective-permute-start.2) | collective-permute-done | bytes 1048608 | tf_op jit(solution)/shard_map/ppermute | solution.py:497
  34.1 2.0 %add_convert_fusion = bf16[2,512,512]{2,1,0:T(8,128)(2,1)S(1)} fusion(f32[2,512,512]{2,1,0:T(8,128)} %get-tuple-element.22, bf16[2,512,512]{2,1,0:T(8,128)(2,1)S(1)} %collective-permute-done.2), kind=kLoop, calls=%fused_computation | loop fusion | flops 1572864 | bytes 4194304 | tf_op jit(solution)/shard_map/convert_element_type | solution.py:541
  36.1 0.0 copy-start.4
  36.1 0.0 copy-done.5
  36.1 0.0 copy-start.1
  36.1 0.4 collective-permute-start.4
  36.6 0.1 fusion.3
  36.7 1.3 %collective-permute-start.5 = (bf16[2,256,512]{2,1,0:T(8,128)(2,1)S(1)}, bf16[2,256,512]{2,1,0:T(8,128)(2,1)S(1)}, u32[]{:S(2)}, u32[]{:S(2)}) collective-permute-start(bf16[2,256,512]{2,1,0:T(8,128)(2,1)S(1)} %get-tuple-element.32), channel_id=1, source_target_pairs={{0,4},{4,8},{8,12},{12,16},{16,20},{20,24},{24,28},{1,5},{5,9},{9,... | collective-permute-start | bytes 1572872 | tf_op jit(solution)/shard_map/ppermute | solution.py:503
  38.0 0.3 collective-permute-done.4
  38.3 0.0 copy-done.4
  38.3 10.4 %collective-permute-start.6 = (bf16[256,256]{1,0:T(8,128)(2,1)S(1)}, bf16[256,256]{1,0:T(8,128)(2,1)S(1)}, u32[]{:S(2)}, u32[]{:S(2)}) collective-permute-start(bf16[256,256]{1,0:T(8,128)(2,1)S(1)} %add_convert_fusion.6), channel_id=1, source_target_pairs={{0,8},{4,12},{8,0},{12,4},{16,24},{20,28},{24,16},{28,20},{1,9},{5... | collective-permute-start | bytes 393224 | tf_op jit(solution)/shard_map/ppermute | solution.py:497
  48.7 0.0 collective-permute-start.3
  48.8 14.4 %collective-permute-done.6 = bf16[256,256]{1,0:T(8,128)(2,1)S(1)} collective-permute-done((bf16[256,256]{1,0:T(8,128)(2,1)S(1)}, bf16[256,256]{1,0:T(8,128)(2,1)S(1)}, u32[]{:S(2)}, u32[]{:S(2)}) %collective-permute-start.6) | collective-permute-done | bytes 131104 | tf_op jit(solution)/shard_map/ppermute | solution.py:497
  63.2 0.1 collective-permute-start.7
  63.3 0.0 collective-permute-done.5
  63.3 0.0 copy-done.1
  63.3 0.3 fusion.1
  63.6 0.0 copy-start
  63.6 7.7 %collective-permute-done.7 = bf16[256,256]{1,0:T(8,128)(2,1)S(1)} collective-permute-done((bf16[256,256]{1,0:T(8,128)(2,1)S(1)}, bf16[256,256]{1,0:T(8,128)(2,1)S(1)}, u32[]{:S(2)}, u32[]{:S(2)}) %collective-permute-start.7) | collective-permute-done | bytes 131104 | tf_op jit(solution)/shard_map/ppermute | solution.py:497
  71.4 0.0 collective-permute-done.3
  71.4 0.1 collective-permute-start.8
  71.5 0.1 add_convert_fusion.2.own
  71.7 0.6 collective-permute-start.9
  72.3 1.5 %collective-permute-done.9.theirs = bf16[2,256,512]{2,1,0:T(8,128)(2,1)S(1)} collective-permute-done((bf16[2,256,512]{2,1,0:T(8,128)(2,1)S(1)}, bf16[2,256,512]{2,1,0:T(8,128)(2,1)S(1)}, u32[]{:S(2)}, u32[]{:S(2)}) %collective-permute-start.9) | collective-permute-done | bytes 524320 | tf_op jit(solution)/shard_map/ppermute | solution.py:497
  73.8 2.0 %write_rows.2.rest_0_ = f32[2,2,512,512]{3,2,1,0:T(8,128)} custom-call(s32[3]{0:T(128)S(1)} %copy-done, bf16[2,256,512]{2,1,0:T(8,128)(2,1)S(1)} %add_convert_fusion.2.own, bf16[2,256,512]{2,1,0:T(8,128)(2,1)S(1)} %collective-permute-done.9.theirs), custom_call_target="tpu_custom_call" | custom-call | tf_op jit(solution)/shard_map/write_rows/pallas_call | solution.py:480
  75.8 11.4 %collective-permute-done.8 = bf16[640,512]{1,0:T(8,128)(2,1)S(1)} collective-permute-done((bf16[640,512]{1,0:T(8,128)(2,1)S(1)}, bf16[640,512]{1,0:T(8,128)(2,1)S(1)}, u32[]{:S(2)}, u32[]{:S(2)}) %collective-permute-start.8) | collective-permute-done | bytes 655392 | tf_op jit(solution)/shard_map/ppermute | solution.py:497
  87.3 0.2 add_convert_fusion.1
  87.5 0.1 collective-permute-start.11
  87.6 1.5 %collective-permute-start.10 = (bf16[2,256,512]{2,1,0:T(8,128)(2,1)S(1)}, bf16[2,256,512]{2,1,0:T(8,128)(2,1)S(1)}, u32[]{:S(2)}, u32[]{:S(2)}) collective-permute-start(bf16[2,256,512]{2,1,0:T(8,128)(2,1)S(1)} %bitcast.8), channel_id=1, source_target_pairs={{0,1},{1,0},{2,3},{3,2},{4,5},{5,4},{6,7},{7,6},{8,9},{9,8},{10,11... | collective-permute-start | bytes 1572872 | tf_op jit(solution)/shard_map/ppermute | solution.py:497
  89.1 2.3 %collective-permute-done.11 = bf16[256,256]{1,0:T(8,128)(2,1)S(1)} collective-permute-done((bf16[256,256]{1,0:T(8,128)(2,1)S(1)}, bf16[256,256]{1,0:T(8,128)(2,1)S(1)}, u32[]{:S(2)}, u32[]{:S(2)}) %collective-permute-start.11) | collective-permute-done | bytes 131104 | tf_op jit(solution)/shard_map/ppermute | solution.py:497
  91.4 2.6 %collective-permute-start.12 = (bf16[256,256]{1,0:T(8,128)(2,1)S(1)}, bf16[256,256]{1,0:T(8,128)(2,1)S(1)}, u32[]{:S(2)}, u32[]{:S(2)}) collective-permute-start(bf16[256,256]{1,0:T(8,128)(2,1)S(1)} %add_convert_fusion.3), channel_id=1, source_target_pairs={{0,1},{1,0},{2,3},{3,2},{4,5},{5,4},{6,7},{7,6},{8,9},{9,8},{10,11... | collective-permute-start | bytes 393224 | tf_op jit(solution)/shard_map/ppermute | solution.py:497
  94.0 1.0 %collective-permute-done.12 = bf16[256,256]{1,0:T(8,128)(2,1)S(1)} collective-permute-done((bf16[256,256]{1,0:T(8,128)(2,1)S(1)}, bf16[256,256]{1,0:T(8,128)(2,1)S(1)}, u32[]{:S(2)}, u32[]{:S(2)}) %collective-permute-start.12) | collective-permute-done | bytes 131104 | tf_op jit(solution)/shard_map/ppermute | solution.py:497
  95.0 0.8 fusion.2
  95.8 0.0 collective-permute-done.10.theirs
  95.8 2.0 %write_rows.3 = f32[2,2,512,512]{3,2,1,0:T(8,128)} custom-call(s32[3]{0:T(128)S(1)} %copy-done, bf16[2,256,512]{2,1,0:T(8,128)(2,1)S(1)} %bitcast.9, bf16[2,256,512]{2,1,0:T(8,128)(2,1)S(1)} %collective-permute-done.10.theirs, f32[2,2,512,512]{3,2,1,0:T(8,128)} %write_rows.2.rest_0_), custom_call_target="tpu_custom_call", output_to_operand_aliasing={{}: (3, {})} | custom-call | tf_op jit(solution)/shard_map/write_rows/pallas_call | solution.py:480
  (14 shorter events, 0.3 us)
Async XLA Ops:
  1.7 14.2 %collective-permute-start = (bf16[2,1,256,512]{3,2,1,0:T(8,128)(2,1)S(1)}, bf16[2,1,256,512]{3,2,1,0:T(8,128)(2,1)S(1)}, u32[]{:S(2)}, u32[]{:S(2)}) collective-permute-start(bf16[2,1,256,512]{3,2,1,0:T(8,128)(2,1)S(1)} %constant_dynamic-slice_fusion), channel_id=1, source_target_pairs={{4,0},{8,4},{12,8},{16,12},{20,16},{24,20},{28,24},{5,1},{9,5},{13... | collective-permute-start | bytes 1572872 | tf_op jit(solution)/shard_map/ppermute | solution.py:503
  15.9 2.5 %copy-start.2 = (bf16[2,1,256,512]{3,2,1,0:T(8,128)(2,1)}, bf16[2,1,256,512]{3,2,1,0:T(8,128)(2,1)S(1)}, u32[]{:S(2)}) copy-start(bf16[2,1,256,512]{3,2,1,0:T(8,128)(2,1)S(1)} %collective-permute-done.rim_own_any) | copy-start | bytes 1572868
  15.9 2.5 %collective-permute-start.1 = (bf16[2,1,256,512]{3,2,1,0:T(8,128)(2,1)S(1)}, bf16[2,1,256,512]{3,2,1,0:T(8,128)(2,1)S(1)}, u32[]{:S(2)}, u32[]{:S(2)}) collective-permute-start(bf16[2,1,256,512]{3,2,1,0:T(8,128)(2,1)S(1)} %collective-permute-done.rim_own_any), channel_id=1, source_target_pairs={{0,1},{1,0},{2,3},{3,2},{4,5},{5,4},{6,7},{7,6},{8,9},{9,8},{10,11... | collective-permute-start | bytes 1572872 | tf_op jit(solution)/shard_map/ppermute | solution.py:497
  18.5 0.8 copy-start.3
  27.3 6.8 %collective-permute-start.2 = (bf16[2,512,512]{2,1,0:T(8,128)(2,1)}, bf16[2,512,512]{2,1,0:T(8,128)(2,1)S(1)}, u32[]{:S(2)}, u32[]{:S(2)}) collective-permute-start(bf16[2,512,512]{2,1,0:T(8,128)(2,1)} %get-tuple-element.23), channel_id=1, source_target_pairs={{0,1},{1,0},{2,3},{3,2},{4,5},{5,4},{6,7},{7,6},{8,9},{9,8},{10,11... | collective-permute-start | bytes 3145736 | tf_op jit(solution)/shard_map/ppermute | solution.py:497
  34.1 2.0 %copy-start.5 = (bf16[640,512]{1,0:T(8,128)(2,1)S(1)}, bf16[640,512]{1,0:T(8,128)(2,1)}, u32[]{:S(2)}) copy-start(bf16[640,512]{1,0:T(8,128)(2,1)} %get-tuple-element.26) | copy-start | bytes 1966084
  36.1 2.2 %copy-start.4 = (f32[256,256]{1,0:T(8,128)S(1)}, f32[256,256]{1,0:T(8,128)}, u32[]{:S(2)}) copy-start(f32[256,256]{1,0:T(8,128)} %get-tuple-element.27) | copy-start | bytes 786436
  36.1 27.2 %copy-start.1 = (f32[2,256,512]{2,1,0:T(8,128)S(1)}, f32[2,256,512]{2,1,0:T(8,128)}, u32[]{:S(2)}) copy-start(f32[2,256,512]{2,1,0:T(8,128)} %get-tuple-element.25) | copy-start | bytes 3145732
  36.1 2.2 %collective-permute-start.4 = (bf16[640,512]{1,0:T(8,128)(2,1)S(1)}, bf16[640,512]{1,0:T(8,128)(2,1)S(1)}, u32[]{:S(2)}, u32[]{:S(2)}) collective-permute-start(bf16[640,512]{1,0:T(8,128)(2,1)S(1)} %copy-done.5), channel_id=1, source_target_pairs={{0,1},{1,0},{2,3},{3,2},{4,5},{5,4},{6,7},{7,6},{8,9},{9,8},{10,11... | collective-permute-start | bytes 1966088 | tf_op jit(solution)/shard_map/ppermute | solution.py:497
  36.7 26.6 %collective-permute-start.5 = (bf16[2,256,512]{2,1,0:T(8,128)(2,1)S(1)}, bf16[2,256,512]{2,1,0:T(8,128)(2,1)S(1)}, u32[]{:S(2)}, u32[]{:S(2)}) collective-permute-start(bf16[2,256,512]{2,1,0:T(8,128)(2,1)S(1)} %get-tuple-element.32), channel_id=1, source_target_pairs={{0,4},{4,8},{8,12},{12,16},{16,20},{20,24},{24,28},{1,5},{5,9},{9,... | collective-permute-start | bytes 1572872 | tf_op jit(solution)/shard_map/ppermute | solution.py:503
  38.3 24.8 %collective-permute-start.6 = (bf16[256,256]{1,0:T(8,128)(2,1)S(1)}, bf16[256,256]{1,0:T(8,128)(2,1)S(1)}, u32[]{:S(2)}, u32[]{:S(2)}) collective-permute-start(bf16[256,256]{1,0:T(8,128)(2,1)S(1)} %add_convert_fusion.6), channel_id=1, source_target_pairs={{0,8},{4,12},{8,0},{12,4},{16,24},{20,28},{24,16},{28,20},{1,9},{5... | collective-permute-start | bytes 393224 | tf_op jit(solution)/shard_map/ppermute | solution.py:497
  48.7 22.7 %collective-permute-start.3 = (bf16[2,256,512]{2,1,0:T(8,128)(2,1)S(1)}, bf16[2,256,512]{2,1,0:T(8,128)(2,1)S(1)}, u32[]{:S(2)}, u32[]{:S(2)}) collective-permute-start(bf16[2,256,512]{2,1,0:T(8,128)(2,1)S(1)} %get-tuple-element.33), channel_id=1, source_target_pairs={{0,2},{1,3},{2,0},{3,1},{4,6},{5,7},{6,4},{7,5},{8,10},{9,11},{10,... | collective-permute-start | bytes 1572872 | tf_op jit(solution)/shard_map/ppermute | solution.py:497
  63.2 8.1 %collective-permute-start.7 = (bf16[256,256]{1,0:T(8,128)(2,1)S(1)}, bf16[256,256]{1,0:T(8,128)(2,1)S(1)}, u32[]{:S(2)}, u32[]{:S(2)}) collective-permute-start(bf16[256,256]{1,0:T(8,128)(2,1)S(1)} %add_convert_fusion.5), channel_id=1, source_target_pairs={{0,16},{4,20},{8,24},{12,28},{16,0},{20,4},{24,8},{28,12},{1,17},{... | collective-permute-start | bytes 393224 | tf_op jit(solution)/shard_map/ppermute | solution.py:497
  63.6 10.2 %copy-start = (s32[3]{0:T(128)S(1)}, s32[3]{0:T(128)}, u32[]{:S(2)}) copy-start(s32[3]{0:T(128)} %pad_add_fusion.meta) | copy-start | bytes 40
  71.4 15.8 %collective-permute-start.8 = (bf16[640,512]{1,0:T(8,128)(2,1)S(1)}, bf16[640,512]{1,0:T(8,128)(2,1)S(1)}, u32[]{:S(2)}, u32[]{:S(2)}) collective-permute-start(bf16[640,512]{1,0:T(8,128)(2,1)S(1)} %maximum_maximum_fusion), channel_id=1, source_target_pairs={{0,2},{1,3},{2,0},{3,1},{4,6},{5,7},{6,4},{7,5},{8,10},{9,11},{10,... | collective-permute-start | bytes 1966088 | tf_op jit(solution)/shard_map/ppermute | solution.py:497
  71.7 2.1 %collective-permute-start.9 = (bf16[2,256,512]{2,1,0:T(8,128)(2,1)S(1)}, bf16[2,256,512]{2,1,0:T(8,128)(2,1)S(1)}, u32[]{:S(2)}, u32[]{:S(2)}) collective-permute-start(bf16[2,256,512]{2,1,0:T(8,128)(2,1)S(1)} %add_convert_fusion.2.own), channel_id=1, source_target_pairs={{0,1},{1,0},{2,3},{3,2},{4,5},{5,4},{6,7},{7,6},{8,9},{9,8},{10,11... | collective-permute-start | bytes 1572872 | tf_op jit(solution)/shard_map/ppermute | solution.py:497
  87.5 3.9 %collective-permute-start.11 = (bf16[256,256]{1,0:T(8,128)(2,1)S(1)}, bf16[256,256]{1,0:T(8,128)(2,1)S(1)}, u32[]{:S(2)}, u32[]{:S(2)}) collective-permute-start(bf16[256,256]{1,0:T(8,128)(2,1)S(1)} %pad_maximum_fusion), channel_id=1, source_target_pairs={{0,4},{4,0},{8,12},{12,8},{16,20},{20,16},{24,28},{28,24},{1,5},{5... | collective-permute-start | bytes 393224 | tf_op jit(solution)/shard_map/ppermute | solution.py:497
  87.6 8.2 %collective-permute-start.10 = (bf16[2,256,512]{2,1,0:T(8,128)(2,1)S(1)}, bf16[2,256,512]{2,1,0:T(8,128)(2,1)S(1)}, u32[]{:S(2)}, u32[]{:S(2)}) collective-permute-start(bf16[2,256,512]{2,1,0:T(8,128)(2,1)S(1)} %bitcast.8), channel_id=1, source_target_pairs={{0,1},{1,0},{2,3},{3,2},{4,5},{5,4},{6,7},{7,6},{8,9},{9,8},{10,11... | collective-permute-start | bytes 1572872 | tf_op jit(solution)/shard_map/ppermute | solution.py:497
  91.4 3.6 %collective-permute-start.12 = (bf16[256,256]{1,0:T(8,128)(2,1)S(1)}, bf16[256,256]{1,0:T(8,128)(2,1)S(1)}, u32[]{:S(2)}, u32[]{:S(2)}) collective-permute-start(bf16[256,256]{1,0:T(8,128)(2,1)S(1)} %add_convert_fusion.3), channel_id=1, source_target_pairs={{0,1},{1,0},{2,3},{3,2},{4,5},{5,4},{6,7},{7,6},{8,9},{9,8},{10,11... | collective-permute-start | bytes 393224 | tf_op jit(solution)/shard_map/ppermute | solution.py:497

commit v5 on v3

--- a/solution.py
+++ b/solution.py
@@ -24,14 +24,20 @@
     centred = np.where(index < edge // 2, index, index - edge)
     ramp = np.exp(-1j * (PROP_COEF * math.pi / edge) * centred * centred)
     spread = (np.conj(forward) * ramp[None, :]) @ forward
-
-    def left_form(matrix):
-        return np.block([[matrix.real, -matrix.imag], [matrix.imag, matrix.real]])
-
-    tables = []
-    for matrix in (spread, forward):
-        tables += [left_form(matrix), left_form(matrix).T]
-    return [jnp.asarray(table.astype(ml_dtypes.bfloat16)) for table in tables]
+    planes = [
+        plane for matrix in (spread, forward) for plane in (matrix.real, matrix.imag, -matrix.imag)
+    ]
+    return jnp.asarray(np.stack(planes).astype(ml_dtypes.bfloat16))
+
+
+def lay_tables(planes, tables):
+    edge = planes.shape[1]
+    lo, hi = pl.ds(0, edge), pl.ds(edge, edge)
+    for k in range(2):
+        real, imag, negated = (planes[3 * k + i] for i in range(3))
+        left, right = tables[2 * k : 2 * k + 2]
+        left[lo, lo], left[lo, hi], left[hi, lo], left[hi, hi] = real, negated, imag, real
+        right[lo, lo], right[lo, hi], right[hi, lo], right[hi, hi] = real, imag, negated, real
 
 
 def interleaved(first, second):
@@ -236,13 +242,10 @@
 def early_kernel(
     meta,
     anchor,
-    probe_hbm,
-    spec_hbm,
-    amp_hbm,
-    la_hbm,
-    ra_hbm,
-    lf_hbm,
-    rf_hbm,
+    probe_any,
+    spec_any,
+    amp_any,
+    planes_any,
     acc,
     probe_acc,
     order,
@@ -250,6 +253,7 @@
     probe,
     spec,
     amp,
+    planes,
     la,
     ra,
     lf,
@@ -259,16 +263,14 @@
 ):
     wait = fetch(
         [
-            ("spec", spec_hbm, spec),
-            ("rest", probe_hbm, probe),
-            ("rest", la_hbm, la),
-            ("rest", ra_hbm, ra),
-            ("rest", lf_hbm, lf),
-            ("rest", rf_hbm, rf),
-            ("rest", amp_hbm, amp),
+            ("spec", spec_any, spec),
+            ("planes", planes_any, planes),
+            ("rest", probe_any, probe),
+            ("rest", amp_any, amp),
         ],
         sems,
     )
+    tables = (la, ra, lf, rf)
     slices, tile_rows = spec.shape[1:3]
     for part in range(2):
         for s in range(slices):
@@ -280,25 +282,24 @@
     for part in range(2):
         for s in range(slices):
             widen(wide, spec, 0, part, s, s)
+    wait("planes")
+    lay_tables(planes, tables)
     wait("rest")
-    refs = (anchor, probe, amp, (la, ra, lf, rf), wide, acc, probe_acc)
+    refs = (anchor, probe, amp, tables, wide, acc, probe_acc)
     run_pairs(order, total, meta[1], refs, (work[:5], work[5:]))
 
 
 def late_kernel(
     meta,
     anchor,
-    probe_hbm,
-    spec_hbm,
+    probe_any,
+    spec_any,
     rim_own_any,
     rim_other_any,
     acc_any,
     probe_acc_any,
-    amp_hbm,
-    la_hbm,
-    ra_hbm,
-    lf_hbm,
-    rf_hbm,
+    amp_any,
+    planes_any,
     send_low,
     send_top,
     keep_low,
@@ -309,6 +310,7 @@
     probe,
     spec,
     amp,
+    planes,
     la,
     ra,
     lf,
@@ -324,20 +326,18 @@
     edge = probe.shape[1]
     wait = fetch(
         [
-            ("spec", spec_hbm, spec),
+            ("spec", spec_any, spec),
+            ("planes", planes_any, planes),
             ("rim", rim_own_any, rim_own),
             ("rim", rim_other_any, rim_other),
             ("acc", acc_any, acc.at[:, :, :, pl.ds(0, tile_rows), :]),
             ("acc", probe_acc_any, probe_acc),
-            ("rest", probe_hbm, probe),
-            ("rest", la_hbm, la),
-            ("rest", ra_hbm, ra),
-            ("rest", lf_hbm, lf),
-            ("rest", rf_hbm, rf),
-            ("rest", amp_hbm, amp),
+            ("rest", probe_any, probe),
+            ("rest", amp_any, amp),
         ],
         sems,
     )
+    tables = (la, ra, lf, rf)
     half = meta[2]
     other = 1 - half
     col_tiles = width // LANES
@@ -350,13 +350,15 @@
     for part in range(2):
         for s in range(slices):
             widen(wide, spec, 0, part, s, s)
+    wait("planes")
+    lay_tables(planes, tables)
     wait("rim")
     for part in range(2):
         widen(wide, rim_own, tile_rows, part, 0, half)
         widen(wide, rim_other, tile_rows, part, 0, other)
     wait("acc")
     wait("rest")
-    refs = (anchor, probe, amp, (la, ra, lf, rf), wide, acc, probe_acc)
+    refs = (anchor, probe, amp, tables, wide, acc, probe_acc)
     run_pairs(order, total, meta[1], refs, (work[:5], work[5:]))
 
     low = pl.ds(edge, tile_rows)
@@ -365,25 +367,24 @@
         sign = 1.0 if part == 0 else -1.0
         for t in range(col_tiles):
             cols = pl.ds(t * LANES, LANES)
-            send_low[part, :, cols] = (sign * acc[part, other, t, low, :]).astype(jnp.bfloat16)
+            send_low[pl.ds(part * tile_rows, tile_rows), cols] = (
+                sign * acc[part, other, t, low, :]
+            ).astype(jnp.bfloat16)
             keep_low[part, :, cols] = sign * acc[part, half, t, low, :]
-            send_top[pl.ds(part * edge, edge), cols] = (sign * acc[part, other, t, top, :]).astype(
-                jnp.bfloat16
-            )
+            send_top[part, :, cols] = (sign * acc[part, other, t, top, :]).astype(jnp.bfloat16)
             keep_top[part, :, cols] = sign * acc[part, half, t, top, :]
-    side = width // edge
-    deep = edge // side
+    deep = keep_probe.shape[0]
     flip = jnp.where(other == 1, -1.0, 1.0)
-    for piece in range(side):
-        send_top[pl.ds(2 * edge, deep), pl.ds(piece * edge, edge)] = (
-            flip * probe_acc[other, pl.ds(piece * deep, deep), :]
-        ).astype(jnp.bfloat16)
-    keep_probe[...] = -flip * probe_acc[half]
+    for piece in range(width // edge):
+        rows, cols = pl.ds(piece * deep, deep), pl.ds(piece * edge, edge)
+        send_low[pl.ds(2 * tile_rows, deep), cols] = (flip * probe_acc[other, rows, :]).astype(
+            jnp.bfloat16
+        )
+        keep_probe[:, cols] = -flip * probe_acc[half, rows, :]
 
 
 VMEM = pl.BlockSpec(memory_space=pltpu.VMEM)
 SMEM = pl.BlockSpec(memory_space=pltpu.SMEM)
-HBM = pl.BlockSpec(memory_space=pltpu.HBM)
 ANY = pl.BlockSpec(memory_space=pl.ANY)
 
 
@@ -398,6 +399,7 @@
         planes,
         pltpu.VMEM((2, slices, tile_rows, width), jnp.bfloat16),
         pltpu.VMEM((slots, edge, edge), jnp.bfloat16),
+        pltpu.VMEM((6, edge, edge), jnp.bfloat16),
         table,
         table,
         table,
@@ -407,41 +409,41 @@
     return lead, [planes, planes, planes, stack, joined] * 2
 
 
-def run_early(meta, anchor, probe, spec, amp, tables):
+def run_early(meta, anchor, probe, spec, amp, planes):
     edge = probe.shape[1]
     _, slices, tile_rows, width = spec.shape
-    lead, work = scratch(anchor.shape[0], slices, width, tile_rows, tile_rows, edge, 7)
+    lead, work = scratch(anchor.shape[0], slices, width, tile_rows, tile_rows, edge, 4)
     return pl.pallas_call(
         early_kernel,
         out_shape=(
             jax.ShapeDtypeStruct((2, slices, width // LANES, tile_rows, LANES), jnp.float32),
             jax.ShapeDtypeStruct((2, edge, edge), jnp.float32),
         ),
-        in_specs=[SMEM, SMEM] + [HBM] * 7,
+        in_specs=[SMEM, SMEM] + [ANY] * 4,
         out_specs=(VMEM, VMEM),
         scratch_shapes=lead + work,
         compiler_params=pltpu.CompilerParams(vmem_limit_bytes=32 * 1024 * 1024),
         name="early_slots",
-    )(meta, anchor, probe, spec, amp, *tables)
-
-
-def run_late(meta, anchor, probe, spec, rim_own, rim_other, acc, probe_acc, amp, tables):
+    )(meta, anchor, probe, spec, amp, planes)
+
+
+def run_late(meta, anchor, probe, spec, rim_own, rim_other, acc, probe_acc, amp, planes):
     edge = probe.shape[1]
     _, slices, tile_rows, width = spec.shape
     total = tile_rows + edge
-    side = width // edge
-    lead, work = scratch(anchor.shape[0], slices, width, tile_rows, total, edge, 11)
+    deep = edge * edge // width
+    lead, work = scratch(anchor.shape[0], slices, width, tile_rows, total, edge, 8)
     rim = pltpu.VMEM((2, 1, edge, width), jnp.bfloat16)
     return pl.pallas_call(
         late_kernel,
         out_shape=(
-            jax.ShapeDtypeStruct((2, tile_rows, width), jnp.bfloat16),
-            jax.ShapeDtypeStruct((2 * edge + edge // side, width), jnp.bfloat16),
+            jax.ShapeDtypeStruct((2 * tile_rows + deep, width), jnp.bfloat16),
+            jax.ShapeDtypeStruct((2, edge, width), jnp.bfloat16),
             jax.ShapeDtypeStruct((2, tile_rows, width), jnp.float32),
             jax.ShapeDtypeStruct((2, edge, width), jnp.float32),
-            jax.ShapeDtypeStruct((edge, edge), jnp.float32),
+            jax.ShapeDtypeStruct((deep, width), jnp.float32),
         ),
-        in_specs=[SMEM, SMEM, HBM, HBM] + [ANY] * 4 + [HBM] * 5,
+        in_specs=[SMEM, SMEM] + [ANY] * 8,
         out_specs=(VMEM,) * 5,
         scratch_shapes=lead
         + [
@@ -453,7 +455,7 @@
         + work,
         compiler_params=pltpu.CompilerParams(vmem_limit_bytes=36 * 1024 * 1024),
         name="late_slots",
-    )(meta, anchor, probe, spec, rim_own, rim_other, acc, probe_acc, amp, *tables)
+    )(meta, anchor, probe, spec, rim_own, rim_other, acc, probe_acc, amp, planes)
 
 
 def write_rows(meta, own, theirs, start, shape, base=None):
@@ -480,8 +482,8 @@
     return pl.pallas_call(
         kernel,
         out_shape=jax.ShapeDtypeStruct(shape, jnp.float32),
-        in_specs=[SMEM, VMEM, VMEM] + [HBM] * len(extra),
-        out_specs=HBM,
+        in_specs=[SMEM, VMEM, VMEM] + [ANY] * len(extra),
+        out_specs=ANY,
         input_output_aliases={} if base is None else {3: 0},
         scratch_shapes=[
             pltpu.VMEM((slices, 2, rows, width), jnp.float32),
@@ -507,18 +509,21 @@
     return (own.astype(jnp.float32) + got.astype(jnp.float32)).astype(jnp.bfloat16)
 
 
+def unfolded(value, edge):
+    return jnp.concatenate([value[:, k : k + edge] for k in range(0, value.shape[1], edge)], 0)
+
+
 def body(probe_field, specimen, amplitude, scan_anchor, counts):
     edge = probe_field.shape[1]
     _, slices, tile_rows, width = specimen.shape
-    side = width // edge
     half = lax.axis_index("pos") % 2
     base_row = lax.axis_index("tile") * tile_rows
     meta = jnp.stack([counts[0], base_row, half]).astype(jnp.int32)
-    tables = fixed_tables(edge)
+    planes = fixed_tables(edge)
     rim_own = passed_along(
         lax.dynamic_slice(specimen, (0, half, 0, 0), (2, 1, edge, width)), "tile", -1
     )
-    acc, probe_acc = run_early(meta, scan_anchor, probe_field, specimen, amplitude, tables)
+    acc, probe_acc = run_early(meta, scan_anchor, probe_field, specimen, amplitude, planes)
     rim_own, probe_acc = lax.optimization_barrier((rim_own, probe_acc))
     rim_other = traded(rim_own, "pos", 1)
     sent_low, sent_top, kept_low, kept_top, kept_probe = run_late(
@@ -531,43 +536,40 @@
         acc,
         probe_acc,
         amplitude,
-        tables,
+        planes,
     )
     got_low = traded(sent_low, "pos", 1)
     got_top = traded(sent_top, "pos", 1)
-    low = (kept_low + got_low.astype(jnp.float32)).astype(jnp.bfloat16)
-    got_top, low = lax.optimization_barrier((got_top, low))
-    lower = low[:, : tile_rows - edge]
-    lower_got = traded(lower, "pos", 2)
+    low = kept_low + got_low[: 2 * tile_rows].reshape(kept_low.shape).astype(jnp.float32)
+    low = low.astype(jnp.bfloat16)
+    probe_part = (kept_probe + got_low[2 * tile_rows :].astype(jnp.float32)).astype(jnp.bfloat16)
     below = passed_along(low[:, tile_rows - edge :], "tile", 1)
-    top = kept_top + got_top[: 2 * edge].reshape(2, edge, width).astype(jnp.float32)
-    got_probe = jnp.concatenate(
-        [got_top[2 * edge :, p * edge : (p + 1) * edge] for p in range(side)], 0
+    mid_rows = 2 * (tile_rows - edge)
+    mid = jnp.concatenate([low[:, : tile_rows - edge].reshape(mid_rows, width), probe_part], 0)
+    mid = narrow_sum(mid, traded(mid, "pos", 2))
+    top = kept_top + got_top.astype(jnp.float32)
+    upper = (top + below.astype(jnp.float32)).astype(jnp.bfloat16)
+    mid, upper = lax.optimization_barrier((mid, upper))
+    upper_got = traded(upper, "pos", 2)
+    probe_part = mid[mid_rows:]
+    distance = lax.axis_size("tile")
+    while distance > 2:
+        distance //= 2
+        probe_part = narrow_sum(probe_part, traded(probe_part, "tile", distance))
+    lower = mid[:mid_rows].reshape(2, tile_rows - edge, width)
+    tile_grad = write_rows(meta, lower, traded(lower, "pos", 1), edge, specimen.shape)
+    upper_got, tile_grad, probe_part = lax.optimization_barrier(
+        (upper_got, tile_grad, probe_part)
     )
-    probe_part = (kept_probe + got_probe.astype(jnp.float32)).astype(jnp.bfloat16)
-    probe_part = narrow_sum(probe_part, traded(probe_part, "pos", 2))
     probe_part = narrow_sum(probe_part, traded(probe_part, "tile", 1))
-    below, probe_part = lax.optimization_barrier((below, probe_part))
-    upper = (top + below.astype(jnp.float32)).astype(jnp.bfloat16)
-    lower_got, upper = lax.optimization_barrier((lower_got, upper))
-    upper_got = traded(upper, "pos", 2)
-    distance = 2
-    while distance < lax.axis_size("tile"):
-        probe_part = narrow_sum(probe_part, traded(probe_part, "tile", distance))
-        distance *= 2
-    lower = narrow_sum(lower, lower_got)
-    lower_theirs = traded(lower, "pos", 1)
-    tile_grad = write_rows(meta, lower, lower_theirs, edge, specimen.shape)
-    probe_theirs = traded(probe_part, "pos", 1)
+    upper = narrow_sum(upper, upper_got)
+    tile_grad = write_rows(meta, upper, traded(upper, "pos", 1), 0, specimen.shape, tile_grad)
+    probe_own, probe_theirs = [
+        unfolded(value, edge) for value in (probe_part, traded(probe_part, "pos", 1))
+    ]
     probe_total = jnp.where(
-        half == 0, jnp.stack([probe_part, probe_theirs]), jnp.stack([probe_theirs, probe_part])
+        half == 0, jnp.stack([probe_own, probe_theirs]), jnp.stack([probe_theirs, probe_own])
     ).astype(jnp.float32)
-    upper_got, tile_grad, probe_total = lax.optimization_barrier(
-        (upper_got, tile_grad, probe_total)
-    )
-    upper = narrow_sum(upper, upper_got)
-    upper_theirs = traded(upper, "pos", 1)
-    tile_grad = write_rows(meta, upper, upper_theirs, 0, specimen.shape, tile_grad)
     return (tile_grad, probe_total)
 
 

time: 86.8 us -> 84.1 us (0.969); the launches traced: 88.3 us -> 83.5 us
  starting transfers between devices: 28.5 us -> 15.5 us
  Pallas kernels: 16.1 us -> 23.9 us
  waiting for transfers between devices: 30.3 us -> 34.7 us
  local copies, waits for them, and re-layouts: 9.99 us -> 5.91 us
    ppermute x12 -> x11, starting transfers between devices: 25.9 us -> 12.9 us  [traded(): return lax.ppermute(value, axis, [(i, i ^ distance) for i in range(count)])]
    unnamed x23 -> x13, local copies, waits for them, and re-layouts: 8.79 us -> 4.53 us
    pallas_call x1, Pallas kernels: 5.45 us -> 9.34 us  [run_early(): pl.pallas_call(early_kernel, out_shape=(jax.ShapeDtypeStruct((2, slices,...]
    pallas_call x1, Pallas kernels: 6.62 us -> 10.5 us  [run_late(): pl.pallas_call(late_kernel, out_shape=(jax.ShapeDtypeStruct((2 * tile_row...]
    ppermute x2, waiting for transfers between devices: 0.48 us -> 3.74 us  [passed_along(): lax.ppermute(value, axis, [(source, source + steps) for source in range(i...]
    ppermute x12 -> x11, waiting for transfers between devices: 29.8 us -> 31 us  [traded(): return lax.ppermute(value, axis, [(i, i ^ distance) for i in range(count)])]
  transfers between devices with their start and end apart: 14 -> 13, of which waited for: 11 -> 10; matrix products, arithmetic and copies ran while one was open for 3% -> 3% of each run, Pallas kernels for 8% -> 14%
where the time goes in v5:
time: 84.1 us; the launch traced here: 83.5 us
  waiting for transfers between devices  34.7 us (41%)
  Pallas kernels  23.9 us (28%)
  starting transfers between devices  15.5 us (18%)
  local copies, waits for them, and re-layouts  5.91 us (7%)
  other arithmetic  1.98 us (2%)
  between operations  1.51 us (2%)
    ppermute x11, waiting for transfers between devices, traded(): return lax.ppermute(value, axis, [(i, i ^ distance) for i in range(count)])  31 us
    ppermute x11, starting transfers between devices, traded(): return lax.ppermute(value, axis, [(i, i ^ distance) for i in range(count)])  12.9 us
    pallas_call x1, Pallas kernels, run_late(): pl.pallas_call(late_kernel, out_shape=(jax.ShapeDtypeStruct((2 * tile_row...  10.5 us
    pallas_call x1, Pallas kernels, run_early(): pl.pallas_call(early_kernel, out_shape=(jax.ShapeDtypeStruct((2, slices,...  9.34 us
    unnamed x13, local copies, waits for them, and re-layouts  4.53 us
    pallas_call x2, Pallas kernels, write_rows(): pl.pallas_call(kernel, out_shape=jax.ShapeDtypeStruct(shape, jnp.float32)...  4.05 us
    ppermute x2, waiting for transfers between devices, passed_along(): lax.ppermute(value, axis, [(source, source + steps) for source in range(i...  3.74 us
    ppermute x2, starting transfers between devices, passed_along(): lax.ppermute(value, axis, [(source, source + steps) for source in range(i...  2.61 us
  transfers between devices with their start and end apart: 13, of which 10 were waited for; matrix products, arithmetic and copies ran while one was open for 3% of the time, Pallas kernels for 14%

profile of v5, /device:TPU:0, one launch (start us, length us, event | category | flops | bytes accessed | tf_op | source)
XLA Modules:
  0.0 83.5 jit_solution(10650513761626244832)
XLA Ops:
  0.6 0.0 copy-start.2
  0.7 1.2 %constant_dynamic-slice_fusion = bf16[2,1,256,512]{3,2,1,0:T(8,128)(2,1)S(1)} fusion(bf16[2,2,512,512]{3,2,1,0:T(8,128)(2,1)} %spec_any.3, s32[]{:T(128)S(6)} %select_n.19), kind=kLoop, calls=%fused_computation.15 | loop fusion | bytes 1048580 | tf_op jit(solution)/shard_map/dynamic_slice | solution.py:524
  1.8 1.3 %collective-permute-start = (bf16[2,1,256,512]{3,2,1,0:T(8,128)(2,1)S(1)}, bf16[2,1,256,512]{3,2,1,0:T(8,128)(2,1)S(1)}, u32[]{:S(2)}, u32[]{:S(2)}) collective-permute-start(bf16[2,1,256,512]{3,2,1,0:T(8,128)(2,1)S(1)} %constant_dynamic-slice_fusion), channel_id=1, source_target_pairs={{4,0},{8,4},{12,8},{16,12},{20,16},{24,20},{28,24},{5,1},{9,5},{13... | collective-permute-start | bytes 1572872 | tf_op jit(solution)/shard_map/ppermute | solution.py:505
  3.8 0.8 copy.10.anchor
  4.5 0.1 pad_add_fusion.meta
  4.6 0.0 copy-done.2
  4.6 1.6 %copy-done = bf16[2,2,512,512]{3,2,1,0:T(8,128)(2,1)S(1)} copy-done((bf16[2,2,512,512]{3,2,1,0:T(8,128)(2,1)S(1)}, bf16[2,2,512,512]{3,2,1,0:T(8,128)(2,1)}, u32[]{:S(2)}) %copy-start) | copy-done | bytes 2097176
  6.2 0.0 copy-start.3
  6.2 1.1 %copy-done.3 = bf16[6,256,256]{2,1,0:T(8,128)(2,1)S(1)} copy-done((bf16[6,256,256]{2,1,0:T(8,128)(2,1)S(1)}, bf16[6,256,256]{2,1,0:T(8,128)(2,1)}, u32[]{:S(2)}) %copy-start.3) | copy-done | bytes 786456
  7.3 1.0 %copy-done.4 = f32[2,256,256]{2,1,0:T(8,128)S(1)} copy-done((f32[2,256,256]{2,1,0:T(8,128)S(1)}, f32[2,256,256]{2,1,0:T(8,128)}, u32[]{:S(2)}) %copy-start.4) | copy-done | bytes 524312
  8.4 9.3 %early_slots.1 = (f32[2,2,4,512,128]{4,3,2,1,0:T(8,128)S(1)}, f32[2,256,256]{2,1,0:T(8,128)S(1)}) custom-call(s32[3]{0:T(128)S(1)} %pad_add_fusion.meta, s32[8,2]{1,0:T(8,128)S(1)} %copy.10.anchor, f32[2,256,256]{2,1,0:T(8,128)S(1)} %copy-done.4, bf16[2,2,512,512]{3,2,1,0:T(8,128)(2,1)S(1)} %copy-done, bf16[8,256,256]{2,1,0:T(8,128)(2,1)S(1)} %copy-done.2, ...), custom_call_target="tpu_custom_call" | custom-call | tf_op jit(solution)/shard_map/early_slots/pallas_call | solution.py:416
  17.7 0.9 %collective-permute-done.rim_own_any = bf16[2,1,256,512]{3,2,1,0:T(8,128)(2,1)S(1)} collective-permute-done((bf16[2,1,256,512]{3,2,1,0:T(8,128)(2,1)S(1)}, bf16[2,1,256,512]{3,2,1,0:T(8,128)(2,1)S(1)}, u32[]{:S(2)}, u32[]{:S(2)}) %collective-permute-start) | collective-permute-done | bytes 524320 | tf_op jit(solution)/shard_map/ppermute | solution.py:505
  18.6 0.0 collective-permute-start.1
  18.6 1.9 %collective-permute-done.1.rim_other_any = bf16[2,1,256,512]{3,2,1,0:T(8,128)(2,1)S(1)} collective-permute-done((bf16[2,1,256,512]{3,2,1,0:T(8,128)(2,1)S(1)}, bf16[2,1,256,512]{3,2,1,0:T(8,128)(2,1)S(1)}, u32[]{:S(2)}, u32[]{:S(2)}) %collective-permute-start.1) | collective-permute-done | bytes 524320 | tf_op jit(solution)/shard_map/ppermute | solution.py:499
  20.5 0.0 copy-done.1
  20.5 0.0 copy-done.5
  20.5 10.5 %late_slots.1 = (bf16[1152,512]{1,0:T(8,128)(2,1)S(1)}, bf16[2,256,512]{2,1,0:T(8,128)(2,1)S(1)}, f32[2,512,512]{2,1,0:T(8,128)S(1)}, f32[2,256,512]{2,1,0:T(8,128)S(1)}, f32[128,512]{1,0:T(8,128)S(1)}) custom-call(s32[3]{0:T(128)S(1)} %pad_add_fusion.meta, s32[8,2]{1,0:T(8,128)S(1)} %copy.10.anchor, f32[2,256,256]{2,1,0:T(8,128)S(1)} %copy-done.5, ...), custom_call_target="tpu_custom_call" | custom-call | tf_op jit(solution)/shard_map/late_slots/pallas_call | solution.py:437
  31.0 0.2 collective-permute-start.2
  31.2 0.4 collective-permute-start.4
  31.6 2.3 %collective-permute-done.2 = bf16[1152,512]{1,0:T(8,128)(2,1)S(1)} collective-permute-done((bf16[1152,512]{1,0:T(8,128)(2,1)S(1)}, bf16[1152,512]{1,0:T(8,128)(2,1)S(1)}, u32[]{:S(2)}, u32[]{:S(2)}) %collective-permute-start.2) | collective-permute-done | bytes 1179680 | tf_op jit(solution)/shard_map/ppermute | solution.py:499
  33.9 0.1 slice.40
  34.0 0.4 fusion
  34.3 0.1 fusion.2
  34.4 1.3 %collective-permute-start.5 = (bf16[2,256,512]{2,1,0:T(8,128)(2,1)S(1)}, bf16[2,256,512]{2,1,0:T(8,128)(2,1)S(1)}, u32[]{:S(2)}, u32[]{:S(2)}) collective-permute-start(bf16[2,256,512]{2,1,0:T(8,128)(2,1)S(1)} %get-tuple-element.30), channel_id=1, source_target_pairs={{0,4},{4,8},{8,12},{12,16},{16,20},{20,24},{24,28},{1,5},{5,9},{9,... | collective-permute-start | bytes 1572872 | tf_op jit(solution)/shard_map/ppermute | solution.py:505
  35.8 8.7 %collective-permute-start.3 = (bf16[640,512]{1,0:T(8,128)(2,1)S(1)}, bf16[640,512]{1,0:T(8,128)(2,1)S(1)}, u32[]{:S(2)}, u32[]{:S(2)}) collective-permute-start(bf16[640,512]{1,0:T(8,128)(2,1)S(1)} %pad_maximum_fusion), channel_id=1, source_target_pairs={{0,2},{1,3},{2,0},{3,1},{4,6},{5,7},{6,4},{7,5},{8,10},{9,11},{10,... | collective-permute-start | bytes 1966088 | tf_op jit(solution)/shard_map/ppermute | solution.py:499
  44.6 0.0 collective-permute-done.4
  44.6 2.9 %collective-permute-done.5 = bf16[2,256,512]{2,1,0:T(8,128)(2,1)S(1)} collective-permute-done((bf16[2,256,512]{2,1,0:T(8,128)(2,1)S(1)}, bf16[2,256,512]{2,1,0:T(8,128)(2,1)S(1)}, u32[]{:S(2)}, u32[]{:S(2)}) %collective-permute-start.5) | collective-permute-done | bytes 524320 | tf_op jit(solution)/shard_map/ppermute | solution.py:505
  47.5 0.2 add_convert_fusion.2
  47.7 11.6 %collective-permute-done.3 = bf16[640,512]{1,0:T(8,128)(2,1)S(1)} collective-permute-done((bf16[640,512]{1,0:T(8,128)(2,1)S(1)}, bf16[640,512]{1,0:T(8,128)(2,1)S(1)}, u32[]{:S(2)}, u32[]{:S(2)}) %collective-permute-start.3) | collective-permute-done | bytes 655392 | tf_op jit(solution)/shard_map/ppermute | solution.py:499
  59.3 0.2 add_convert_fusion
  59.5 0.1 collective-permute-start.8
  59.7 0.1 collective-permute-start.7
  59.7 1.8 %collective-permute-start.6 = (bf16[2,256,512]{2,1,0:T(8,128)(2,1)S(1)}, bf16[2,256,512]{2,1,0:T(8,128)(2,1)S(1)}, u32[]{:S(2)}, u32[]{:S(2)}) collective-permute-start(bf16[2,256,512]{2,1,0:T(8,128)(2,1)S(1)} %add_convert_fusion.2), channel_id=1, source_target_pairs={{0,2},{1,3},{2,0},{3,1},{4,6},{5,7},{6,4},{7,5},{8,10},{9,11},{10,... | collective-permute-start | bytes 1572872 | tf_op jit(solution)/shard_map/ppermute | solution.py:499
  61.5 3.9 %collective-permute-done.8 = bf16[128,512]{1,0:T(8,128)(2,1)S(1)} collective-permute-done((bf16[128,512]{1,0:T(8,128)(2,1)S(1)}, bf16[128,512]{1,0:T(8,128)(2,1)S(1)}, u32[]{:S(2)}, u32[]{:S(2)}) %collective-permute-start.8) | collective-permute-done | bytes 131104 | tf_op jit(solution)/shard_map/ppermute | solution.py:499
  65.5 0.1 collective-permute-start.9
  65.6 4.9 %collective-permute-done.9 = bf16[128,512]{1,0:T(8,128)(2,1)S(1)} collective-permute-done((bf16[128,512]{1,0:T(8,128)(2,1)S(1)}, bf16[128,512]{1,0:T(8,128)(2,1)S(1)}, u32[]{:S(2)}, u32[]{:S(2)}) %collective-permute-start.9) | collective-permute-done | bytes 131104 | tf_op jit(solution)/shard_map/ppermute | solution.py:499
  70.6 0.0 collective-permute-done.7.theirs
  70.6 2.0 %write_rows.2.rest_0_ = f32[2,2,512,512]{3,2,1,0:T(8,128)} custom-call(s32[3]{0:T(128)S(1)} %pad_add_fusion.meta, bf16[2,256,512]{2,1,0:T(8,128)(2,1)S(1)} %bitcast.11, bf16[2,256,512]{2,1,0:T(8,128)(2,1)S(1)} %collective-permute-done.7.theirs), custom_call_target="tpu_custom_call" | custom-call | tf_op jit(solution)/shard_map/write_rows/pallas_call | solution.py:482
  72.6 1.5 %collective-permute-done.6 = bf16[2,256,512]{2,1,0:T(8,128)(2,1)S(1)} collective-permute-done((bf16[2,256,512]{2,1,0:T(8,128)(2,1)S(1)}, bf16[2,256,512]{2,1,0:T(8,128)(2,1)S(1)}, u32[]{:S(2)}, u32[]{:S(2)}) %collective-permute-start.6) | collective-permute-done | bytes 524320 | tf_op jit(solution)/shard_map/ppermute | solution.py:499
  74.1 1.4 %collective-permute-start.11 = (bf16[128,512]{1,0:T(8,128)(2,1)S(1)}, bf16[128,512]{1,0:T(8,128)(2,1)S(1)}, u32[]{:S(2)}, u32[]{:S(2)}) collective-permute-start(bf16[128,512]{1,0:T(8,128)(2,1)S(1)} %add_convert_fusion.4), channel_id=1, source_target_pairs={{0,4},{4,0},{8,12},{12,8},{16,20},{20,16},{24,28},{28,24},{1,5},{5... | collective-permute-start | bytes 393224 | tf_op jit(solution)/shard_map/ppermute | solution.py:499
  75.5 0.1 add_convert_fusion.1.own
  75.6 0.1 collective-permute-start.10
  75.7 3.4 %collective-permute-done.11 = bf16[128,512]{1,0:T(8,128)(2,1)S(1)} collective-permute-done((bf16[128,512]{1,0:T(8,128)(2,1)S(1)}, bf16[128,512]{1,0:T(8,128)(2,1)S(1)}, u32[]{:S(2)}, u32[]{:S(2)}) %collective-permute-start.11) | collective-permute-done | bytes 131104 | tf_op jit(solution)/shard_map/ppermute | solution.py:499
  79.2 0.1 collective-permute-start.12
  79.3 1.3 %collective-permute-done.12 = bf16[128,512]{1,0:T(8,128)(2,1)S(1)} collective-permute-done((bf16[128,512]{1,0:T(8,128)(2,1)S(1)}, bf16[128,512]{1,0:T(8,128)(2,1)S(1)}, u32[]{:S(2)}, u32[]{:S(2)}) %collective-permute-start.12) | collective-permute-done | bytes 131104 | tf_op jit(solution)/shard_map/ppermute | solution.py:499
  80.6 0.8 fusion.1
  81.5 0.0 collective-permute-done.10.theirs
  81.5 2.0 %write_rows.3 = f32[2,2,512,512]{3,2,1,0:T(8,128)} custom-call(s32[3]{0:T(128)S(1)} %pad_add_fusion.meta, bf16[2,256,512]{2,1,0:T(8,128)(2,1)S(1)} %add_convert_fusion.1.own, bf16[2,256,512]{2,1,0:T(8,128)(2,1)S(1)} %collective-permute-done.10.theirs, f32[2,2,512,512]{3,2,1,0:T(8,128)} %write_rows.2.rest_0_), custom_call_target="tpu_custom_call", output_to_operand_aliasing={{}: (3, {})} | custom-call | tf_op jit(solution)/shard_map/write_rows/pallas_call | solution.py:482
  (14 shorter events, 0.3 us)
Async XLA Ops:
  0.6 4.0 %copy-start.2 = (bf16[8,256,256]{2,1,0:T(8,128)(2,1)S(1)}, bf16[8,256,256]{2,1,0:T(8,128)(2,1)}, u32[]{:S(2)}) copy-start(bf16[8,256,256]{2,1,0:T(8,128)(2,1)} %amp_any.3) | copy-start | bytes 3145732
  1.8 16.8 %collective-permute-start = (bf16[2,1,256,512]{3,2,1,0:T(8,128)(2,1)S(1)}, bf16[2,1,256,512]{3,2,1,0:T(8,128)(2,1)S(1)}, u32[]{:S(2)}, u32[]{:S(2)}) collective-permute-start(bf16[2,1,256,512]{3,2,1,0:T(8,128)(2,1)S(1)} %constant_dynamic-slice_fusion), channel_id=1, source_target_pairs={{4,0},{8,4},{12,8},{16,12},{20,16},{24,20},{28,24},{5,1},{9,5},{13... | collective-permute-start | bytes 1572872 | tf_op jit(solution)/shard_map/ppermute | solution.py:505
  4.6 1.6 %copy-start = (bf16[2,2,512,512]{3,2,1,0:T(8,128)(2,1)S(1)}, bf16[2,2,512,512]{3,2,1,0:T(8,128)(2,1)}, u32[]{:S(2)}) copy-start(bf16[2,2,512,512]{3,2,1,0:T(8,128)(2,1)} %spec_any.3) | copy-start | bytes 6291460
  6.2 1.1 %copy-start.3 = (bf16[6,256,256]{2,1,0:T(8,128)(2,1)S(1)}, bf16[6,256,256]{2,1,0:T(8,128)(2,1)}, u32[]{:S(2)}) copy-start(bf16[6,256,256]{2,1,0:T(8,128)(2,1)} %constant.27.clone.planes_any) | copy-start | bytes 2359300
  7.3 1.0 %copy-start.4 = (f32[2,256,256]{2,1,0:T(8,128)S(1)}, f32[2,256,256]{2,1,0:T(8,128)}, u32[]{:S(2)}) copy-start(f32[2,256,256]{2,1,0:T(8,128)} %probe_any.3) | copy-start | bytes 1572868
  8.4 12.1 %copy-start.1 = (bf16[2,2,512,512]{3,2,1,0:T(8,128)(2,1)S(1)}, bf16[2,2,512,512]{3,2,1,0:T(8,128)(2,1)}, u32[]{:S(2)}) copy-start(bf16[2,2,512,512]{3,2,1,0:T(8,128)(2,1)} %spec_any.3) | copy-start | bytes 6291460
  8.4 12.1 %copy-start.5 = (f32[2,256,256]{2,1,0:T(8,128)S(1)}, f32[2,256,256]{2,1,0:T(8,128)}, u32[]{:S(2)}) copy-start(f32[2,256,256]{2,1,0:T(8,128)} %probe_any.3) | copy-start | bytes 1572868
  18.6 1.9 %collective-permute-start.1 = (bf16[2,1,256,512]{3,2,1,0:T(8,128)(2,1)S(1)}, bf16[2,1,256,512]{3,2,1,0:T(8,128)(2,1)S(1)}, u32[]{:S(2)}, u32[]{:S(2)}) collective-permute-start(bf16[2,1,256,512]{3,2,1,0:T(8,128)(2,1)S(1)} %collective-permute-done.rim_own_any), channel_id=1, source_target_pairs={{0,1},{1,0},{2,3},{3,2},{4,5},{5,4},{6,7},{7,6},{8,9},{9,8},{10,11... | collective-permute-start | bytes 1572872 | tf_op jit(solution)/shard_map/ppermute | solution.py:499
  31.0 2.9 %collective-permute-start.2 = (bf16[1152,512]{1,0:T(8,128)(2,1)S(1)}, bf16[1152,512]{1,0:T(8,128)(2,1)S(1)}, u32[]{:S(2)}, u32[]{:S(2)}) collective-permute-start(bf16[1152,512]{1,0:T(8,128)(2,1)S(1)} %get-tuple-element.21), channel_id=1, source_target_pairs={{0,1},{1,0},{2,3},{3,2},{4,5},{5,4},{6,7},{7,6},{8,9},{9,8},{10,11... | collective-permute-start | bytes 3538952 | tf_op jit(solution)/shard_map/ppermute | solution.py:499
  31.2 13.4 %collective-permute-start.4 = (bf16[2,256,512]{2,1,0:T(8,128)(2,1)S(1)}, bf16[2,256,512]{2,1,0:T(8,128)(2,1)S(1)}, u32[]{:S(2)}, u32[]{:S(2)}) collective-permute-start(bf16[2,256,512]{2,1,0:T(8,128)(2,1)S(1)} %get-tuple-element.24), channel_id=1, source_target_pairs={{0,1},{1,0},{2,3},{3,2},{4,5},{5,4},{6,7},{7,6},{8,9},{9,8},{10,11... | collective-permute-start | bytes 1572872 | tf_op jit(solution)/shard_map/ppermute | solution.py:499
  34.4 13.0 %collective-permute-start.5 = (bf16[2,256,512]{2,1,0:T(8,128)(2,1)S(1)}, bf16[2,256,512]{2,1,0:T(8,128)(2,1)S(1)}, u32[]{:S(2)}, u32[]{:S(2)}) collective-permute-start(bf16[2,256,512]{2,1,0:T(8,128)(2,1)S(1)} %get-tuple-element.30), channel_id=1, source_target_pairs={{0,4},{4,8},{8,12},{12,16},{16,20},{20,24},{24,28},{1,5},{5,9},{9,... | collective-permute-start | bytes 1572872 | tf_op jit(solution)/shard_map/ppermute | solution.py:505
  35.8 23.5 %collective-permute-start.3 = (bf16[640,512]{1,0:T(8,128)(2,1)S(1)}, bf16[640,512]{1,0:T(8,128)(2,1)S(1)}, u32[]{:S(2)}, u32[]{:S(2)}) collective-permute-start(bf16[640,512]{1,0:T(8,128)(2,1)S(1)} %pad_maximum_fusion), channel_id=1, source_target_pairs={{0,2},{1,3},{2,0},{3,1},{4,6},{5,7},{6,4},{7,5},{8,10},{9,11},{10,... | collective-permute-start | bytes 1966088 | tf_op jit(solution)/shard_map/ppermute | solution.py:499
  59.5 5.9 %collective-permute-start.8 = (bf16[128,512]{1,0:T(8,128)(2,1)S(1)}, bf16[128,512]{1,0:T(8,128)(2,1)S(1)}, u32[]{:S(2)}, u32[]{:S(2)}) collective-permute-start(bf16[128,512]{1,0:T(8,128)(2,1)S(1)} %slice.35), channel_id=1, source_target_pairs={{0,16},{4,20},{8,24},{12,28},{16,0},{20,4},{24,8},{28,12},{1,17},{... | collective-permute-start | bytes 393224 | tf_op jit(solution)/shard_map/ppermute | solution.py:499
  59.7 10.9 %collective-permute-start.7 = (bf16[2,256,512]{2,1,0:T(8,128)(2,1)S(1)}, bf16[2,256,512]{2,1,0:T(8,128)(2,1)S(1)}, u32[]{:S(2)}, u32[]{:S(2)}) collective-permute-start(bf16[2,256,512]{2,1,0:T(8,128)(2,1)S(1)} %bitcast.10), channel_id=1, source_target_pairs={{0,1},{1,0},{2,3},{3,2},{4,5},{5,4},{6,7},{7,6},{8,9},{9,8},{10,11... | collective-permute-start | bytes 1572872 | tf_op jit(solution)/shard_map/ppermute | solution.py:499
  59.7 14.3 %collective-permute-start.6 = (bf16[2,256,512]{2,1,0:T(8,128)(2,1)S(1)}, bf16[2,256,512]{2,1,0:T(8,128)(2,1)S(1)}, u32[]{:S(2)}, u32[]{:S(2)}) collective-permute-start(bf16[2,256,512]{2,1,0:T(8,128)(2,1)S(1)} %add_convert_fusion.2), channel_id=1, source_target_pairs={{0,2},{1,3},{2,0},{3,1},{4,6},{5,7},{6,4},{7,5},{8,10},{9,11},{10,... | collective-permute-start | bytes 1572872 | tf_op jit(solution)/shard_map/ppermute | solution.py:499
  65.5 5.0 %collective-permute-start.9 = (bf16[128,512]{1,0:T(8,128)(2,1)S(1)}, bf16[128,512]{1,0:T(8,128)(2,1)S(1)}, u32[]{:S(2)}, u32[]{:S(2)}) collective-permute-start(bf16[128,512]{1,0:T(8,128)(2,1)S(1)} %add_convert_fusion.5), channel_id=1, source_target_pairs={{0,8},{4,12},{8,0},{12,4},{16,24},{20,28},{24,16},{28,20},{1,9},{5... | collective-permute-start | bytes 393224 | tf_op jit(solution)/shard_map/ppermute | solution.py:499
  74.1 5.1 %collective-permute-start.11 = (bf16[128,512]{1,0:T(8,128)(2,1)S(1)}, bf16[128,512]{1,0:T(8,128)(2,1)S(1)}, u32[]{:S(2)}, u32[]{:S(2)}) collective-permute-start(bf16[128,512]{1,0:T(8,128)(2,1)S(1)} %add_convert_fusion.4), channel_id=1, source_target_pairs={{0,4},{4,0},{8,12},{12,8},{16,20},{20,16},{24,28},{28,24},{1,5},{5... | collective-permute-start | bytes 393224 | tf_op jit(solution)/shard_map/ppermute | solution.py:499
  75.6 5.8 %collective-permute-start.10 = (bf16[2,256,512]{2,1,0:T(8,128)(2,1)S(1)}, bf16[2,256,512]{2,1,0:T(8,128)(2,1)S(1)}, u32[]{:S(2)}, u32[]{:S(2)}) collective-permute-start(bf16[2,256,512]{2,1,0:T(8,128)(2,1)S(1)} %add_convert_fusion.1.own), channel_id=1, source_target_pairs={{0,1},{1,0},{2,3},{3,2},{4,5},{5,4},{6,7},{7,6},{8,9},{9,8},{10,11... | collective-permute-start | bytes 1572872 | tf_op jit(solution)/shard_map/ppermute | solution.py:499
  79.2 1.4 %collective-permute-start.12 = (bf16[128,512]{1,0:T(8,128)(2,1)S(1)}, bf16[128,512]{1,0:T(8,128)(2,1)S(1)}, u32[]{:S(2)}, u32[]{:S(2)}) collective-permute-start(bf16[128,512]{1,0:T(8,128)(2,1)S(1)} %add_convert_fusion.3), channel_id=1, source_target_pairs={{0,1},{1,0},{2,3},{3,2},{4,5},{5,4},{6,7},{7,6},{8,9},{9,8},{10,11... | collective-permute-start | bytes 393224 | tf_op jit(solution)/shard_map/ppermute | solution.py:499

commit v6 on v5

--- a/solution.py
+++ b/solution.py
@@ -13,6 +13,8 @@
 AMP_EPS = 0.05
 LANES = 128
 CHUNK = 32
+EARLY_PAIRS = 2
+SHARDS = 4
 
 
 def fixed_tables(edge):
@@ -183,7 +185,7 @@
         jnp.where((q < live) & (anchor[q, 0] - base_row + edge <= tile_rows), 1, 0)
         for q in range(slots)
     ]
-    early = sum(inner) // 2 * 2
+    early = jnp.minimum(sum(inner) // 2, EARLY_PAIRS) * 2
     taken = jnp.int32(0)
     rank = jnp.int32(0)
     order[0] = 0
@@ -490,6 +492,9 @@
             pltpu.SemaphoreType.DMA((2 * slices,)),
         ],
         compiler_params=pltpu.CompilerParams(vmem_limit_bytes=16 * 1024 * 1024),
+        cost_estimate=pl.CostEstimate(
+            flops=0, bytes_accessed=2 * slices * rows * width * 6, transcendentals=0
+        ),
         name="write_rows",
     )(meta, own, theirs, *extra)
 
@@ -511,6 +516,43 @@
 
 def unfolded(value, edge):
     return jnp.concatenate([value[:, k : k + edge] for k in range(0, value.shape[1], edge)], 0)
+
+
+def split_probe(place, whole, first, group):
+    width = whole.shape[1]
+    rows = (whole.shape[0] - first) // group
+
+    def kernel(place, whole, *shares):
+        for d, share in enumerate(shares):
+            start = pl.multiple_of(first + (place[0] ^ d) * rows, rows)
+            share[...] = whole[pl.ds(start, rows), :]
+
+    return pl.pallas_call(
+        kernel,
+        out_shape=(jax.ShapeDtypeStruct((rows, width), jnp.bfloat16),) * group,
+        in_specs=[SMEM, VMEM],
+        out_specs=(VMEM,) * group,
+        compiler_params=pltpu.CompilerParams(vmem_limit_bytes=8 * 1024 * 1024),
+        name="split_probe",
+    )(place, whole)
+
+
+def join_probe(place, shares):
+    rows, width = shares[0].shape
+
+    def kernel(place, *rest):
+        out = rest[-1]
+        for d, share in enumerate(rest[:-1]):
+            out[pl.ds(pl.multiple_of((place[0] ^ d) * rows, rows), rows), :] = share[...]
+
+    return pl.pallas_call(
+        kernel,
+        out_shape=jax.ShapeDtypeStruct((rows * len(shares), width), jnp.bfloat16),
+        in_specs=[SMEM] + [VMEM] * len(shares),
+        out_specs=VMEM,
+        compiler_params=pltpu.CompilerParams(vmem_limit_bytes=8 * 1024 * 1024),
+        name="join_probe",
+    )(place, *shares)
 
 
 def body(probe_field, specimen, amplitude, scan_anchor, counts):
@@ -543,30 +585,38 @@
     low = kept_low + got_low[: 2 * tile_rows].reshape(kept_low.shape).astype(jnp.float32)
     low = low.astype(jnp.bfloat16)
     probe_part = (kept_probe + got_low[2 * tile_rows :].astype(jnp.float32)).astype(jnp.bfloat16)
-    below = passed_along(low[:, tile_rows - edge :], "tile", 1)
     mid_rows = 2 * (tile_rows - edge)
     mid = jnp.concatenate([low[:, : tile_rows - edge].reshape(mid_rows, width), probe_part], 0)
     mid = narrow_sum(mid, traded(mid, "pos", 2))
+    below = passed_along(low[:, tile_rows - edge :], "tile", 1)
+    mid, below = lax.optimization_barrier((mid, below))
     top = kept_top + got_top.astype(jnp.float32)
     upper = (top + below.astype(jnp.float32)).astype(jnp.bfloat16)
     mid, upper = lax.optimization_barrier((mid, upper))
     upper_got = traded(upper, "pos", 2)
-    probe_part = mid[mid_rows:]
-    distance = lax.axis_size("tile")
-    while distance > 2:
-        distance //= 2
-        probe_part = narrow_sum(probe_part, traded(probe_part, "tile", distance))
+    tiles = lax.axis_size("tile")
+    group = min(tiles // 2, SHARDS)
+    place = (lax.axis_index("tile") // 2 % group).astype(jnp.int32).reshape(1)
+    share, *others = split_probe(place, mid, mid_rows, group)
+    share = share.astype(jnp.float32)
+    for d, other in enumerate(others, 1):
+        share = share + traded(other, "tile", 2 * d).astype(jnp.float32)
+    share = share.astype(jnp.bfloat16)
+    distance = 2 * group
+    while distance < tiles:
+        share = narrow_sum(share, traded(share, "tile", distance))
+        distance *= 2
+    share = narrow_sum(share, traded(share, "tile", 1))
     lower = mid[:mid_rows].reshape(2, tile_rows - edge, width)
     tile_grad = write_rows(meta, lower, traded(lower, "pos", 1), edge, specimen.shape)
-    upper_got, tile_grad, probe_part = lax.optimization_barrier(
-        (upper_got, tile_grad, probe_part)
-    )
-    probe_part = narrow_sum(probe_part, traded(probe_part, "tile", 1))
+    upper_got, tile_grad, share = lax.optimization_barrier((upper_got, tile_grad, share))
     upper = narrow_sum(upper, upper_got)
     tile_grad = write_rows(meta, upper, traded(upper, "pos", 1), 0, specimen.shape, tile_grad)
-    probe_own, probe_theirs = [
-        unfolded(value, edge) for value in (probe_part, traded(probe_part, "pos", 1))
-    ]
+    probe_part = join_probe(
+        place, [share] + [traded(share, "tile", 2 * d) for d in range(1, group)]
+    )
+    probe_theirs, tile_grad = lax.optimization_barrier((traded(probe_part, "pos", 1), tile_grad))
+    probe_own, probe_theirs = [unfolded(value, edge) for value in (probe_part, probe_theirs)]
     probe_total = jnp.where(
         half == 0, jnp.stack([probe_own, probe_theirs]), jnp.stack([probe_theirs, probe_own])
     ).astype(jnp.float32)

time: 84.1 us -> 84 us (level)
  starting transfers between devices: 15.5 us -> 20.9 us
  waiting for transfers between devices: 34.7 us -> 29.9 us
    ppermute x2, starting transfers between devices: 2.61 us -> 5.88 us  [passed_along(): lax.ppermute(value, axis, [(source, source + steps) for source in range(i...]
    ppermute x2, waiting for transfers between devices: 3.74 us -> 0.94 us  [passed_along(): lax.ppermute(value, axis, [(source, source + steps) for source in range(i...]
    ppermute x11 -> x15, starting transfers between devices: 12.9 us -> 15 us  [traded(): return lax.ppermute(value, axis, [(i, i ^ distance) for i in range(count)])]
    ppermute x11 -> x15, waiting for transfers between devices: 31 us -> 29 us  [traded(): return lax.ppermute(value, axis, [(i, i ^ distance) for i in range(count)])]
  transfers between devices with their start and end apart: 13 -> 17, of which waited for: 10 -> 9; matrix products, arithmetic and copies ran while one was open for 3% -> 1% of each run, Pallas kernels for 14% -> 16%
where the time goes in v6:
time: 84 us
  waiting for transfers between devices  29.9 us (36%)
  Pallas kernels  23.8 us (28%)
  starting transfers between devices  20.9 us (25%)
  local copies, waits for them, and re-layouts  5.92 us (7%)
  other arithmetic  1.93 us (2%)
  between operations  1.56 us (2%)
    ppermute x15, waiting for transfers between devices, traded(): return lax.ppermute(value, axis, [(i, i ^ distance) for i in range(count)])  29 us
    ppermute x15, starting transfers between devices, traded(): return lax.ppermute(value, axis, [(i, i ^ distance) for i in range(count)])  15 us
    pallas_call x1, Pallas kernels, run_late(): pl.pallas_call(late_kernel, out_shape=(jax.ShapeDtypeStruct((2 * tile_row...  10.5 us
    pallas_call x1, Pallas kernels, run_early(): pl.pallas_call(early_kernel, out_shape=(jax.ShapeDtypeStruct((2, slices,...  9.26 us
    ppermute x2, starting transfers between devices, passed_along(): lax.ppermute(value, axis, [(source, source + steps) for source in range(i...  5.88 us
    unnamed x13, local copies, waits for them, and re-layouts  4.53 us
    pallas_call x2, Pallas kernels, write_rows(): pl.pallas_call(kernel, out_shape=jax.ShapeDtypeStruct(shape, jnp.float32)...  4.05 us
  transfers between devices with their start and end apart: 17, of which 9 were waited for; matrix products, arithmetic and copies ran while one was open for 1% of the time, Pallas kernels for 16%

profile of v6, /device:TPU:0, one launch (start us, length us, event | category | flops | bytes accessed | tf_op | source)
XLA Modules:
  0.0 84.0 jit_solution(14622721159191580345)
XLA Ops:
  0.7 1.2 %constant_dynamic-slice_fusion = bf16[2,1,256,512]{3,2,1,0:T(8,128)(2,1)S(1)} fusion(bf16[2,2,512,512]{3,2,1,0:T(8,128)(2,1)} %spec_any.3, s32[]{:T(128)S(6)} %select_n.29), kind=kLoop, calls=%fused_computation.14 | loop fusion | bytes 1048580 | tf_op jit(solution)/shard_map/dynamic_slice | solution.py:566
  1.8 1.3 %collective-permute-start = (bf16[2,1,256,512]{3,2,1,0:T(8,128)(2,1)S(1)}, bf16[2,1,256,512]{3,2,1,0:T(8,128)(2,1)S(1)}, u32[]{:S(2)}, u32[]{:S(2)}) collective-permute-start(bf16[2,1,256,512]{3,2,1,0:T(8,128)(2,1)S(1)} %constant_dynamic-slice_fusion), channel_id=1, source_target_pairs={{4,0},{8,4},{12,8},{16,12},{20,16},{24,20},{28,24},{5,1},{9,5},{13... | collective-permute-start | bytes 1572872 | tf_op jit(solution)/shard_map/ppermute | solution.py:510
  3.8 0.8 copy.10.anchor
  4.5 0.1 pad_add_fusion.meta
  4.6 1.6 %copy-done = bf16[2,2,512,512]{3,2,1,0:T(8,128)(2,1)S(1)} copy-done((bf16[2,2,512,512]{3,2,1,0:T(8,128)(2,1)S(1)}, bf16[2,2,512,512]{3,2,1,0:T(8,128)(2,1)}, u32[]{:S(2)}) %copy-start) | copy-done | bytes 2097176
  6.2 1.1 %copy-done.3 = bf16[6,256,256]{2,1,0:T(8,128)(2,1)S(1)} copy-done((bf16[6,256,256]{2,1,0:T(8,128)(2,1)S(1)}, bf16[6,256,256]{2,1,0:T(8,128)(2,1)}, u32[]{:S(2)}) %copy-start.3) | copy-done | bytes 786456
  7.3 1.0 %copy-done.4 = f32[2,256,256]{2,1,0:T(8,128)S(1)} copy-done((f32[2,256,256]{2,1,0:T(8,128)S(1)}, f32[2,256,256]{2,1,0:T(8,128)}, u32[]{:S(2)}) %copy-start.4) | copy-done | bytes 524312
  8.4 9.3 %early_slots.1 = (f32[2,2,4,512,128]{4,3,2,1,0:T(8,128)S(1)}, f32[2,256,256]{2,1,0:T(8,128)S(1)}) custom-call(s32[3]{0:T(128)S(1)} %pad_add_fusion.meta, s32[8,2]{1,0:T(8,128)S(1)} %copy.10.anchor, f32[2,256,256]{2,1,0:T(8,128)S(1)} %copy-done.4, bf16[2,2,512,512]{3,2,1,0:T(8,128)(2,1)S(1)} %copy-done, bf16[8,256,256]{2,1,0:T(8,128)(2,1)S(1)} %copy-done.2, ...), custom_call_target="tpu_custom_call" | custom-call | tf_op jit(solution)/shard_map/early_slots/pallas_call | solution.py:418
  17.7 0.9 %collective-permute-done.rim_own_any = bf16[2,1,256,512]{3,2,1,0:T(8,128)(2,1)S(1)} collective-permute-done((bf16[2,1,256,512]{3,2,1,0:T(8,128)(2,1)S(1)}, bf16[2,1,256,512]{3,2,1,0:T(8,128)(2,1)S(1)}, u32[]{:S(2)}, u32[]{:S(2)}) %collective-permute-start) | collective-permute-done | bytes 524320 | tf_op jit(solution)/shard_map/ppermute | solution.py:510
  18.6 0.0 collective-permute-start.1
  18.6 1.9 %collective-permute-done.1.rim_other_any = bf16[2,1,256,512]{3,2,1,0:T(8,128)(2,1)S(1)} collective-permute-done((bf16[2,1,256,512]{3,2,1,0:T(8,128)(2,1)S(1)}, bf16[2,1,256,512]{3,2,1,0:T(8,128)(2,1)S(1)}, u32[]{:S(2)}, u32[]{:S(2)}) %collective-permute-start.1) | collective-permute-done | bytes 524320 | tf_op jit(solution)/shard_map/ppermute | solution.py:504
  20.5 10.5 %late_slots.1 = (bf16[1152,512]{1,0:T(8,128)(2,1)S(1)}, bf16[2,256,512]{2,1,0:T(8,128)(2,1)S(1)}, f32[2,512,512]{2,1,0:T(8,128)S(1)}, f32[2,256,512]{2,1,0:T(8,128)S(1)}, f32[128,512]{1,0:T(8,128)S(1)}) custom-call(s32[3]{0:T(128)S(1)} %pad_add_fusion.meta, s32[8,2]{1,0:T(8,128)S(1)} %copy.10.anchor, f32[2,256,256]{2,1,0:T(8,128)S(1)} %copy-done.5, ...), custom_call_target="tpu_custom_call" | custom-call | tf_op jit(solution)/shard_map/late_slots/pallas_call | solution.py:439
  31.0 0.1 collective-permute-start.2
  31.0 2.8 %collective-permute-done.2 = bf16[1152,512]{1,0:T(8,128)(2,1)S(1)} collective-permute-done((bf16[1152,512]{1,0:T(8,128)(2,1)S(1)}, bf16[1152,512]{1,0:T(8,128)(2,1)S(1)}, u32[]{:S(2)}, u32[]{:S(2)}) %collective-permute-start.2) | collective-permute-done | bytes 1179680 | tf_op jit(solution)/shard_map/ppermute | solution.py:504
  33.9 0.1 slice.36
  34.0 0.4 fusion
  34.3 0.1 fusion.2
  34.5 0.1 collective-permute-start.3
  34.6 4.6 %collective-permute-start.4 = (bf16[2,256,512]{2,1,0:T(8,128)(2,1)S(1)}, bf16[2,256,512]{2,1,0:T(8,128)(2,1)S(1)}, u32[]{:S(2)}, u32[]{:S(2)}) collective-permute-start(bf16[2,256,512]{2,1,0:T(8,128)(2,1)S(1)} %get-tuple-element.46), channel_id=1, source_target_pairs={{0,4},{4,8},{8,12},{12,16},{16,20},{20,24},{24,28},{1,5},{5,9},{9,... | collective-permute-start | bytes 1572872 | tf_op jit(solution)/shard_map/ppermute | solution.py:510
  39.2 0.1 collective-permute-start.5
  39.3 12.1 %collective-permute-done.3 = bf16[640,512]{1,0:T(8,128)(2,1)S(1)} collective-permute-done((bf16[640,512]{1,0:T(8,128)(2,1)S(1)}, bf16[640,512]{1,0:T(8,128)(2,1)S(1)}, u32[]{:S(2)}, u32[]{:S(2)}) %collective-permute-start.3) | collective-permute-done | bytes 655392 | tf_op jit(solution)/shard_map/ppermute | solution.py:504
  51.3 0.2 add_convert_fusion.whole
  51.5 0.0 collective-permute-done.4
  51.5 0.0 collective-permute-done.5
  51.5 0.2 add_convert_fusion.2
  51.8 0.1 collective-permute-start.7
  51.9 0.9 %collective-permute-start.6 = (bf16[2,256,512]{2,1,0:T(8,128)(2,1)S(1)}, bf16[2,256,512]{2,1,0:T(8,128)(2,1)S(1)}, u32[]{:S(2)}, u32[]{:S(2)}) collective-permute-start(bf16[2,256,512]{2,1,0:T(8,128)(2,1)S(1)} %add_convert_fusion.2), channel_id=1, source_target_pairs={{0,2},{1,3},{2,0},{3,1},{4,6},{5,7},{6,4},{7,5},{8,10},{9,11},{10,... | collective-permute-start | bytes 1572872 | tf_op jit(solution)/shard_map/ppermute | solution.py:504
  52.8 4.5 %collective-permute-start.8 = (bf16[32,512]{1,0:T(8,128)(2,1)S(1)}, bf16[32,512]{1,0:T(8,128)(2,1)S(1)}, u32[]{:S(2)}, u32[]{:S(2)}) collective-permute-start(bf16[32,512]{1,0:T(8,128)(2,1)S(1)} %get-tuple-element.38), channel_id=1, source_target_pairs={{0,8},{4,12},{8,0},{12,4},{16,24},{20,28},{24,16},{28,20},{1,9},{5... | collective-permute-start | bytes 98312 | tf_op jit(solution)/shard_map/ppermute | solution.py:504
  57.3 4.6 %collective-permute-start.9 = (bf16[32,512]{1,0:T(8,128)(2,1)S(1)}, bf16[32,512]{1,0:T(8,128)(2,1)S(1)}, u32[]{:S(2)}, u32[]{:S(2)}) collective-permute-start(bf16[32,512]{1,0:T(8,128)(2,1)S(1)} %get-tuple-element.39), channel_id=1, source_target_pairs={{0,16},{4,20},{8,24},{12,28},{16,0},{20,4},{24,8},{28,12},{1,17},{... | collective-permute-start | bytes 98312 | tf_op jit(solution)/shard_map/ppermute | solution.py:504
  61.9 0.0 collective-permute-start.10
  61.9 0.0 collective-permute-done.8
  61.9 2.4 %collective-permute-done.9 = bf16[32,512]{1,0:T(8,128)(2,1)S(1)} collective-permute-done((bf16[32,512]{1,0:T(8,128)(2,1)S(1)}, bf16[32,512]{1,0:T(8,128)(2,1)S(1)}, u32[]{:S(2)}, u32[]{:S(2)}) %collective-permute-start.9) | collective-permute-done | bytes 32800 | tf_op jit(solution)/shard_map/ppermute | solution.py:504
  64.3 3.3 %collective-permute-done.10 = bf16[32,512]{1,0:T(8,128)(2,1)S(1)} collective-permute-done((bf16[32,512]{1,0:T(8,128)(2,1)S(1)}, bf16[32,512]{1,0:T(8,128)(2,1)S(1)}, u32[]{:S(2)}, u32[]{:S(2)}) %collective-permute-start.10) | collective-permute-done | bytes 32800 | tf_op jit(solution)/shard_map/ppermute | solution.py:504
  67.6 0.1 collective-permute-start.11
  67.7 3.9 %collective-permute-done.11 = bf16[32,512]{1,0:T(8,128)(2,1)S(1)} collective-permute-done((bf16[32,512]{1,0:T(8,128)(2,1)S(1)}, bf16[32,512]{1,0:T(8,128)(2,1)S(1)}, u32[]{:S(2)}, u32[]{:S(2)}) %collective-permute-start.11) | collective-permute-done | bytes 32800 | tf_op jit(solution)/shard_map/ppermute | solution.py:504
  71.6 0.0 collective-permute-done.7.theirs
  71.7 2.0 %write_rows.2.rest_0_ = f32[2,2,512,512]{3,2,1,0:T(8,128)} custom-call(s32[3]{0:T(128)S(1)} %pad_add_fusion.meta, bf16[2,256,512]{2,1,0:T(8,128)(2,1)S(1)} %bitcast.12, bf16[2,256,512]{2,1,0:T(8,128)(2,1)S(1)} %collective-permute-done.7.theirs), custom_call_target="tpu_custom_call" | custom-call | bytes 3145728 | tf_op jit(solution)/shard_map/write_rows/pallas_call | solution.py:484
  73.7 0.0 collective-permute-done.6
  73.7 0.1 add_convert_fusion.1.own
  73.8 0.1 collective-permute-start.16
  73.9 1.4 %collective-permute-start.14 = (bf16[32,512]{1,0:T(8,128)(2,1)S(1)}, bf16[32,512]{1,0:T(8,128)(2,1)S(1)}, u32[]{:S(2)}, u32[]{:S(2)}) collective-permute-start(bf16[32,512]{1,0:T(8,128)(2,1)S(1)} %add_convert_fusion.4.rest_0_), channel_id=1, source_target_pairs={{0,24},{4,28},{8,16},{12,20},{16,8},{20,12},{24,0},{28,4},{1,25},{... | collective-permute-start | bytes 98312 | tf_op jit(solution)/shard_map/ppermute | solution.py:504
  75.3 0.0 collective-permute-start.13
  75.3 3.0 %collective-permute-start.12 = (bf16[32,512]{1,0:T(8,128)(2,1)S(1)}, bf16[32,512]{1,0:T(8,128)(2,1)S(1)}, u32[]{:S(2)}, u32[]{:S(2)}) collective-permute-start(bf16[32,512]{1,0:T(8,128)(2,1)S(1)} %add_convert_fusion.4.rest_0_), channel_id=1, source_target_pairs={{0,8},{4,12},{8,0},{12,4},{16,24},{20,28},{24,16},{28,20},{1,9},{5... | collective-permute-start | bytes 98312 | tf_op jit(solution)/shard_map/ppermute | solution.py:504
  78.4 1.6 %collective-permute-done.14.rest_3_ = bf16[32,512]{1,0:T(8,128)(2,1)S(1)} collective-permute-done((bf16[32,512]{1,0:T(8,128)(2,1)S(1)}, bf16[32,512]{1,0:T(8,128)(2,1)S(1)}, u32[]{:S(2)}, u32[]{:S(2)}) %collective-permute-start.14) | collective-permute-done | bytes 32800 | tf_op jit(solution)/shard_map/ppermute | solution.py:504
  80.0 1.0 %collective-permute-done.13.rest_2_ = bf16[32,512]{1,0:T(8,128)(2,1)S(1)} collective-permute-done((bf16[32,512]{1,0:T(8,128)(2,1)S(1)}, bf16[32,512]{1,0:T(8,128)(2,1)S(1)}, u32[]{:S(2)}, u32[]{:S(2)}) %collective-permute-start.13) | collective-permute-done | bytes 32800 | tf_op jit(solution)/shard_map/ppermute | solution.py:504
  80.9 0.1 collective-permute-start.15
  81.1 2.0 %write_rows.3 = f32[2,2,512,512]{3,2,1,0:T(8,128)} custom-call(s32[3]{0:T(128)S(1)} %pad_add_fusion.meta, bf16[2,256,512]{2,1,0:T(8,128)(2,1)S(1)} %add_convert_fusion.1.own, bf16[2,256,512]{2,1,0:T(8,128)(2,1)S(1)} %collective-permute-done.16.theirs, f32[2,2,512,512]{3,2,1,0:T(8,128)} %write_rows.2.rest_0_), custom_call_target="tpu_custom_call", output_to_operand_aliasing={{}: (3, {})} | custom-call | bytes 3145728 | tf_op jit(solution)/shard_map/write_rows/pallas_call | solution.py:484
  83.2 0.8 fusion.1
  (23 shorter events, 0.2 us)
Async XLA Ops:
  0.6 4.0 %copy-start.2 = (bf16[8,256,256]{2,1,0:T(8,128)(2,1)S(1)}, bf16[8,256,256]{2,1,0:T(8,128)(2,1)}, u32[]{:S(2)}) copy-start(bf16[8,256,256]{2,1,0:T(8,128)(2,1)} %amp_any.3) | copy-start | bytes 3145732
  1.8 16.8 %collective-permute-start = (bf16[2,1,256,512]{3,2,1,0:T(8,128)(2,1)S(1)}, bf16[2,1,256,512]{3,2,1,0:T(8,128)(2,1)S(1)}, u32[]{:S(2)}, u32[]{:S(2)}) collective-permute-start(bf16[2,1,256,512]{3,2,1,0:T(8,128)(2,1)S(1)} %constant_dynamic-slice_fusion), channel_id=1, source_target_pairs={{4,0},{8,4},{12,8},{16,12},{20,16},{24,20},{28,24},{5,1},{9,5},{13... | collective-permute-start | bytes 1572872 | tf_op jit(solution)/shard_map/ppermute | solution.py:510
  4.6 1.6 %copy-start = (bf16[2,2,512,512]{3,2,1,0:T(8,128)(2,1)S(1)}, bf16[2,2,512,512]{3,2,1,0:T(8,128)(2,1)}, u32[]{:S(2)}) copy-start(bf16[2,2,512,512]{3,2,1,0:T(8,128)(2,1)} %spec_any.3) | copy-start | bytes 6291460
  6.2 1.1 %copy-start.3 = (bf16[6,256,256]{2,1,0:T(8,128)(2,1)S(1)}, bf16[6,256,256]{2,1,0:T(8,128)(2,1)}, u32[]{:S(2)}) copy-start(bf16[6,256,256]{2,1,0:T(8,128)(2,1)} %constant.48.clone.planes_any) | copy-start | bytes 2359300
  7.3 1.0 %copy-start.4 = (f32[2,256,256]{2,1,0:T(8,128)S(1)}, f32[2,256,256]{2,1,0:T(8,128)}, u32[]{:S(2)}) copy-start(f32[2,256,256]{2,1,0:T(8,128)} %probe_any.3) | copy-start | bytes 1572868
  8.4 12.1 %copy-start.1 = (bf16[2,2,512,512]{3,2,1,0:T(8,128)(2,1)S(1)}, bf16[2,2,512,512]{3,2,1,0:T(8,128)(2,1)}, u32[]{:S(2)}) copy-start(bf16[2,2,512,512]{3,2,1,0:T(8,128)(2,1)} %spec_any.3) | copy-start | bytes 6291460
  8.4 12.1 %copy-start.5 = (f32[2,256,256]{2,1,0:T(8,128)S(1)}, f32[2,256,256]{2,1,0:T(8,128)}, u32[]{:S(2)}) copy-start(f32[2,256,256]{2,1,0:T(8,128)} %probe_any.3) | copy-start | bytes 1572868
  18.6 1.9 %collective-permute-start.1 = (bf16[2,1,256,512]{3,2,1,0:T(8,128)(2,1)S(1)}, bf16[2,1,256,512]{3,2,1,0:T(8,128)(2,1)S(1)}, u32[]{:S(2)}, u32[]{:S(2)}) collective-permute-start(bf16[2,1,256,512]{3,2,1,0:T(8,128)(2,1)S(1)} %collective-permute-done.rim_own_any), channel_id=1, source_target_pairs={{0,1},{1,0},{2,3},{3,2},{4,5},{5,4},{6,7},{7,6},{8,9},{9,8},{10,11... | collective-permute-start | bytes 1572872 | tf_op jit(solution)/shard_map/ppermute | solution.py:504
  31.0 2.9 %collective-permute-start.2 = (bf16[1152,512]{1,0:T(8,128)(2,1)S(1)}, bf16[1152,512]{1,0:T(8,128)(2,1)S(1)}, u32[]{:S(2)}, u32[]{:S(2)}) collective-permute-start(bf16[1152,512]{1,0:T(8,128)(2,1)S(1)} %get-tuple-element.29), channel_id=1, source_target_pairs={{0,1},{1,0},{2,3},{3,2},{4,5},{5,4},{6,7},{7,6},{8,9},{9,8},{10,11... | collective-permute-start | bytes 3538952 | tf_op jit(solution)/shard_map/ppermute | solution.py:504
  34.5 16.8 %collective-permute-start.3 = (bf16[640,512]{1,0:T(8,128)(2,1)S(1)}, bf16[640,512]{1,0:T(8,128)(2,1)S(1)}, u32[]{:S(2)}, u32[]{:S(2)}) collective-permute-start(bf16[640,512]{1,0:T(8,128)(2,1)S(1)} %pad_maximum_fusion), channel_id=1, source_target_pairs={{0,2},{1,3},{2,0},{3,1},{4,6},{5,7},{6,4},{7,5},{8,10},{9,11},{10,... | collective-permute-start | bytes 1966088 | tf_op jit(solution)/shard_map/ppermute | solution.py:504
  34.6 16.9 %collective-permute-start.4 = (bf16[2,256,512]{2,1,0:T(8,128)(2,1)S(1)}, bf16[2,256,512]{2,1,0:T(8,128)(2,1)S(1)}, u32[]{:S(2)}, u32[]{:S(2)}) collective-permute-start(bf16[2,256,512]{2,1,0:T(8,128)(2,1)S(1)} %get-tuple-element.46), channel_id=1, source_target_pairs={{0,4},{4,8},{8,12},{12,16},{16,20},{20,24},{24,28},{1,5},{5,9},{9,... | collective-permute-start | bytes 1572872 | tf_op jit(solution)/shard_map/ppermute | solution.py:510
  39.2 12.3 %collective-permute-start.5 = (bf16[2,256,512]{2,1,0:T(8,128)(2,1)S(1)}, bf16[2,256,512]{2,1,0:T(8,128)(2,1)S(1)}, u32[]{:S(2)}, u32[]{:S(2)}) collective-permute-start(bf16[2,256,512]{2,1,0:T(8,128)(2,1)S(1)} %get-tuple-element.33), channel_id=1, source_target_pairs={{0,1},{1,0},{2,3},{3,2},{4,5},{5,4},{6,7},{7,6},{8,9},{9,8},{10,11... | collective-permute-start | bytes 1572872 | tf_op jit(solution)/shard_map/ppermute | solution.py:504
  51.8 19.8 %collective-permute-start.7 = (bf16[2,256,512]{2,1,0:T(8,128)(2,1)S(1)}, bf16[2,256,512]{2,1,0:T(8,128)(2,1)S(1)}, u32[]{:S(2)}, u32[]{:S(2)}) collective-permute-start(bf16[2,256,512]{2,1,0:T(8,128)(2,1)S(1)} %bitcast.11), channel_id=1, source_target_pairs={{0,1},{1,0},{2,3},{3,2},{4,5},{5,4},{6,7},{7,6},{8,9},{9,8},{10,11... | collective-permute-start | bytes 1572872 | tf_op jit(solution)/shard_map/ppermute | solution.py:504
  51.9 21.8 %collective-permute-start.6 = (bf16[2,256,512]{2,1,0:T(8,128)(2,1)S(1)}, bf16[2,256,512]{2,1,0:T(8,128)(2,1)S(1)}, u32[]{:S(2)}, u32[]{:S(2)}) collective-permute-start(bf16[2,256,512]{2,1,0:T(8,128)(2,1)S(1)} %add_convert_fusion.2), channel_id=1, source_target_pairs={{0,2},{1,3},{2,0},{3,1},{4,6},{5,7},{6,4},{7,5},{8,10},{9,11},{10,... | collective-permute-start | bytes 1572872 | tf_op jit(solution)/shard_map/ppermute | solution.py:504
  52.8 9.2 %collective-permute-start.8 = (bf16[32,512]{1,0:T(8,128)(2,1)S(1)}, bf16[32,512]{1,0:T(8,128)(2,1)S(1)}, u32[]{:S(2)}, u32[]{:S(2)}) collective-permute-start(bf16[32,512]{1,0:T(8,128)(2,1)S(1)} %get-tuple-element.38), channel_id=1, source_target_pairs={{0,8},{4,12},{8,0},{12,4},{16,24},{20,28},{24,16},{28,20},{1,9},{5... | collective-permute-start | bytes 98312 | tf_op jit(solution)/shard_map/ppermute | solution.py:504
  57.3 7.0 %collective-permute-start.9 = (bf16[32,512]{1,0:T(8,128)(2,1)S(1)}, bf16[32,512]{1,0:T(8,128)(2,1)S(1)}, u32[]{:S(2)}, u32[]{:S(2)}) collective-permute-start(bf16[32,512]{1,0:T(8,128)(2,1)S(1)} %get-tuple-element.39), channel_id=1, source_target_pairs={{0,16},{4,20},{8,24},{12,28},{16,0},{20,4},{24,8},{28,12},{1,17},{... | collective-permute-start | bytes 98312 | tf_op jit(solution)/shard_map/ppermute | solution.py:504
  61.9 5.7 %collective-permute-start.10 = (bf16[32,512]{1,0:T(8,128)(2,1)S(1)}, bf16[32,512]{1,0:T(8,128)(2,1)S(1)}, u32[]{:S(2)}, u32[]{:S(2)}) collective-permute-start(bf16[32,512]{1,0:T(8,128)(2,1)S(1)} %get-tuple-element.40), channel_id=1, source_target_pairs={{0,24},{4,28},{8,16},{12,20},{16,8},{20,12},{24,0},{28,4},{1,25},{... | collective-permute-start | bytes 98312 | tf_op jit(solution)/shard_map/ppermute | solution.py:504
  67.6 4.0 %collective-permute-start.11 = (bf16[32,512]{1,0:T(8,128)(2,1)S(1)}, bf16[32,512]{1,0:T(8,128)(2,1)S(1)}, u32[]{:S(2)}, u32[]{:S(2)}) collective-permute-start(bf16[32,512]{1,0:T(8,128)(2,1)S(1)} %add_convert_fusion.5), channel_id=1, source_target_pairs={{0,4},{4,0},{8,12},{12,8},{16,20},{20,16},{24,28},{28,24},{1,5},{5... | collective-permute-start | bytes 98312 | tf_op jit(solution)/shard_map/ppermute | solution.py:504
  73.8 7.2 %collective-permute-start.16 = (bf16[2,256,512]{2,1,0:T(8,128)(2,1)S(1)}, bf16[2,256,512]{2,1,0:T(8,128)(2,1)S(1)}, u32[]{:S(2)}, u32[]{:S(2)}) collective-permute-start(bf16[2,256,512]{2,1,0:T(8,128)(2,1)S(1)} %add_convert_fusion.1.own), channel_id=1, source_target_pairs={{0,1},{1,0},{2,3},{3,2},{4,5},{5,4},{6,7},{7,6},{8,9},{9,8},{10,11... | collective-permute-start | bytes 1572872 | tf_op jit(solution)/shard_map/ppermute | solution.py:504
  73.9 6.1 %collective-permute-start.14 = (bf16[32,512]{1,0:T(8,128)(2,1)S(1)}, bf16[32,512]{1,0:T(8,128)(2,1)S(1)}, u32[]{:S(2)}, u32[]{:S(2)}) collective-permute-start(bf16[32,512]{1,0:T(8,128)(2,1)S(1)} %add_convert_fusion.4.rest_0_), channel_id=1, source_target_pairs={{0,24},{4,28},{8,16},{12,20},{16,8},{20,12},{24,0},{28,4},{1,25},{... | collective-permute-start | bytes 98312 | tf_op jit(solution)/shard_map/ppermute | solution.py:504
  75.3 5.6 %collective-permute-start.13 = (bf16[32,512]{1,0:T(8,128)(2,1)S(1)}, bf16[32,512]{1,0:T(8,128)(2,1)S(1)}, u32[]{:S(2)}, u32[]{:S(2)}) collective-permute-start(bf16[32,512]{1,0:T(8,128)(2,1)S(1)} %add_convert_fusion.4.rest_0_), channel_id=1, source_target_pairs={{0,16},{4,20},{8,24},{12,28},{16,0},{20,4},{24,8},{28,12},{1,17},{... | collective-permute-start | bytes 98312 | tf_op jit(solution)/shard_map/ppermute | solution.py:504
  75.3 5.6 %collective-permute-start.12 = (bf16[32,512]{1,0:T(8,128)(2,1)S(1)}, bf16[32,512]{1,0:T(8,128)(2,1)S(1)}, u32[]{:S(2)}, u32[]{:S(2)}) collective-permute-start(bf16[32,512]{1,0:T(8,128)(2,1)S(1)} %add_convert_fusion.4.rest_0_), channel_id=1, source_target_pairs={{0,8},{4,12},{8,0},{12,4},{16,24},{20,28},{24,16},{28,20},{1,9},{5... | collective-permute-start | bytes 98312 | tf_op jit(solution)/shard_map/ppermute | solution.py:504
  80.9 2.2 %collective-permute-start.15 = (bf16[128,512]{1,0:T(8,128)(2,1)S(1)}, bf16[128,512]{1,0:T(8,128)(2,1)S(1)}, u32[]{:S(2)}, u32[]{:S(2)}) collective-permute-start(bf16[128,512]{1,0:T(8,128)(2,1)S(1)} %join_probe.1), channel_id=1, source_target_pairs={{0,1},{1,0},{2,3},{3,2},{4,5},{5,4},{6,7},{7,6},{8,9},{9,8},{10,11... | collective-permute-start | bytes 393224 | tf_op jit(solution)/shard_map/ppermute | solution.py:504
